TPU v7x, 256 devices: a whole 4x4x8 slice. The times are simulated.
256 devices in a mesh: island: 32 (over z_hi, x, y), fsdp: 8 (over z_lo, core).
Axes of the slice: x: 4, y: 4, z: 8 (z_hi: 2, z_lo: 4; z = z_hi * 4 + z_lo), core: 2. Of those that a mesh axis runs over, the one named last changes fastest.
Arguments:
- global_weights: float32 [256, 28672], P('fsdp'), may hold values from -4 to 4
- local_weights: float32 [32, 256, 28672], P('island', 'fsdp')
- momentum: float32 [256, 28672], P('fsdp', 'island'), may hold values from -0.6 to 0.6
Outputs:
- new_global: float32 [256, 28672], P('fsdp')
- new_momentum: float32 [256, 28672], P('fsdp', 'island')
All inputs are finite; a program needn't handle non-finite values.
Results may differ from a plain program's by a relative error of at most 0.00002.
Values sent between devices are 32-bit elements; how exact they have to be, the bound alone decides.
No kernel may reach another device: no remote copies, remote signals or barrier semaphores. Data moves between devices by JAX's collectives and lax.ppermute only.
A program may use at most 64 MiB of HBM per device.

v0:
```python
import jax
import jax.numpy as jnp
from jax import lax
from jax.sharding import PartitionSpec as P

clip_level = 0.1
outer_rate = 0.7
moment_decay = 0.9


def per_device(global_weights, local_weights, momentum):
    islands = lax.axis_size("island")
    shards = lax.axis_size("fsdp")
    pseudo = global_weights - local_weights[0]
    summed = lax.psum_scatter(pseudo, "island", scatter_dimension=1, tiled=True)
    average = summed / islands
    count = average.shape[0] * average.shape[1] * islands * shards
    squares = lax.psum(jnp.sum(average * average), ("island", "fsdp"))
    spread = jnp.sqrt(squares / count + 1e-06)
    factor = jnp.minimum(1.0, clip_level / spread)
    width = average.shape[1]
    owned = lax.dynamic_slice_in_dim(global_weights, lax.axis_index("island") * width, width, 1)
    clipped = factor * average
    new_momentum = moment_decay * momentum + clipped
    updated = owned - outer_rate * (clipped + moment_decay * new_momentum)
    new_global = lax.all_gather(updated, "island", axis=1, tiled=True)
    return (new_global, new_momentum)


def solution(mesh):
    placed = (P("fsdp", None), P("island", "fsdp", None), P("fsdp", "island"))
    return jax.shard_map(
        per_device,
        mesh=mesh,
        in_specs=placed,
        out_specs=(P("fsdp", None), P("fsdp", "island")),
        check_vma=False,
    )
```

profile of v0, /device:TPU:2, one launch (start us, length us, event | category | flops | bytes accessed | tf_op | source)
XLA Modules:
  0.0 439.1 jit_solution(9565199145720236319)
XLA Ops:
  7.2 0.0 reduce-scatter.2.cloned.1.call-start
  7.2 5.4 %bitcast_subtract_fusion = f32[32,28672]{1,0:T(8,128)} fusion(f32[32,28672]{1,0:T(8,128)} %param.3, f32[1,32,28672]{2,1,0:T(8,128)} %param.4), kind=kLoop, calls=%fused_computation | loop fusion | flops 917504 | bytes 11010048 | tf_op jit(solution)/shard_map/sub | solution.py:14
  12.6 0.0 copy-start
  12.6 0.0 reduce-scatter.2.cloned.1.call-update
  12.6 0.0 all-gather.2.cloned.1.call-start
  12.6 222.4 %reduce-scatter.2.cloned.1.call-done = f32[32,896]{1,0:T(8,128)} async-done(((f32[32,28672]{1,0:T(8,128)}), f32[32,896]{1,0:T(8,128)}) %reduce-scatter.2.cloned.1.call-update) | async-done | bytes 114704 | tf_op jit(solution)/shard_map/reduce_scatter | solution.py:15
  235.1 1.5 multiply_reduce_fusion
  236.6 86.9 %psum.7 = f32[]{:T(128)} all-reduce(f32[]{:T(128)} %multiply_reduce_fusion), channel_id=1, replica_groups=mesh['island'=32,'fsdp'=8] {'island','fsdp'}, use_global_device_ids=true, to_apply=%region_2.0 | all-reduce | flops 1 | bytes 8 | tf_op jit(solution)/shard_map/psum | solution.py:18
  324.2 0.0 copy-done
  324.2 1.7 multiply_subtract_fusion
  325.9 0.0 all-gather.2.cloned.1.call-update
  325.9 102.3 %all-gather.2.cloned.1.call-done = f32[32,28672]{1,0:T(8,128)} async-done(((f32[32,896]{1,0:T(8,128)}), f32[32,28672]{1,0:T(8,128)}) %all-gather.2.cloned.1.call-update) | async-done | bytes 3670032 | tf_op jit(solution)/shard_map/all_gather | solution.py:26
  428.2 4.1 copy.6
Async XLA Ops:
  7.2 227.9 %reduce-scatter.2.cloned.1.call-start = ((), (), s32[]{:S(2)}) async-start(), calls=%async_computation.1 | async-start | bytes 3784704 | tf_op jit(solution)/shard_map/reduce_scatter | solution.py:15
  12.6 311.6 %copy-start = (f32[32,896]{1,0:T(8,128)S(1)}, f32[32,896]{1,0:T(8,128)}, u32[]{:S(2)}) copy-start(f32[32,896]{1,0:T(8,128)} %param.5) | copy-start | bytes 344068
  12.6 415.6 %all-gather.2.cloned.1.call-start = ((), (), s32[]{:S(2)}) async-start(), calls=%async_computation.2 | async-start | bytes 3784704 | tf_op jit(solution)/shard_map/all_gather | solution.py:26
Sparse Core Ops, SparseCore 0:
  12.7 222.3 reduce-scatter.1
  326.0 102.1 all-gather.1
where the time goes:
time: 440 us; the launch traced here: 439 us
  waiting for transfers between devices  325 us (74%)
  blocking collectives  86.9 us (20%)
  between operations  14.7 us (3%)
  other arithmetic  8.56 us (2%)
    reduce_scatter x1, waiting for transfers between devices, per_device(): summed = lax.psum_scatter(pseudo, 'island', scatter_dimension=1, tiled=True)  222 us
    all_gather x1, waiting for transfers between devices, per_device(): new_global = lax.all_gather(updated, 'island', axis=1, tiled=True)  102 us
    psum x1, blocking collectives, per_device(): squares = lax.psum(jnp.sum(average * average), ('island', 'fsdp'))  86.9 us
  transfers between devices with their start and end apart: 2, of which 2 were waited for; matrix products, arithmetic and copies ran while one was open for 0% of the time, Pallas kernels for 0%

commit v1 on v0

v1 whole, which is shorter than its diff:
```python
import functools

import jax
import jax.numpy as jnp
from jax import lax
from jax.experimental import pallas as pl
from jax.experimental.pallas import tpu as pltpu
from jax.sharding import PartitionSpec as P

clip_level = 0.1
outer_rate = 0.7
moment_decay = 0.9

AXES = ("island", "fsdp")
HALVES, SIDE, RUN, CORES = 2, 4, 4, 2


def pairs(move):
    out = []
    for zh in range(HALVES):
        for x in range(SIDE):
            for y in range(SIDE):
                for zl in range(RUN):
                    for core in range(CORES):
                        there = move(zh, x, y, zl, core)
                        place = lambda h, i, j, k, c: ((h * SIDE + i) * SIDE + j) * RUN * CORES + k * CORES + c
                        out.append((place(zh, x, y, zl, core), place(*there)))
    return out


def along(first, step):
    def move(zh, x, y, zl, core):
        if (core == 0) == first:
            return zh, (x + step) % SIDE, y, zl, core
        return zh, x, (y + step) % SIDE, zl, core

    return pairs(move)


FIRST = {step: along(True, step) for step in (1, 2, 3)}
SECOND = {step: along(False, step) for step in (1, 2, 3)}
ACROSS = pairs(lambda zh, x, y, zl, core: (1 - zh, x, y, zl, core))
UP = {step: pairs(lambda zh, x, y, zl, core, s=step: (zh, x, y, (zl + s) % RUN, core)) for step in (1, 2, 3)}
TWIN = pairs(lambda zh, x, y, zl, core: (zh, x, y, zl, 1 - core))


def send(value, route):
    return lax.ppermute(value, AXES, route)


def place_of(width, step, near, half):
    island = lax.axis_index("island")
    core = lax.rem(lax.axis_index("fsdp"), CORES)
    zh = island // (SIDE * SIDE)
    x = lax.rem(island // SIDE, SIDE)
    y = lax.rem(island, SIDE)
    one = jnp.where(core == 0, x, y)
    two = jnp.where(core == 0, y, x)
    one = lax.rem(one + step, SIDE)
    two = lax.rem(two + near, SIDE)
    zh = lax.rem(zh + half, HALVES)
    block = zh * SIDE * SIDE + jnp.where(core == 0, one * SIDE + two, two * SIDE + one)
    return pl.multiple_of(block * width, 128)


def pack_kernel(step, width, whole, piece, sems):
    copies = []
    for near in range(SIDE):
        for half in range(HALVES):
            n = near * HALVES + half
            copy = pltpu.make_async_copy(
                whole.at[:, pl.ds(place_of(width, step, near, half), width)], piece.at[near, half], sems.at[n]
            )
            copy.start()
            copies.append(copy)
    for copy in copies:
        copy.wait()


def pack(whole, step, width):
    rows = whole.shape[0]
    return pl.pallas_call(
        functools.partial(pack_kernel, step, width),
        out_shape=jax.ShapeDtypeStruct((SIDE, HALVES, rows, width), whole.dtype),
        in_specs=[pl.BlockSpec(memory_space=pl.ANY)],
        out_specs=pl.BlockSpec(memory_space=pl.ANY),
        scratch_shapes=[pltpu.SemaphoreType.DMA((SIDE * HALVES,))],
        cost_estimate=pl.CostEstimate(flops=0, bytes_accessed=2 * 4 * SIDE * HALVES * rows * width, transcendentals=0),
        name=f"pack{step}",
    )(whole)


def unpack_kernel(step, width, piece, *rest):
    whole, sems = rest[-2], rest[-1]
    copies = []
    for near in range(SIDE):
        for half in range(HALVES):
            n = near * HALVES + half
            copy = pltpu.make_async_copy(
                piece.at[near, half], whole.at[:, pl.ds(place_of(width, step, near, half), width)], sems.at[n]
            )
            copy.start()
            copies.append(copy)
    for copy in copies:
        copy.wait()


def unpack(piece, whole, step, shape):
    _, _, rows, width = piece.shape
    given = [] if whole is None else [whole]
    return pl.pallas_call(
        functools.partial(unpack_kernel, step, width),
        out_shape=jax.ShapeDtypeStruct(shape, piece.dtype),
        in_specs=[pl.BlockSpec(memory_space=pl.ANY)] * (1 + len(given)),
        out_specs=pl.BlockSpec(memory_space=pl.ANY),
        scratch_shapes=[pltpu.SemaphoreType.DMA((SIDE * HALVES,))],
        input_output_aliases={1: 0} if given else {},
        cost_estimate=pl.CostEstimate(flops=0, bytes_accessed=2 * 4 * SIDE * HALVES * rows * width, transcendentals=0),
        name=f"unpack{step}",
    )(piece, *given)


def per_device(global_weights, local_weights, momentum):
    islands = lax.axis_size("island")
    shards = lax.axis_size("fsdp")
    rows, columns = global_weights.shape
    width = columns // islands
    local = local_weights[0]

    arrived = [send(pack(local, step, width), FIRST[step]) for step in (2, 1, 3)]
    base = pack(global_weights, 0, width)
    mine = pack(local, 0, width)
    parts = []
    for near in range(SIDE):
        total = base[near] - mine[near]
        for piece in arrived:
            total = total + (base[near] - piece[near])
        parts.append(total)
    got = [send(parts[step], SECOND[step]) for step in (2, 1, 3)]
    half = parts[0] + got[0] + got[1] + got[2]
    summed = half[0] + send(half[1], ACROSS)
    average = summed / islands

    count = rows * columns * shards
    squares = jnp.sum(average * average).reshape(1, 1)
    squares = jnp.broadcast_to(squares, (8, 128))
    squares = squares + send(squares, TWIN)
    for route in (FIRST, SECOND, UP):
        squares = squares + send(squares, route[1]) + send(squares, route[2]) + send(squares, route[3])
    squares = squares + send(squares, ACROSS)
    spread = jnp.sqrt(squares[0, 0] / count + 1e-06)
    factor = jnp.minimum(1.0, clip_level / spread)

    clipped = factor * average
    new_momentum = moment_decay * momentum + clipped
    updated = base[0, 0] - outer_rate * (clipped + moment_decay * new_momentum)

    both = jnp.stack([updated, send(updated, ACROSS)])
    near = [None] * SIDE
    near[0] = both
    for step in (2, 1, 3):
        near[SIDE - step] = send(both, SECOND[step])
    piece = jnp.stack(near)
    new_global = None
    others = [(SIDE - step, send(piece, FIRST[step])) for step in (2, 1, 3)]
    for place, got in [(0, piece)] + others:
        new_global = unpack(got, new_global, place, (rows, columns))
    return (new_global, new_momentum)


def solution(mesh):
    placed = (P("fsdp", None), P("island", "fsdp", None), P("fsdp", "island"))
    return jax.shard_map(
        per_device,
        mesh=mesh,
        in_specs=placed,
        out_specs=(P("fsdp", None), P("fsdp", "island")),
        check_vma=False,
    )
```

time: 440 us -> 367 us (0.83)
  waiting for transfers between devices: 325 us -> 42.9 us
  Pallas kernels: 0 us -> 261 us
  blocking collectives: 86.9 us -> 0 us
  starting transfers between devices: 0.08 us -> 52.2 us
  between operations: 14.7 us -> 1.73 us
    pallas_call x0 -> x9, Pallas kernels: none -> 261 us  [the longest x5 145 us: pack(): pl.pallas_call(functools.partial(pack_kernel, step, width), out_shape=jax...]
    reduce_scatter x1 -> x0, waiting for transfers between devices: 222 us -> none  [per_device(): summed = lax.psum_scatter(pseudo, 'island', scatter_dimension=1, tiled=True)]
    all_gather x1 -> x0, waiting for transfers between devices: 102 us -> none  [per_device(): new_global = lax.all_gather(updated, 'island', axis=1, tiled=True)]
    psum x1 -> x0, blocking collectives: 86.9 us -> none  [per_device(): squares = lax.psum(jnp.sum(average * average), ('island', 'fsdp'))]
    ppermute x0 -> x25, starting transfers between devices: none -> 52.2 us  [send(): return lax.ppermute(value, AXES, route)]
    ppermute x0 -> x25, waiting for transfers between devices: none -> 42.9 us  [send(): return lax.ppermute(value, AXES, route)]
    sub x2 -> x1, other arithmetic: 7.03 us -> 1.59 us  [per_device(): updated = base[0, 0] - outer_rate * (clipped + moment_decay * new_momentum)]
  transfers between devices with their start and end apart: 2 -> 25, of which waited for: 2 -> 15; matrix products, arithmetic and copies ran while one was open for 0% -> 0% of each run, Pallas kernels for 0% -> 55%
where the time goes in v1:
time: 367 us
  Pallas kernels  261 us (71%)
  starting transfers between devices  52.2 us (14%)
  waiting for transfers between devices  42.9 us (12%)
  other arithmetic  6.42 us (2%)
    pallas_call x5, Pallas kernels, pack(): pl.pallas_call(functools.partial(pack_kernel, step, width), out_shape=jax...  145 us
    pallas_call x4, Pallas kernels, unpack(): pl.pallas_call(functools.partial(unpack_kernel, step, width), out_shape=j...  116 us
    ppermute x25, starting transfers between devices, send(): return lax.ppermute(value, AXES, route)  52.2 us
    ppermute x25, waiting for transfers between devices, send(): return lax.ppermute(value, AXES, route)  42.9 us
  transfers between devices with their start and end apart: 25, of which 15 were waited for; matrix products, arithmetic and copies ran while one was open for 0% of the time, Pallas kernels for 55%

profile of v1, /device:TPU:2, one launch (start us, length us, event | category | flops | bytes accessed | tf_op | source)
XLA Modules:
  0.0 367.0 jit_solution(2868226973758362373)
XLA Ops:
  0.6 29.0 %pack2.1 = f32[4,2,32,896]{3,2,1,0:T(8,128)} custom-call(f32[32,28672]{1,0:T(8,128)} %bitcast.40), custom_call_target="tpu_custom_call" | custom-call | bytes 1835008 | tf_op jit(solution)/shard_map/pack2/pallas_call | solution.py:82
  29.6 2.2 collective-permute-start
  31.8 29.0 %pack1.1 = f32[4,2,32,896]{3,2,1,0:T(8,128)} custom-call(f32[32,28672]{1,0:T(8,128)} %bitcast.41), custom_call_target="tpu_custom_call" | custom-call | bytes 1835008 | tf_op jit(solution)/shard_map/pack1/pallas_call | solution.py:82
  60.8 1.7 collective-permute-start.1
  62.5 29.0 %pack3.1 = f32[4,2,32,896]{3,2,1,0:T(8,128)} custom-call(f32[32,28672]{1,0:T(8,128)} %bitcast.42), custom_call_target="tpu_custom_call" | custom-call | bytes 1835008 | tf_op jit(solution)/shard_map/pack3/pallas_call | solution.py:82
  91.5 0.5 collective-permute-start.2
  92.0 29.0 %pack0.3 = f32[4,2,32,896]{3,2,1,0:T(8,128)} custom-call(f32[32,28672]{1,0:T(8,128)} %bitcast.43), custom_call_target="tpu_custom_call" | custom-call | bytes 1835008 | tf_op jit(solution)/shard_map/pack0/pallas_call | solution.py:82
  121.0 29.0 %pack0.2 = f32[4,2,32,896]{3,2,1,0:T(8,128)} custom-call(f32[32,28672]{1,0:T(8,128)} %whole.1), custom_call_target="tpu_custom_call" | custom-call | bytes 1835008 | tf_op jit(solution)/shard_map/pack0/pallas_call | solution.py:82
  150.0 0.0 copy-start.4
  150.0 0.0 collective-permute-done
  150.0 0.0 collective-permute-done.1
  150.0 1.7 fusion.9
  151.7 3.3 collective-permute-start.3
  155.0 0.7 collective-permute-start.4
  155.6 2.6 collective-permute-start.5
  158.2 1.1 collective-permute-done.3
  159.3 2.9 collective-permute-done.4
  162.2 0.0 collective-permute-done.5
  162.2 1.1 fusion.16
  163.3 7.3 %collective-permute-start.6 = (f32[32,896]{1,0:T(8,128)S(1)}, f32[32,896]{1,0:T(8,128)S(1)}, u32[]{:S(2)}, u32[]{:S(2)}) collective-permute-start(f32[32,896]{1,0:T(8,128)S(1)} %slice_bitcast_fusion), channel_id=1, source_target_pairs={{0,128},{1,129},{2,130},{3,131},{4,132},{5,133},{6,134},{7,135},{8... | collective-permute-start | bytes 344072 | tf_op jit(solution)/shard_map/ppermute | solution.py:48
  170.6 3.5 collective-permute-done.6
  174.1 0.6 multiply_reduce_fusion
  174.7 0.6 broadcast_in_dim.2
  175.4 0.1 collective-permute-start.7
  175.5 1.2 collective-permute-done.7
  176.6 0.6 broadcast_add_fusion
  177.3 2.4 collective-permute-start.10
  179.7 2.9 collective-permute-start.9
  182.5 0.0 collective-permute-done.10
  182.5 0.7 collective-permute-done.8
  183.3 1.5 collective-permute-done.9
  184.8 0.7 add_add_fusion.2
  185.4 1.7 collective-permute-start.11
  187.2 3.1 collective-permute-start.12
  190.2 0.0 collective-permute-start.13
  190.2 0.1 collective-permute-done.11
  190.4 1.9 collective-permute-done.12
  192.3 1.6 collective-permute-done.13
  193.8 1.4 collective-permute-start.14
  195.3 2.1 collective-permute-start.15
  197.4 2.2 collective-permute-start.16
  199.6 0.2 collective-permute-done.15
  199.8 1.2 collective-permute-done.16
  201.0 5.3 %collective-permute-start.17 = (f32[8,128]{1,0:T(8,128)S(1)}, f32[8,128]{1,0:T(8,128)S(1)}, u32[]{:S(2)}, u32[]{:S(2)}) collective-permute-start(f32[8,128]{1,0:T(8,128)S(1)} %add_add_fusion), channel_id=1, source_target_pairs={{0,128},{1,129},{2,130},{3,131},{4,132},{5,133},{6,134},{7,135},{8... | collective-permute-start | bytes 12296 | tf_op jit(solution)/shard_map/ppermute | solution.py:48
  206.3 2.2 collective-permute-done.17
  208.5 0.5 slice.107
  209.7 1.6 fusion.20
  211.3 5.3 %collective-permute-start.18 = (f32[32,896]{1,0:T(8,128)S(1)}, f32[32,896]{1,0:T(8,128)S(1)}, u32[]{:S(2)}, u32[]{:S(2)}) collective-permute-start(f32[32,896]{1,0:T(8,128)S(1)} %get-tuple-element.2), channel_id=1, source_target_pairs={{0,128},{1,129},{2,130},{3,131},{4,132},{5,133},{6,134},{7,135},{8... | collective-permute-start | bytes 344072 | tf_op jit(solution)/shard_map/ppermute | solution.py:48
  216.6 3.6 collective-permute-done.18
  220.2 2.2 collective-permute-start.19
  222.4 0.7 collective-permute-start.20
  223.1 0.3 collective-permute-start.21
  223.4 15.2 %collective-permute-done.19 = f32[2,32,896]{2,1,0:T(8,128)S(1)} collective-permute-done((f32[2,32,896]{2,1,0:T(8,128)S(1)}, f32[2,32,896]{2,1,0:T(8,128)S(1)}, u32[]{:S(2)}, u32[]{:S(2)}) %collective-permute-start.19) | collective-permute-done | bytes 229408 | tf_op jit(solution)/shard_map/ppermute | solution.py:48
  238.6 6.0 %collective-permute-done.21 = f32[2,32,896]{2,1,0:T(8,128)S(1)} collective-permute-done((f32[2,32,896]{2,1,0:T(8,128)S(1)}, f32[2,32,896]{2,1,0:T(8,128)S(1)}, u32[]{:S(2)}, u32[]{:S(2)}) %collective-permute-start.21) | collective-permute-done | bytes 229408 | tf_op jit(solution)/shard_map/ppermute | solution.py:48
  244.6 0.1 pad_maximum_fusion.piece
  244.7 2.3 collective-permute-start.24
  247.0 0.5 collective-permute-start.23
  247.5 1.5 collective-permute-start.22
  249.0 29.0 %unpack0.1.rest_0_ = f32[32,28672]{1,0:T(8,128)} custom-call(f32[4,2,32,896]{3,2,1,0:T(8,128)} %copy-done), custom_call_target="tpu_custom_call" | custom-call | bytes 1835008 | tf_op jit(solution)/shard_map/unpack0/pallas_call | solution.py:111
  278.0 29.0 %unpack2.1.rest_0_ = f32[32,28672]{1,0:T(8,128)} custom-call(f32[4,2,32,896]{3,2,1,0:T(8,128)} %collective-permute-done.24.piece, f32[32,28672]{1,0:T(8,128)} %unpack0.1.rest_0_), custom_call_target="tpu_custom_call", output_to_operand_aliasing={{}: (1, {})} | custom-call | bytes 1835008 | tf_op jit(solution)/shard_map/unpack2/pallas_call | solution.py:111
  307.0 0.9 copy-done.3
  308.0 29.0 %unpack3.1.rest_0_ = f32[32,28672]{1,0:T(8,128)} custom-call(f32[4,2,32,896]{3,2,1,0:T(8,128)} %copy-done.3, f32[32,28672]{1,0:T(8,128)} %unpack2.1.rest_0_), custom_call_target="tpu_custom_call", output_to_operand_aliasing={{}: (1, {})} | custom-call | bytes 1835008 | tf_op jit(solution)/shard_map/unpack3/pallas_call | solution.py:111
  337.0 0.9 copy-done.2
  337.9 29.0 %unpack1.1 = f32[32,28672]{1,0:T(8,128)} custom-call(f32[4,2,32,896]{3,2,1,0:T(8,128)} %copy-done.2, f32[32,28672]{1,0:T(8,128)} %unpack3.1.rest_0_), custom_call_target="tpu_custom_call", output_to_operand_aliasing={{}: (1, {})} | custom-call | bytes 1835008 | tf_op jit(solution)/shard_map/unpack1/pallas_call | solution.py:111
  (19 shorter events, 0.1 us)
Async XLA Ops:
  29.6 120.3 %collective-permute-start = (f32[4,2,32,896]{3,2,1,0:T(8,128)}, f32[4,2,32,896]{3,2,1,0:T(8,128)S(1)}, u32[]{:S(2)}, u32[]{:S(2)}) collective-permute-start(f32[4,2,32,896]{3,2,1,0:T(8,128)} %pack2.1), channel_id=1, source_target_pairs={{0,64},{1,17},{2,66},{3,19},{4,68},{5,21},{6,70},{7,23},{8,72},{9,... | collective-permute-start | bytes 2752520 | tf_op jit(solution)/shard_map/ppermute | solution.py:48
  60.8 89.2 %collective-permute-start.1 = (f32[4,2,32,896]{3,2,1,0:T(8,128)}, f32[4,2,32,896]{3,2,1,0:T(8,128)S(1)}, u32[]{:S(2)}, u32[]{:S(2)}) collective-permute-start(f32[4,2,32,896]{3,2,1,0:T(8,128)} %pack1.1), channel_id=1, source_target_pairs={{0,32},{1,9},{2,34},{3,11},{4,36},{5,13},{6,38},{7,15},{8,40},{9,1... | collective-permute-start | bytes 2752520 | tf_op jit(solution)/shard_map/ppermute | solution.py:48
  91.5 58.5 %collective-permute-start.2 = (f32[4,2,32,896]{3,2,1,0:T(8,128)}, f32[4,2,32,896]{3,2,1,0:T(8,128)}, u32[]{:S(2)}, u32[]{:S(2)}) collective-permute-start(f32[4,2,32,896]{3,2,1,0:T(8,128)} %pack3.1), channel_id=1, source_target_pairs={{0,96},{1,25},{2,98},{3,27},{4,100},{5,29},{6,102},{7,31},{8,104},... | collective-permute-start | bytes 2752520 | tf_op jit(solution)/shard_map/ppermute | solution.py:48
  120.9 29.1 %copy-start.1 = (f32[4,2,32,896]{3,2,1,0:T(8,128)S(1)}, f32[4,2,32,896]{3,2,1,0:T(8,128)}, u32[]{:S(2)}) copy-start(f32[4,2,32,896]{3,2,1,0:T(8,128)} %pack0.3) | copy-start | bytes 2752516
  150.0 59.8 %copy-start.4 = (f32[32,896]{1,0:T(8,128)S(1)}, f32[32,896]{1,0:T(8,128)}, u32[]{:S(2)}) copy-start(f32[32,896]{1,0:T(8,128)} %param.5) | copy-start | bytes 344068
  151.7 7.6 %collective-permute-start.3 = (f32[2,32,896]{2,1,0:T(8,128)S(1)}, f32[2,32,896]{2,1,0:T(8,128)S(1)}, u32[]{:S(2)}, u32[]{:S(2)}) collective-permute-start(f32[2,32,896]{2,1,0:T(8,128)S(1)} %get-tuple-element.4), channel_id=1, source_target_pairs={{0,16},{1,65},{2,18},{3,67},{4,20},{5,69},{6,22},{7,71},{8,24},{9,... | collective-permute-start | bytes 688136 | tf_op jit(solution)/shard_map/ppermute | solution.py:48
  155.0 7.2 %collective-permute-start.4 = (f32[2,32,896]{2,1,0:T(8,128)S(1)}, f32[2,32,896]{2,1,0:T(8,128)S(1)}, u32[]{:S(2)}, u32[]{:S(2)}) collective-permute-start(f32[2,32,896]{2,1,0:T(8,128)S(1)} %get-tuple-element.6), channel_id=1, source_target_pairs={{0,8},{1,33},{2,10},{3,35},{4,12},{5,37},{6,14},{7,39},{8,16},{9,4... | collective-permute-start | bytes 688136 | tf_op jit(solution)/shard_map/ppermute | solution.py:48
  155.6 6.6 %collective-permute-start.5 = (f32[2,32,896]{2,1,0:T(8,128)S(1)}, f32[2,32,896]{2,1,0:T(8,128)S(1)}, u32[]{:S(2)}, u32[]{:S(2)}) collective-permute-start(f32[2,32,896]{2,1,0:T(8,128)S(1)} %get-tuple-element.5), channel_id=1, source_target_pairs={{0,24},{1,97},{2,26},{3,99},{4,28},{5,101},{6,30},{7,103},{8,0},{9... | collective-permute-start | bytes 688136 | tf_op jit(solution)/shard_map/ppermute | solution.py:48
  163.3 10.7 %collective-permute-start.6 = (f32[32,896]{1,0:T(8,128)S(1)}, f32[32,896]{1,0:T(8,128)S(1)}, u32[]{:S(2)}, u32[]{:S(2)}) collective-permute-start(f32[32,896]{1,0:T(8,128)S(1)} %slice_bitcast_fusion), channel_id=1, source_target_pairs={{0,128},{1,129},{2,130},{3,131},{4,132},{5,133},{6,134},{7,135},{8... | collective-permute-start | bytes 344072 | tf_op jit(solution)/shard_map/ppermute | solution.py:48
  175.4 1.3 collective-permute-start.7
  177.3 5.3 %collective-permute-start.10 = (f32[8,128]{1,0:T(8,128)S(1)}, f32[8,128]{1,0:T(8,128)S(1)}, u32[]{:S(2)}, u32[]{:S(2)}) collective-permute-start(f32[8,128]{1,0:T(8,128)S(1)} %broadcast_add_fusion), channel_id=1, source_target_pairs={{0,96},{1,25},{2,98},{3,27},{4,100},{5,29},{6,102},{7,31},{8,104},... | collective-permute-start | bytes 12296 | tf_op jit(solution)/shard_map/ppermute | solution.py:48
  179.7 3.6 collective-permute-start.8
  179.7 5.1 %collective-permute-start.9 = (f32[8,128]{1,0:T(8,128)S(1)}, f32[8,128]{1,0:T(8,128)S(1)}, u32[]{:S(2)}, u32[]{:S(2)}) collective-permute-start(f32[8,128]{1,0:T(8,128)S(1)} %broadcast_add_fusion), channel_id=1, source_target_pairs={{0,64},{1,17},{2,66},{3,19},{4,68},{5,21},{6,70},{7,23},{8,72},{9,... | collective-permute-start | bytes 12296 | tf_op jit(solution)/shard_map/ppermute | solution.py:48
  185.4 4.9 %collective-permute-start.11 = (f32[8,128]{1,0:T(8,128)S(1)}, f32[8,128]{1,0:T(8,128)S(1)}, u32[]{:S(2)}, u32[]{:S(2)}) collective-permute-start(f32[8,128]{1,0:T(8,128)S(1)} %add_add_fusion.2), channel_id=1, source_target_pairs={{0,8},{1,33},{2,10},{3,35},{4,12},{5,37},{6,14},{7,39},{8,16},{9,4... | collective-permute-start | bytes 12296 | tf_op jit(solution)/shard_map/ppermute | solution.py:48
  187.2 5.1 %collective-permute-start.12 = (f32[8,128]{1,0:T(8,128)S(1)}, f32[8,128]{1,0:T(8,128)S(1)}, u32[]{:S(2)}, u32[]{:S(2)}) collective-permute-start(f32[8,128]{1,0:T(8,128)S(1)} %add_add_fusion.2), channel_id=1, source_target_pairs={{0,16},{1,65},{2,18},{3,67},{4,20},{5,69},{6,22},{7,71},{8,24},{9,... | collective-permute-start | bytes 12296 | tf_op jit(solution)/shard_map/ppermute | solution.py:48
  190.2 3.6 collective-permute-start.13
  193.8 5.8 %collective-permute-start.14 = (f32[8,128]{1,0:T(8,128)S(1)}, f32[8,128]{1,0:T(8,128)S(1)}, u32[]{:S(2)}, u32[]{:S(2)}) collective-permute-start(f32[8,128]{1,0:T(8,128)S(1)} %add_add_fusion.1), channel_id=1, source_target_pairs={{0,2},{1,3},{2,4},{3,5},{4,6},{5,7},{6,0},{7,1},{8,10},{9,11},{10,... | collective-permute-start | bytes 12296 | tf_op jit(solution)/shard_map/ppermute | solution.py:48
  195.3 4.5 %collective-permute-start.15 = (f32[8,128]{1,0:T(8,128)S(1)}, f32[8,128]{1,0:T(8,128)S(1)}, u32[]{:S(2)}, u32[]{:S(2)}) collective-permute-start(f32[8,128]{1,0:T(8,128)S(1)} %add_add_fusion.1), channel_id=1, source_target_pairs={{0,4},{1,5},{2,6},{3,7},{4,0},{5,1},{6,2},{7,3},{8,12},{9,13},{10,... | collective-permute-start | bytes 12296 | tf_op jit(solution)/shard_map/ppermute | solution.py:48
  197.4 3.6 collective-permute-start.16
  201.0 7.5 %collective-permute-start.17 = (f32[8,128]{1,0:T(8,128)S(1)}, f32[8,128]{1,0:T(8,128)S(1)}, u32[]{:S(2)}, u32[]{:S(2)}) collective-permute-start(f32[8,128]{1,0:T(8,128)S(1)} %add_add_fusion), channel_id=1, source_target_pairs={{0,128},{1,129},{2,130},{3,131},{4,132},{5,133},{6,134},{7,135},{8... | collective-permute-start | bytes 12296 | tf_op jit(solution)/shard_map/ppermute | solution.py:48
  211.3 8.9 %collective-permute-start.18 = (f32[32,896]{1,0:T(8,128)S(1)}, f32[32,896]{1,0:T(8,128)S(1)}, u32[]{:S(2)}, u32[]{:S(2)}) collective-permute-start(f32[32,896]{1,0:T(8,128)S(1)} %get-tuple-element.2), channel_id=1, source_target_pairs={{0,128},{1,129},{2,130},{3,131},{4,132},{5,133},{6,134},{7,135},{8... | collective-permute-start | bytes 344072 | tf_op jit(solution)/shard_map/ppermute | solution.py:48
  220.2 18.3 %collective-permute-start.19 = (f32[2,32,896]{2,1,0:T(8,128)S(1)}, f32[2,32,896]{2,1,0:T(8,128)S(1)}, u32[]{:S(2)}, u32[]{:S(2)}) collective-permute-start(f32[2,32,896]{2,1,0:T(8,128)S(1)} %get-tuple-element.8), channel_id=1, source_target_pairs={{0,24},{1,97},{2,26},{3,99},{4,28},{5,101},{6,30},{7,103},{8,0},{9... | collective-permute-start | bytes 688136 | tf_op jit(solution)/shard_map/ppermute | solution.py:48
  222.4 16.2 %collective-permute-start.20 = (f32[2,32,896]{2,1,0:T(8,128)S(1)}, f32[2,32,896]{2,1,0:T(8,128)S(1)}, u32[]{:S(2)}, u32[]{:S(2)}) collective-permute-start(f32[2,32,896]{2,1,0:T(8,128)S(1)} %get-tuple-element.8), channel_id=1, source_target_pairs={{0,16},{1,65},{2,18},{3,67},{4,20},{5,69},{6,22},{7,71},{8,24},{9,... | collective-permute-start | bytes 688136 | tf_op jit(solution)/shard_map/ppermute | solution.py:48
  223.1 21.5 %collective-permute-start.21 = (f32[2,32,896]{2,1,0:T(8,128)S(1)}, f32[2,32,896]{2,1,0:T(8,128)S(1)}, u32[]{:S(2)}, u32[]{:S(2)}) collective-permute-start(f32[2,32,896]{2,1,0:T(8,128)S(1)} %get-tuple-element.8), channel_id=1, source_target_pairs={{0,8},{1,33},{2,10},{3,35},{4,12},{5,37},{6,14},{7,39},{8,16},{9,4... | collective-permute-start | bytes 688136 | tf_op jit(solution)/shard_map/ppermute | solution.py:48
  244.7 4.4 %copy-start = (f32[4,2,32,896]{3,2,1,0:T(8,128)}, f32[4,2,32,896]{3,2,1,0:T(8,128)S(1)}, u32[]{:S(2)}) copy-start(f32[4,2,32,896]{3,2,1,0:T(8,128)S(1)} %pad_maximum_fusion.piece) | copy-start | bytes 2752516
  244.7 33.3 %collective-permute-start.24 = (f32[4,2,32,896]{3,2,1,0:T(8,128)S(1)}, f32[4,2,32,896]{3,2,1,0:T(8,128)}, u32[]{:S(2)}, u32[]{:S(2)}) collective-permute-start(f32[4,2,32,896]{3,2,1,0:T(8,128)S(1)} %pad_maximum_fusion.piece), channel_id=1, source_target_pairs={{0,64},{1,17},{2,66},{3,19},{4,68},{5,21},{6,70},{7,23},{8,72},{9,... | collective-permute-start | bytes 2752520 | tf_op jit(solution)/shard_map/ppermute | solution.py:48
  247.0 60.0 %collective-permute-start.23 = (f32[4,2,32,896]{3,2,1,0:T(8,128)S(1)}, f32[4,2,32,896]{3,2,1,0:T(8,128)S(1)}, u32[]{:S(2)}, u32[]{:S(2)}) collective-permute-start(f32[4,2,32,896]{3,2,1,0:T(8,128)S(1)} %pad_maximum_fusion.piece), channel_id=1, source_target_pairs={{0,32},{1,9},{2,34},{3,11},{4,36},{5,13},{6,38},{7,15},{8,40},{9,1... | collective-permute-start | bytes 2752520 | tf_op jit(solution)/shard_map/ppermute | solution.py:48
  247.5 89.5 %collective-permute-start.22 = (f32[4,2,32,896]{3,2,1,0:T(8,128)S(1)}, f32[4,2,32,896]{3,2,1,0:T(8,128)S(1)}, u32[]{:S(2)}, u32[]{:S(2)}) collective-permute-start(f32[4,2,32,896]{3,2,1,0:T(8,128)S(1)} %pad_maximum_fusion.piece), channel_id=1, source_target_pairs={{0,96},{1,25},{2,98},{3,27},{4,100},{5,29},{6,102},{7,31},{8,104},... | collective-permute-start | bytes 2752520 | tf_op jit(solution)/shard_map/ppermute | solution.py:48
  307.0 1.0 copy-start.3
  337.0 1.0 copy-start.2

commit v2 on v1

--- a/solution.py
+++ b/solution.py
@@ -82,8 +82,8 @@
     return pl.pallas_call(
         functools.partial(pack_kernel, step, width),
         out_shape=jax.ShapeDtypeStruct((SIDE, HALVES, rows, width), whole.dtype),
-        in_specs=[pl.BlockSpec(memory_space=pl.ANY)],
-        out_specs=pl.BlockSpec(memory_space=pl.ANY),
+        in_specs=[pl.BlockSpec(memory_space=pltpu.HBM)],
+        out_specs=pl.BlockSpec(memory_space=pltpu.VMEM),
         scratch_shapes=[pltpu.SemaphoreType.DMA((SIDE * HALVES,))],
         cost_estimate=pl.CostEstimate(flops=0, bytes_accessed=2 * 4 * SIDE * HALVES * rows * width, transcendentals=0),
         name=f"pack{step}",
@@ -111,8 +111,8 @@
     return pl.pallas_call(
         functools.partial(unpack_kernel, step, width),
         out_shape=jax.ShapeDtypeStruct(shape, piece.dtype),
-        in_specs=[pl.BlockSpec(memory_space=pl.ANY)] * (1 + len(given)),
-        out_specs=pl.BlockSpec(memory_space=pl.ANY),
+        in_specs=[pl.BlockSpec(memory_space=pltpu.VMEM)] + [pl.BlockSpec(memory_space=pltpu.HBM)] * len(given),
+        out_specs=pl.BlockSpec(memory_space=pltpu.HBM),
         scratch_shapes=[pltpu.SemaphoreType.DMA((SIDE * HALVES,))],
         input_output_aliases={1: 0} if given else {},
         cost_estimate=pl.CostEstimate(flops=0, bytes_accessed=2 * 4 * SIDE * HALVES * rows * width, transcendentals=0),

time: 367 us -> 153 us (0.42)
  Pallas kernels: 261 us -> 20 us
  waiting for transfers between devices: 42.9 us -> 69.2 us
    pallas_call x5, Pallas kernels: 145 us -> 11.4 us  [pack(): pl.pallas_call(functools.partial(pack_kernel, step, width), out_shape=jax...]
    pallas_call x4, Pallas kernels: 116 us -> 8.62 us  [unpack(): pl.pallas_call(functools.partial(unpack_kernel, step, width), out_shape=j...]
    ppermute x25, waiting for transfers between devices: 42.9 us -> 69.2 us  [send(): return lax.ppermute(value, AXES, route)]
  transfers between devices with their start and end apart: 25 -> 25, of which waited for: 15 -> 18; matrix products, arithmetic and copies ran while one was open for 0% -> 0% of each run, Pallas kernels for 55% -> 10%
where the time goes in v2:
time: 153 us
  waiting for transfers between devices  69.2 us (45%)
  starting transfers between devices  52.3 us (34%)
  Pallas kernels  20 us (13%)
  other arithmetic  6.41 us (4%)
  local copies, waits for them, and re-layouts  3.08 us (2%)
  between operations  1.68 us (1%)
    ppermute x25, waiting for transfers between devices, send(): return lax.ppermute(value, AXES, route)  69.2 us
    ppermute x25, starting transfers between devices, send(): return lax.ppermute(value, AXES, route)  52.3 us
    pallas_call x5, Pallas kernels, pack(): pl.pallas_call(functools.partial(pack_kernel, step, width), out_shape=jax...  11.4 us
    pallas_call x4, Pallas kernels, unpack(): pl.pallas_call(functools.partial(unpack_kernel, step, width), out_shape=j...  8.62 us
  transfers between devices with their start and end apart: 25, of which 18 were waited for; matrix products, arithmetic and copies ran while one was open for 0% of the time, Pallas kernels for 10%

profile of v2, /device:TPU:2, one launch (start us, length us, event | category | flops | bytes accessed | tf_op | source)
XLA Modules:
  0.0 152.7 jit_solution(14533881540166901342)
XLA Ops:
  0.6 2.3 %pack2.1 = f32[4,2,32,896]{3,2,1,0:T(8,128)} custom-call(f32[32,28672]{1,0:T(8,128)} %bitcast.40), custom_call_target="tpu_custom_call" | custom-call | bytes 1835008 | tf_op jit(solution)/shard_map/pack2/pallas_call | solution.py:82
  2.9 2.2 %collective-permute-start = (f32[4,2,32,896]{3,2,1,0:T(8,128)}, f32[4,2,32,896]{3,2,1,0:T(8,128)S(1)}, u32[]{:S(2)}, u32[]{:S(2)}) collective-permute-start(f32[4,2,32,896]{3,2,1,0:T(8,128)} %pack2.1), channel_id=1, source_target_pairs={{0,64},{1,17},{2,66},{3,19},{4,68},{5,21},{6,70},{7,23},{8,72},{9,... | collective-permute-start | bytes 2752520 | tf_op jit(solution)/shard_map/ppermute | solution.py:48
  5.1 2.3 %pack1.1 = f32[4,2,32,896]{3,2,1,0:T(8,128)} custom-call(f32[32,28672]{1,0:T(8,128)} %bitcast.41), custom_call_target="tpu_custom_call" | custom-call | bytes 1835008 | tf_op jit(solution)/shard_map/pack1/pallas_call | solution.py:82
  7.4 1.7 %collective-permute-start.1 = (f32[4,2,32,896]{3,2,1,0:T(8,128)}, f32[4,2,32,896]{3,2,1,0:T(8,128)S(1)}, u32[]{:S(2)}, u32[]{:S(2)}) collective-permute-start(f32[4,2,32,896]{3,2,1,0:T(8,128)} %pack1.1), channel_id=1, source_target_pairs={{0,32},{1,9},{2,34},{3,11},{4,36},{5,13},{6,38},{7,15},{8,40},{9,1... | collective-permute-start | bytes 2752520 | tf_op jit(solution)/shard_map/ppermute | solution.py:48
  9.1 2.2 %pack3.1 = f32[4,2,32,896]{3,2,1,0:T(8,128)} custom-call(f32[32,28672]{1,0:T(8,128)} %bitcast.42), custom_call_target="tpu_custom_call" | custom-call | bytes 1835008 | tf_op jit(solution)/shard_map/pack3/pallas_call | solution.py:82
  11.4 0.5 collective-permute-start.2
  11.9 2.2 %pack0.3 = f32[4,2,32,896]{3,2,1,0:T(8,128)} custom-call(f32[32,28672]{1,0:T(8,128)} %bitcast.43), custom_call_target="tpu_custom_call" | custom-call | bytes 1835008 | tf_op jit(solution)/shard_map/pack0/pallas_call | solution.py:82
  14.1 2.3 %pack0.2 = f32[4,2,32,896]{3,2,1,0:T(8,128)} custom-call(f32[32,28672]{1,0:T(8,128)} %whole.1), custom_call_target="tpu_custom_call" | custom-call | bytes 1835008 | tf_op jit(solution)/shard_map/pack0/pallas_call | solution.py:82
  16.5 0.0 copy-start.4
  16.5 1.7 %collective-permute-done = f32[4,2,32,896]{3,2,1,0:T(8,128)S(1)} collective-permute-done((f32[4,2,32,896]{3,2,1,0:T(8,128)}, f32[4,2,32,896]{3,2,1,0:T(8,128)S(1)}, u32[]{:S(2)}, u32[]{:S(2)}) %collective-permute-start) | collective-permute-done | bytes 917536 | tf_op jit(solution)/shard_map/ppermute | solution.py:48
  18.2 9.8 %collective-permute-done.1 = f32[4,2,32,896]{3,2,1,0:T(8,128)S(1)} collective-permute-done((f32[4,2,32,896]{3,2,1,0:T(8,128)}, f32[4,2,32,896]{3,2,1,0:T(8,128)S(1)}, u32[]{:S(2)}, u32[]{:S(2)}) %collective-permute-start.1) | collective-permute-done | bytes 917536 | tf_op jit(solution)/shard_map/ppermute | solution.py:48
  28.0 0.0 collective-permute-done.2
  28.1 1.7 %fusion.9 = (f32[2,32,896]{2,1,0:T(8,128)S(1)}, f32[2,32,896]{2,1,0:T(8,128)S(1)}, f32[2,32,896]{2,1,0:T(8,128)S(1)}) fusion(f32[4,2,32,896]{3,2,1,0:T(8,128)} %collective-permute-done.2, f32[4,2,32,896]{3,2,1,0:T(8,128)S(1)} %collective-permute-done.1, f32[4,2,32,896]{3,2,1,0:T(8,128)S(1)} %collective-permute-done, f32[4,2,32,896]{3,2,1,0:T(8,128)S(1)} %copy-done.1, ...), kind=kLoop, calls=%fused_computation.19 | loop fusion | flops 1204224 | bytes 4128768 | tf_op jit(solution)/shard_map/add | solution.py:137
  29.7 3.3 %collective-permute-start.3 = (f32[2,32,896]{2,1,0:T(8,128)S(1)}, f32[2,32,896]{2,1,0:T(8,128)S(1)}, u32[]{:S(2)}, u32[]{:S(2)}) collective-permute-start(f32[2,32,896]{2,1,0:T(8,128)S(1)} %get-tuple-element.4), channel_id=1, source_target_pairs={{0,16},{1,65},{2,18},{3,67},{4,20},{5,69},{6,22},{7,71},{8,24},{9,... | collective-permute-start | bytes 688136 | tf_op jit(solution)/shard_map/ppermute | solution.py:48
  33.0 0.7 collective-permute-start.4
  33.7 2.6 %collective-permute-start.5 = (f32[2,32,896]{2,1,0:T(8,128)S(1)}, f32[2,32,896]{2,1,0:T(8,128)S(1)}, u32[]{:S(2)}, u32[]{:S(2)}) collective-permute-start(f32[2,32,896]{2,1,0:T(8,128)S(1)} %get-tuple-element.5), channel_id=1, source_target_pairs={{0,24},{1,97},{2,26},{3,99},{4,28},{5,101},{6,30},{7,103},{8,0},{9... | collective-permute-start | bytes 688136 | tf_op jit(solution)/shard_map/ppermute | solution.py:48
  36.2 1.1 collective-permute-done.3
  37.3 2.9 %collective-permute-done.4 = f32[2,32,896]{2,1,0:T(8,128)S(1)} collective-permute-done((f32[2,32,896]{2,1,0:T(8,128)S(1)}, f32[2,32,896]{2,1,0:T(8,128)S(1)}, u32[]{:S(2)}, u32[]{:S(2)}) %collective-permute-start.4) | collective-permute-done | bytes 229408 | tf_op jit(solution)/shard_map/ppermute | solution.py:48
  40.2 0.0 collective-permute-done.5
  40.2 1.1 fusion.16
  41.4 7.3 %collective-permute-start.6 = (f32[32,896]{1,0:T(8,128)S(1)}, f32[32,896]{1,0:T(8,128)S(1)}, u32[]{:S(2)}, u32[]{:S(2)}) collective-permute-start(f32[32,896]{1,0:T(8,128)S(1)} %slice_bitcast_fusion), channel_id=1, source_target_pairs={{0,128},{1,129},{2,130},{3,131},{4,132},{5,133},{6,134},{7,135},{8... | collective-permute-start | bytes 344072 | tf_op jit(solution)/shard_map/ppermute | solution.py:48
  48.7 3.1 %collective-permute-done.6 = f32[32,896]{1,0:T(8,128)S(1)} collective-permute-done((f32[32,896]{1,0:T(8,128)S(1)}, f32[32,896]{1,0:T(8,128)S(1)}, u32[]{:S(2)}, u32[]{:S(2)}) %collective-permute-start.6) | collective-permute-done | bytes 114720 | tf_op jit(solution)/shard_map/ppermute | solution.py:48
  51.8 0.6 multiply_reduce_fusion
  52.4 0.6 broadcast_in_dim.2
  53.1 0.1 collective-permute-start.7
  53.2 1.2 collective-permute-done.7
  54.3 0.6 broadcast_add_fusion
  55.0 0.7 collective-permute-start.10
  55.7 1.5 collective-permute-start.8
  57.2 3.2 %collective-permute-start.9 = (f32[8,128]{1,0:T(8,128)S(1)}, f32[8,128]{1,0:T(8,128)S(1)}, u32[]{:S(2)}, u32[]{:S(2)}) collective-permute-start(f32[8,128]{1,0:T(8,128)S(1)} %broadcast_add_fusion), channel_id=1, source_target_pairs={{0,64},{1,17},{2,66},{3,19},{4,68},{5,21},{6,70},{7,23},{8,72},{9,... | collective-permute-start | bytes 12296 | tf_op jit(solution)/shard_map/ppermute | solution.py:48
  60.4 1.9 %collective-permute-done.9 = f32[8,128]{1,0:T(8,128)S(1)} collective-permute-done((f32[8,128]{1,0:T(8,128)S(1)}, f32[8,128]{1,0:T(8,128)S(1)}, u32[]{:S(2)}, u32[]{:S(2)}) %collective-permute-start.9) | collective-permute-done | bytes 4128 | tf_op jit(solution)/shard_map/ppermute | solution.py:48
  62.3 0.7 add_add_fusion.2
  63.0 1.4 collective-permute-start.11
  64.3 3.9 %collective-permute-start.12 = (f32[8,128]{1,0:T(8,128)S(1)}, f32[8,128]{1,0:T(8,128)S(1)}, u32[]{:S(2)}, u32[]{:S(2)}) collective-permute-start(f32[8,128]{1,0:T(8,128)S(1)} %add_add_fusion.2), channel_id=1, source_target_pairs={{0,16},{1,65},{2,18},{3,67},{4,20},{5,69},{6,22},{7,71},{8,24},{9,... | collective-permute-start | bytes 12296 | tf_op jit(solution)/shard_map/ppermute | solution.py:48
  68.3 0.1 collective-permute-done.11
  68.4 1.5 collective-permute-done.12
  69.9 2.0 %collective-permute-done.13 = f32[8,128]{1,0:T(8,128)S(1)} collective-permute-done((f32[8,128]{1,0:T(8,128)S(1)}, f32[8,128]{1,0:T(8,128)S(1)}, u32[]{:S(2)}, u32[]{:S(2)}) %collective-permute-start.13) | collective-permute-done | bytes 4128 | tf_op jit(solution)/shard_map/ppermute | solution.py:48
  71.9 0.8 collective-permute-start.14
  72.7 2.2 %collective-permute-start.15 = (f32[8,128]{1,0:T(8,128)S(1)}, f32[8,128]{1,0:T(8,128)S(1)}, u32[]{:S(2)}, u32[]{:S(2)}) collective-permute-start(f32[8,128]{1,0:T(8,128)S(1)} %add_add_fusion.1), channel_id=1, source_target_pairs={{0,4},{1,5},{2,6},{3,7},{4,0},{5,1},{6,2},{7,3},{8,12},{9,13},{10,... | collective-permute-start | bytes 12296 | tf_op jit(solution)/shard_map/ppermute | solution.py:48
  74.9 1.6 %collective-permute-start.16 = (f32[8,128]{1,0:T(8,128)S(1)}, f32[8,128]{1,0:T(8,128)S(1)}, u32[]{:S(2)}, u32[]{:S(2)}) collective-permute-start(f32[8,128]{1,0:T(8,128)S(1)} %add_add_fusion.1), channel_id=1, source_target_pairs={{0,6},{1,7},{2,0},{3,1},{4,2},{5,3},{6,4},{7,5},{8,14},{9,15},{10,... | collective-permute-start | bytes 12296 | tf_op jit(solution)/shard_map/ppermute | solution.py:48
  76.5 0.8 collective-permute-done.14
  77.3 1.2 collective-permute-done.16
  78.5 5.2 %collective-permute-start.17 = (f32[8,128]{1,0:T(8,128)S(1)}, f32[8,128]{1,0:T(8,128)S(1)}, u32[]{:S(2)}, u32[]{:S(2)}) collective-permute-start(f32[8,128]{1,0:T(8,128)S(1)} %add_add_fusion), channel_id=1, source_target_pairs={{0,128},{1,129},{2,130},{3,131},{4,132},{5,133},{6,134},{7,135},{8... | collective-permute-start | bytes 12296 | tf_op jit(solution)/shard_map/ppermute | solution.py:48
  83.7 2.3 %collective-permute-done.17 = f32[8,128]{1,0:T(8,128)S(1)} collective-permute-done((f32[8,128]{1,0:T(8,128)S(1)}, f32[8,128]{1,0:T(8,128)S(1)}, u32[]{:S(2)}, u32[]{:S(2)}) %collective-permute-start.17) | collective-permute-done | bytes 4128 | tf_op jit(solution)/shard_map/ppermute | solution.py:48
  86.1 0.5 slice.107
  87.3 1.6 %fusion.20 = (f32[32,896]{1,0:T(8,128)S(1)}, f32[32,896]{1,0:T(8,128)}) fusion(f32[4,2,32,896]{3,2,1,0:T(8,128)} %pack0.2, f32[]{:T(128)} %bitcast.8, f32[32,896]{1,0:T(8,128)S(1)} %collective-permute-done.6, f32[2,32,896]{2,1,0:T(8,128)S(1)} %fusion.16, f32[32,896]{1,0:T(8,128)S(1)} %copy-done.4), kind=kLoop, calls=%fused_computation.41 | loop fusion | flops 229376 | bytes 688132 | tf_op jit(solution)/shard_map/sub | solution.py:156
  88.9 5.2 %collective-permute-start.18 = (f32[32,896]{1,0:T(8,128)S(1)}, f32[32,896]{1,0:T(8,128)S(1)}, u32[]{:S(2)}, u32[]{:S(2)}) collective-permute-start(f32[32,896]{1,0:T(8,128)S(1)} %get-tuple-element.2), channel_id=1, source_target_pairs={{0,128},{1,129},{2,130},{3,131},{4,132},{5,133},{6,134},{7,135},{8... | collective-permute-start | bytes 344072 | tf_op jit(solution)/shard_map/ppermute | solution.py:48
  94.0 3.6 %collective-permute-done.18 = f32[32,896]{1,0:T(8,128)S(1)} collective-permute-done((f32[32,896]{1,0:T(8,128)S(1)}, f32[32,896]{1,0:T(8,128)S(1)}, u32[]{:S(2)}, u32[]{:S(2)}) %collective-permute-start.18) | collective-permute-done | bytes 114720 | tf_op jit(solution)/shard_map/ppermute | solution.py:48
  97.7 2.5 %collective-permute-start.19 = (f32[2,32,896]{2,1,0:T(8,128)S(1)}, f32[2,32,896]{2,1,0:T(8,128)S(1)}, u32[]{:S(2)}, u32[]{:S(2)}) collective-permute-start(f32[2,32,896]{2,1,0:T(8,128)S(1)} %get-tuple-element.8), channel_id=1, source_target_pairs={{0,24},{1,97},{2,26},{3,99},{4,28},{5,101},{6,30},{7,103},{8,0},{9... | collective-permute-start | bytes 688136 | tf_op jit(solution)/shard_map/ppermute | solution.py:48
  100.2 1.0 collective-permute-start.21
  101.2 15.7 %collective-permute-done.19 = f32[2,32,896]{2,1,0:T(8,128)S(1)} collective-permute-done((f32[2,32,896]{2,1,0:T(8,128)S(1)}, f32[2,32,896]{2,1,0:T(8,128)S(1)}, u32[]{:S(2)}, u32[]{:S(2)}) %collective-permute-start.19) | collective-permute-done | bytes 229408 | tf_op jit(solution)/shard_map/ppermute | solution.py:48
  116.8 4.6 %collective-permute-done.21 = f32[2,32,896]{2,1,0:T(8,128)S(1)} collective-permute-done((f32[2,32,896]{2,1,0:T(8,128)S(1)}, f32[2,32,896]{2,1,0:T(8,128)S(1)}, u32[]{:S(2)}, u32[]{:S(2)}) %collective-permute-start.21) | collective-permute-done | bytes 229408 | tf_op jit(solution)/shard_map/ppermute | solution.py:48
  121.4 0.1 pad_maximum_fusion.piece
  121.5 2.8 %collective-permute-start.24 = (f32[4,2,32,896]{3,2,1,0:T(8,128)S(1)}, f32[4,2,32,896]{3,2,1,0:T(8,128)}, u32[]{:S(2)}, u32[]{:S(2)}) collective-permute-start(f32[4,2,32,896]{3,2,1,0:T(8,128)S(1)} %pad_maximum_fusion.piece), channel_id=1, source_target_pairs={{0,64},{1,17},{2,66},{3,19},{4,68},{5,21},{6,70},{7,23},{8,72},{9,... | collective-permute-start | bytes 2752520 | tf_op jit(solution)/shard_map/ppermute | solution.py:48
  124.3 0.8 collective-permute-start.23
  125.2 1.2 collective-permute-start.22
  126.4 2.2 %unpack0.1.rest_0_ = f32[32,28672]{1,0:T(8,128)} custom-call(f32[4,2,32,896]{3,2,1,0:T(8,128)} %copy-done), custom_call_target="tpu_custom_call" | custom-call | bytes 1835008 | tf_op jit(solution)/shard_map/unpack0/pallas_call | solution.py:111
  128.5 8.2 %collective-permute-done.24.piece = f32[4,2,32,896]{3,2,1,0:T(8,128)} collective-permute-done((f32[4,2,32,896]{3,2,1,0:T(8,128)S(1)}, f32[4,2,32,896]{3,2,1,0:T(8,128)}, u32[]{:S(2)}, u32[]{:S(2)}) %collective-permute-start.24) | collective-permute-done | bytes 917536 | tf_op jit(solution)/shard_map/ppermute | solution.py:48
  136.7 2.2 %unpack2.1.rest_0_ = f32[32,28672]{1,0:T(8,128)} custom-call(f32[4,2,32,896]{3,2,1,0:T(8,128)} %collective-permute-done.24.piece, f32[32,28672]{1,0:T(8,128)} %unpack0.1.rest_0_), custom_call_target="tpu_custom_call", output_to_operand_aliasing={{}: (1, {})} | custom-call | bytes 1835008 | tf_op jit(solution)/shard_map/unpack2/pallas_call | solution.py:111
  138.9 7.5 %collective-permute-done.23.piece = f32[4,2,32,896]{3,2,1,0:T(8,128)S(1)} collective-permute-done((f32[4,2,32,896]{3,2,1,0:T(8,128)S(1)}, f32[4,2,32,896]{3,2,1,0:T(8,128)S(1)}, u32[]{:S(2)}, u32[]{:S(2)}) %collective-permute-start.23) | collective-permute-done | bytes 917536 | tf_op jit(solution)/shard_map/ppermute | solution.py:48
  146.4 0.9 copy-done.3
  147.3 2.2 %unpack3.1.rest_0_ = f32[32,28672]{1,0:T(8,128)} custom-call(f32[4,2,32,896]{3,2,1,0:T(8,128)} %copy-done.3, f32[32,28672]{1,0:T(8,128)} %unpack2.1.rest_0_), custom_call_target="tpu_custom_call", output_to_operand_aliasing={{}: (1, {})} | custom-call | bytes 1835008 | tf_op jit(solution)/shard_map/unpack3/pallas_call | solution.py:111
  149.5 0.9 copy-done.2
  150.4 2.2 %unpack1.1 = f32[32,28672]{1,0:T(8,128)} custom-call(f32[4,2,32,896]{3,2,1,0:T(8,128)} %copy-done.2, f32[32,28672]{1,0:T(8,128)} %unpack3.1.rest_0_), custom_call_target="tpu_custom_call", output_to_operand_aliasing={{}: (1, {})} | custom-call | bytes 1835008 | tf_op jit(solution)/shard_map/unpack1/pallas_call | solution.py:111
  (19 shorter events, 0.1 us)
Async XLA Ops:
  2.9 15.3 %collective-permute-start = (f32[4,2,32,896]{3,2,1,0:T(8,128)}, f32[4,2,32,896]{3,2,1,0:T(8,128)S(1)}, u32[]{:S(2)}, u32[]{:S(2)}) collective-permute-start(f32[4,2,32,896]{3,2,1,0:T(8,128)} %pack2.1), channel_id=1, source_target_pairs={{0,64},{1,17},{2,66},{3,19},{4,68},{5,21},{6,70},{7,23},{8,72},{9,... | collective-permute-start | bytes 2752520 | tf_op jit(solution)/shard_map/ppermute | solution.py:48
  7.4 20.6 %collective-permute-start.1 = (f32[4,2,32,896]{3,2,1,0:T(8,128)}, f32[4,2,32,896]{3,2,1,0:T(8,128)S(1)}, u32[]{:S(2)}, u32[]{:S(2)}) collective-permute-start(f32[4,2,32,896]{3,2,1,0:T(8,128)} %pack1.1), channel_id=1, source_target_pairs={{0,32},{1,9},{2,34},{3,11},{4,36},{5,13},{6,38},{7,15},{8,40},{9,1... | collective-permute-start | bytes 2752520 | tf_op jit(solution)/shard_map/ppermute | solution.py:48
  11.4 16.7 %collective-permute-start.2 = (f32[4,2,32,896]{3,2,1,0:T(8,128)}, f32[4,2,32,896]{3,2,1,0:T(8,128)}, u32[]{:S(2)}, u32[]{:S(2)}) collective-permute-start(f32[4,2,32,896]{3,2,1,0:T(8,128)} %pack3.1), channel_id=1, source_target_pairs={{0,96},{1,25},{2,98},{3,27},{4,100},{5,29},{6,102},{7,31},{8,104},... | collective-permute-start | bytes 2752520 | tf_op jit(solution)/shard_map/ppermute | solution.py:48
  14.1 14.0 %copy-start.1 = (f32[4,2,32,896]{3,2,1,0:T(8,128)S(1)}, f32[4,2,32,896]{3,2,1,0:T(8,128)}, u32[]{:S(2)}) copy-start(f32[4,2,32,896]{3,2,1,0:T(8,128)} %pack0.3) | copy-start | bytes 2752516
  16.5 70.8 %copy-start.4 = (f32[32,896]{1,0:T(8,128)S(1)}, f32[32,896]{1,0:T(8,128)}, u32[]{:S(2)}) copy-start(f32[32,896]{1,0:T(8,128)} %param.5) | copy-start | bytes 344068
  29.7 7.6 %collective-permute-start.3 = (f32[2,32,896]{2,1,0:T(8,128)S(1)}, f32[2,32,896]{2,1,0:T(8,128)S(1)}, u32[]{:S(2)}, u32[]{:S(2)}) collective-permute-start(f32[2,32,896]{2,1,0:T(8,128)S(1)} %get-tuple-element.4), channel_id=1, source_target_pairs={{0,16},{1,65},{2,18},{3,67},{4,20},{5,69},{6,22},{7,71},{8,24},{9,... | collective-permute-start | bytes 688136 | tf_op jit(solution)/shard_map/ppermute | solution.py:48
  33.0 7.2 %collective-permute-start.4 = (f32[2,32,896]{2,1,0:T(8,128)S(1)}, f32[2,32,896]{2,1,0:T(8,128)S(1)}, u32[]{:S(2)}, u32[]{:S(2)}) collective-permute-start(f32[2,32,896]{2,1,0:T(8,128)S(1)} %get-tuple-element.6), channel_id=1, source_target_pairs={{0,8},{1,33},{2,10},{3,35},{4,12},{5,37},{6,14},{7,39},{8,16},{9,4... | collective-permute-start | bytes 688136 | tf_op jit(solution)/shard_map/ppermute | solution.py:48
  33.7 6.6 %collective-permute-start.5 = (f32[2,32,896]{2,1,0:T(8,128)S(1)}, f32[2,32,896]{2,1,0:T(8,128)S(1)}, u32[]{:S(2)}, u32[]{:S(2)}) collective-permute-start(f32[2,32,896]{2,1,0:T(8,128)S(1)} %get-tuple-element.5), channel_id=1, source_target_pairs={{0,24},{1,97},{2,26},{3,99},{4,28},{5,101},{6,30},{7,103},{8,0},{9... | collective-permute-start | bytes 688136 | tf_op jit(solution)/shard_map/ppermute | solution.py:48
  41.4 10.4 %collective-permute-start.6 = (f32[32,896]{1,0:T(8,128)S(1)}, f32[32,896]{1,0:T(8,128)S(1)}, u32[]{:S(2)}, u32[]{:S(2)}) collective-permute-start(f32[32,896]{1,0:T(8,128)S(1)} %slice_bitcast_fusion), channel_id=1, source_target_pairs={{0,128},{1,129},{2,130},{3,131},{4,132},{5,133},{6,134},{7,135},{8... | collective-permute-start | bytes 344072 | tf_op jit(solution)/shard_map/ppermute | solution.py:48
  53.1 1.3 collective-permute-start.7
  55.0 5.4 %collective-permute-start.10 = (f32[8,128]{1,0:T(8,128)S(1)}, f32[8,128]{1,0:T(8,128)S(1)}, u32[]{:S(2)}, u32[]{:S(2)}) collective-permute-start(f32[8,128]{1,0:T(8,128)S(1)} %broadcast_add_fusion), channel_id=1, source_target_pairs={{0,96},{1,25},{2,98},{3,27},{4,100},{5,29},{6,102},{7,31},{8,104},... | collective-permute-start | bytes 12296 | tf_op jit(solution)/shard_map/ppermute | solution.py:48
  55.7 4.7 %collective-permute-start.8 = (f32[8,128]{1,0:T(8,128)S(1)}, f32[8,128]{1,0:T(8,128)S(1)}, u32[]{:S(2)}, u32[]{:S(2)}) collective-permute-start(f32[8,128]{1,0:T(8,128)S(1)} %broadcast_add_fusion), channel_id=1, source_target_pairs={{0,32},{1,9},{2,34},{3,11},{4,36},{5,13},{6,38},{7,15},{8,40},{9,1... | collective-permute-start | bytes 12296 | tf_op jit(solution)/shard_map/ppermute | solution.py:48
  57.2 5.1 %collective-permute-start.9 = (f32[8,128]{1,0:T(8,128)S(1)}, f32[8,128]{1,0:T(8,128)S(1)}, u32[]{:S(2)}, u32[]{:S(2)}) collective-permute-start(f32[8,128]{1,0:T(8,128)S(1)} %broadcast_add_fusion), channel_id=1, source_target_pairs={{0,64},{1,17},{2,66},{3,19},{4,68},{5,21},{6,70},{7,23},{8,72},{9,... | collective-permute-start | bytes 12296 | tf_op jit(solution)/shard_map/ppermute | solution.py:48
  63.0 5.4 %collective-permute-start.11 = (f32[8,128]{1,0:T(8,128)S(1)}, f32[8,128]{1,0:T(8,128)S(1)}, u32[]{:S(2)}, u32[]{:S(2)}) collective-permute-start(f32[8,128]{1,0:T(8,128)S(1)} %add_add_fusion.2), channel_id=1, source_target_pairs={{0,8},{1,33},{2,10},{3,35},{4,12},{5,37},{6,14},{7,39},{8,16},{9,4... | collective-permute-start | bytes 12296 | tf_op jit(solution)/shard_map/ppermute | solution.py:48
  64.3 5.6 %collective-permute-start.12 = (f32[8,128]{1,0:T(8,128)S(1)}, f32[8,128]{1,0:T(8,128)S(1)}, u32[]{:S(2)}, u32[]{:S(2)}) collective-permute-start(f32[8,128]{1,0:T(8,128)S(1)} %add_add_fusion.2), channel_id=1, source_target_pairs={{0,16},{1,65},{2,18},{3,67},{4,20},{5,69},{6,22},{7,71},{8,24},{9,... | collective-permute-start | bytes 12296 | tf_op jit(solution)/shard_map/ppermute | solution.py:48
  68.3 3.6 %collective-permute-start.13 = (f32[8,128]{1,0:T(8,128)S(1)}, f32[8,128]{1,0:T(8,128)S(1)}, u32[]{:S(2)}, u32[]{:S(2)}) collective-permute-start(f32[8,128]{1,0:T(8,128)S(1)} %add_add_fusion.2), channel_id=1, source_target_pairs={{0,24},{1,97},{2,26},{3,99},{4,28},{5,101},{6,30},{7,103},{8,0},{9... | collective-permute-start | bytes 12296 | tf_op jit(solution)/shard_map/ppermute | solution.py:48
  71.9 5.4 %collective-permute-start.14 = (f32[8,128]{1,0:T(8,128)S(1)}, f32[8,128]{1,0:T(8,128)S(1)}, u32[]{:S(2)}, u32[]{:S(2)}) collective-permute-start(f32[8,128]{1,0:T(8,128)S(1)} %add_add_fusion.1), channel_id=1, source_target_pairs={{0,2},{1,3},{2,4},{3,5},{4,6},{5,7},{6,0},{7,1},{8,10},{9,11},{10,... | collective-permute-start | bytes 12296 | tf_op jit(solution)/shard_map/ppermute | solution.py:48
  72.7 4.6 %collective-permute-start.15 = (f32[8,128]{1,0:T(8,128)S(1)}, f32[8,128]{1,0:T(8,128)S(1)}, u32[]{:S(2)}, u32[]{:S(2)}) collective-permute-start(f32[8,128]{1,0:T(8,128)S(1)} %add_add_fusion.1), channel_id=1, source_target_pairs={{0,4},{1,5},{2,6},{3,7},{4,0},{5,1},{6,2},{7,3},{8,12},{9,13},{10,... | collective-permute-start | bytes 12296 | tf_op jit(solution)/shard_map/ppermute | solution.py:48
  74.9 3.6 %collective-permute-start.16 = (f32[8,128]{1,0:T(8,128)S(1)}, f32[8,128]{1,0:T(8,128)S(1)}, u32[]{:S(2)}, u32[]{:S(2)}) collective-permute-start(f32[8,128]{1,0:T(8,128)S(1)} %add_add_fusion.1), channel_id=1, source_target_pairs={{0,6},{1,7},{2,0},{3,1},{4,2},{5,3},{6,4},{7,5},{8,14},{9,15},{10,... | collective-permute-start | bytes 12296 | tf_op jit(solution)/shard_map/ppermute | solution.py:48
  78.5 7.5 %collective-permute-start.17 = (f32[8,128]{1,0:T(8,128)S(1)}, f32[8,128]{1,0:T(8,128)S(1)}, u32[]{:S(2)}, u32[]{:S(2)}) collective-permute-start(f32[8,128]{1,0:T(8,128)S(1)} %add_add_fusion), channel_id=1, source_target_pairs={{0,128},{1,129},{2,130},{3,131},{4,132},{5,133},{6,134},{7,135},{8... | collective-permute-start | bytes 12296 | tf_op jit(solution)/shard_map/ppermute | solution.py:48
  88.9 8.8 %collective-permute-start.18 = (f32[32,896]{1,0:T(8,128)S(1)}, f32[32,896]{1,0:T(8,128)S(1)}, u32[]{:S(2)}, u32[]{:S(2)}) collective-permute-start(f32[32,896]{1,0:T(8,128)S(1)} %get-tuple-element.2), channel_id=1, source_target_pairs={{0,128},{1,129},{2,130},{3,131},{4,132},{5,133},{6,134},{7,135},{8... | collective-permute-start | bytes 344072 | tf_op jit(solution)/shard_map/ppermute | solution.py:48
  97.7 19.1 %collective-permute-start.19 = (f32[2,32,896]{2,1,0:T(8,128)S(1)}, f32[2,32,896]{2,1,0:T(8,128)S(1)}, u32[]{:S(2)}, u32[]{:S(2)}) collective-permute-start(f32[2,32,896]{2,1,0:T(8,128)S(1)} %get-tuple-element.8), channel_id=1, source_target_pairs={{0,24},{1,97},{2,26},{3,99},{4,28},{5,101},{6,30},{7,103},{8,0},{9... | collective-permute-start | bytes 688136 | tf_op jit(solution)/shard_map/ppermute | solution.py:48
  100.2 16.6 %collective-permute-start.20 = (f32[2,32,896]{2,1,0:T(8,128)S(1)}, f32[2,32,896]{2,1,0:T(8,128)S(1)}, u32[]{:S(2)}, u32[]{:S(2)}) collective-permute-start(f32[2,32,896]{2,1,0:T(8,128)S(1)} %get-tuple-element.8), channel_id=1, source_target_pairs={{0,16},{1,65},{2,18},{3,67},{4,20},{5,69},{6,22},{7,71},{8,24},{9,... | collective-permute-start | bytes 688136 | tf_op jit(solution)/shard_map/ppermute | solution.py:48
  100.2 21.2 %collective-permute-start.21 = (f32[2,32,896]{2,1,0:T(8,128)S(1)}, f32[2,32,896]{2,1,0:T(8,128)S(1)}, u32[]{:S(2)}, u32[]{:S(2)}) collective-permute-start(f32[2,32,896]{2,1,0:T(8,128)S(1)} %get-tuple-element.8), channel_id=1, source_target_pairs={{0,8},{1,33},{2,10},{3,35},{4,12},{5,37},{6,14},{7,39},{8,16},{9,4... | collective-permute-start | bytes 688136 | tf_op jit(solution)/shard_map/ppermute | solution.py:48
  121.5 4.9 %copy-start = (f32[4,2,32,896]{3,2,1,0:T(8,128)}, f32[4,2,32,896]{3,2,1,0:T(8,128)S(1)}, u32[]{:S(2)}) copy-start(f32[4,2,32,896]{3,2,1,0:T(8,128)S(1)} %pad_maximum_fusion.piece) | copy-start | bytes 2752516
  121.5 15.2 %collective-permute-start.24 = (f32[4,2,32,896]{3,2,1,0:T(8,128)S(1)}, f32[4,2,32,896]{3,2,1,0:T(8,128)}, u32[]{:S(2)}, u32[]{:S(2)}) collective-permute-start(f32[4,2,32,896]{3,2,1,0:T(8,128)S(1)} %pad_maximum_fusion.piece), channel_id=1, source_target_pairs={{0,64},{1,17},{2,66},{3,19},{4,68},{5,21},{6,70},{7,23},{8,72},{9,... | collective-permute-start | bytes 2752520 | tf_op jit(solution)/shard_map/ppermute | solution.py:48
  124.3 22.0 %collective-permute-start.23 = (f32[4,2,32,896]{3,2,1,0:T(8,128)S(1)}, f32[4,2,32,896]{3,2,1,0:T(8,128)S(1)}, u32[]{:S(2)}, u32[]{:S(2)}) collective-permute-start(f32[4,2,32,896]{3,2,1,0:T(8,128)S(1)} %pad_maximum_fusion.piece), channel_id=1, source_target_pairs={{0,32},{1,9},{2,34},{3,11},{4,36},{5,13},{6,38},{7,15},{8,40},{9,1... | collective-permute-start | bytes 2752520 | tf_op jit(solution)/shard_map/ppermute | solution.py:48
  125.2 24.3 %collective-permute-start.22 = (f32[4,2,32,896]{3,2,1,0:T(8,128)S(1)}, f32[4,2,32,896]{3,2,1,0:T(8,128)S(1)}, u32[]{:S(2)}, u32[]{:S(2)}) collective-permute-start(f32[4,2,32,896]{3,2,1,0:T(8,128)S(1)} %pad_maximum_fusion.piece), channel_id=1, source_target_pairs={{0,96},{1,25},{2,98},{3,27},{4,100},{5,29},{6,102},{7,31},{8,104},... | collective-permute-start | bytes 2752520 | tf_op jit(solution)/shard_map/ppermute | solution.py:48
  146.4 1.0 copy-start.3
  149.5 1.0 copy-start.2

commit v3 on v2

v3 whole, which is shorter than its diff:
```python
import functools

import jax
import jax.numpy as jnp
from jax import lax
from jax.experimental import pallas as pl
from jax.experimental.pallas import tpu as pltpu
from jax.sharding import PartitionSpec as P

clip_level = 0.1
outer_rate = 0.7
moment_decay = 0.9

AXES = ("island", "fsdp")
HALVES, SIDE, RUN, CORES = 2, 4, 4, 2
BLOCKS = 2 * HALVES
ROOM = 16 * 2**20


def pairs(move):
    out = []
    for zh in range(HALVES):
        for x in range(SIDE):
            for y in range(SIDE):
                for zl in range(RUN):
                    for core in range(CORES):
                        there = move(zh, x, y, zl, core)
                        place = lambda h, i, j, k, c: ((h * SIDE + i) * SIDE + j) * RUN * CORES + k * CORES + c
                        out.append((place(zh, x, y, zl, core), place(*there)))
    return out


def along(first, step):
    def move(zh, x, y, zl, core):
        if (core == 0) == first:
            return zh, (x + step) % SIDE, y, zl, core
        return zh, x, (y + step) % SIDE, zl, core

    return pairs(move)


FIRST = {step: along(True, step) for step in (1, 2, 3)}
SECOND = {step: along(False, step) for step in (1, 2, 3)}
ACROSS = pairs(lambda zh, x, y, zl, core: (1 - zh, x, y, zl, core))
UP = {step: pairs(lambda zh, x, y, zl, core, s=step: (zh, x, y, (zl + s) % RUN, core)) for step in (1, 2, 3)}
TWIN = pairs(lambda zh, x, y, zl, core: (zh, x, y, zl, 1 - core))


def send(value, route):
    return lax.ppermute(value, AXES, route)


def place_of(width, step, near, half):
    island = lax.axis_index("island")
    core = lax.rem(lax.axis_index("fsdp"), CORES)
    zh = island // (SIDE * SIDE)
    x = lax.rem(island // SIDE, SIDE)
    y = lax.rem(island, SIDE)
    one = jnp.where(core == 0, x, y)
    two = jnp.where(core == 0, y, x)
    one = lax.rem(one + step, SIDE)
    two = lax.rem(two + near, SIDE)
    zh = lax.rem(zh + half, HALVES)
    block = zh * SIDE * SIDE + jnp.where(core == 0, one * SIDE + two, two * SIDE + one)
    return pl.multiple_of(block * width, 128)


def blocks_of(groups):
    return [(step, 2 * group + k, half) for step, group in groups for k in range(2) for half in range(HALVES)]


def pack_kernel(jobs, width, *refs):
    sems = refs[-1]
    inputs = len(refs) - 1 - len(jobs)
    copies = []
    for n, (source, step) in enumerate(jobs):
        for near in range(SIDE):
            for half in range(HALVES):
                copy = pltpu.make_async_copy(
                    refs[source].at[:, pl.ds(place_of(width, step, near, half), width)],
                    refs[inputs + n].at[near, half],
                    sems.at[len(copies)],
                )
                copy.start()
                copies.append(copy)
    for copy in copies:
        copy.wait()


def pack(sources, jobs, width, behind=()):
    rows = sources[0].shape[0]
    amount = len(jobs) * SIDE * HALVES
    return pl.pallas_call(
        functools.partial(pack_kernel, jobs, width),
        out_shape=[jax.ShapeDtypeStruct((SIDE, HALVES, rows, width), sources[0].dtype)] * len(jobs),
        in_specs=[pl.BlockSpec(memory_space=pltpu.HBM)] * len(sources)
        + [pl.BlockSpec(memory_space=pl.ANY)] * len(behind),
        out_specs=[pl.BlockSpec(memory_space=pltpu.VMEM)] * len(jobs),
        scratch_shapes=[pltpu.SemaphoreType.DMA((amount,))],
        cost_estimate=pl.CostEstimate(flops=0, bytes_accessed=8 * amount * rows * width, transcendentals=0),
        compiler_params=pltpu.CompilerParams(vmem_limit_bytes=ROOM),
        name=f"pack{len(jobs)}",
    )(*sources, *behind)


def unpack_kernel(groups, width, *refs):
    pieces, (whole, sems) = refs[: len(groups)], refs[-2:]
    copies = []
    for n, block in enumerate(blocks_of(groups)):
        group, k, half = n // BLOCKS, (n % BLOCKS) // HALVES, n % HALVES
        copy = pltpu.make_async_copy(
            pieces[group].at[k, half], whole.at[:, pl.ds(place_of(width, *block), width)], sems.at[n]
        )
        copy.start()
        copies.append(copy)
    for copy in copies:
        copy.wait()


def unpack(groups, pieces, whole, shape):
    rows, width = pieces[0].shape[-2:]
    given = [] if whole is None else [whole]
    vmem, hbm = pl.BlockSpec(memory_space=pltpu.VMEM), pl.BlockSpec(memory_space=pltpu.HBM)
    amount = len(groups) * BLOCKS
    return pl.pallas_call(
        functools.partial(unpack_kernel, groups, width),
        out_shape=jax.ShapeDtypeStruct(shape, pieces[0].dtype),
        in_specs=[vmem] * len(groups) + [hbm] * len(given),
        out_specs=hbm,
        scratch_shapes=[pltpu.SemaphoreType.DMA((amount,))],
        input_output_aliases={len(groups): 0} if given else {},
        cost_estimate=pl.CostEstimate(flops=0, bytes_accessed=8 * amount * rows * width, transcendentals=0),
        compiler_params=pltpu.CompilerParams(vmem_limit_bytes=ROOM),
        name=f"unpack{len(groups)}",
    )(*pieces, *given)


def spread_near(value):
    near = [value] + [None] * (SIDE - 1)
    for step in (2, 1, 3):
        near[SIDE - step] = send(value, SECOND[step])
    return near


def after(value, *others):
    return lax.optimization_barrier((value,) + others)[0]


def per_device(global_weights, local_weights, momentum):
    islands = lax.axis_size("island")
    shards = lax.axis_size("fsdp")
    rows, columns = global_weights.shape
    width = columns // islands
    local = local_weights[0]

    (far,) = pack((local,), ((0, 2),), width)
    right, left = pack((local,), ((0, 1), (0, 3)), width, (far,))
    far = send(far, FIRST[2])
    packed = left
    right, left = send(right, FIRST[1]), send(left, FIRST[3])
    base, mine = pack((global_weights, local), ((0, 0), (1, 0)), width, (packed,))
    speed = after(momentum, base)
    speed = jnp.stack([speed, send(speed, ACROSS)])
    left = after(left, speed)
    parts = []
    for near in range(SIDE):
        total = base[near] - mine[near]
        for piece in (far, right, left):
            total = total + (base[near] - piece[near])
        parts.append(total)
    got = [send(parts[step], SECOND[step]) for step in (2, 1, 3)]
    pair = parts[0] + got[0] + got[1] + got[2]

    other = send(pair, ACROSS)
    summed = pair + jnp.stack([other[1], other[0]])
    speeds = spread_near(after(speed, pair))
    summed = after(summed, *speeds)
    average = summed / islands
    nears = spread_near(average)

    count = rows * columns * shards
    squares = jnp.broadcast_to(jnp.sum(average * average).reshape(1, 1), (8, 128))
    squares = squares + send(squares, TWIN)
    for route in (UP, SECOND, FIRST):
        squares = squares + send(squares, route[1]) + send(squares, route[2]) + send(squares, route[3])
    spread = jnp.sqrt(squares[0, 0] / count + 1e-06)
    factor = jnp.minimum(1.0, clip_level / spread)

    def update(base, average, speed):
        clipped = factor * average
        return base - outer_rate * (clipped + moment_decay * (moment_decay * speed + clipped))

    new_momentum = moment_decay * momentum + factor * average[0]
    early = jnp.stack([update(base[k], nears[k], speeds[k]) for k in range(2)])
    late = jnp.stack([update(base[2 + k], nears[2 + k], speeds[2 + k]) for k in range(2)])

    left_early, right_late = send(early, FIRST[1]), send(late, FIRST[3])
    left_late, right_early = send(late, FIRST[1]), send(early, FIRST[3])
    far_early, far_late = send(left_early, FIRST[1]), send(right_late, FIRST[3])
    groups = ((0, 0), (0, 1), (3, 0), (1, 1), (3, 1), (1, 0), (2, 0), (2, 1))
    pieces = (early, late, left_early, right_late, left_late, right_early, far_early, far_late)
    new_global = None
    for n in range(0, len(groups), 2):
        new_global = unpack(groups[n : n + 2], pieces[n : n + 2], new_global, (rows, columns))
    return (new_global, new_momentum)


def solution(mesh):
    placed = (P("fsdp", None), P("island", "fsdp", None), P("fsdp", "island"))
    return jax.shard_map(
        per_device,
        mesh=mesh,
        in_specs=placed,
        out_specs=(P("fsdp", None), P("fsdp", "island")),
        check_vma=False,
    )
```

time: 153 us -> 115 us (0.75)
  the two profiles are of different devices: /device:TPU:2 before, /device:TPU:32 now
where the time goes in v3:
time: 115 us; the launch traced here: 114 us
  starting transfers between devices  53.2 us (46%)
  waiting for transfers between devices  47 us (41%)
  Pallas kernels  5.99 us (5%)
  other arithmetic  3.3 us (3%)
  local copies, waits for them, and re-layouts  3.22 us (3%)
  between operations  1.68 us (1%)
    ppermute x30, starting transfers between devices, send(): return lax.ppermute(value, AXES, route)  53.2 us
    ppermute x30, waiting for transfers between devices, send(): return lax.ppermute(value, AXES, route)  47 us
    pallas_call x4, Pallas kernels, unpack(): pl.pallas_call(functools.partial(unpack_kernel, groups, width), out_shape...  3.95 us
  transfers between devices with their start and end apart: 30, of which 23 were waited for; matrix products, arithmetic and copies ran while one was open for 1% of the time, Pallas kernels for 3%

profile of v3, /device:TPU:32, one launch (start us, length us, event | category | flops | bytes accessed | tf_op | source)
XLA Modules:
  0.0 114.4 jit_solution(17364754927896609420)
XLA Ops:
  0.6 2.0 %copy-done = f32[1,32,28672]{2,1,0:T(8,128)S(1)} copy-done((f32[1,32,28672]{2,1,0:T(8,128)S(1)}, f32[1,32,28672]{2,1,0:T(8,128)}, u32[]{:S(2)}) %copy-start) | copy-done | bytes 3670040
  2.7 0.4 pack1.1.refs_1_
  3.1 0.9 pack2.2
  3.9 2.8 %collective-permute-start.2 = (f32[4,2,32,896]{3,2,1,0:T(8,128)S(1)}, f32[4,2,32,896]{3,2,1,0:T(8,128)S(1)}, u32[]{:S(2)}, u32[]{:S(2)}) collective-permute-start(f32[4,2,32,896]{3,2,1,0:T(8,128)S(1)} %get-tuple-element.10.refs_2_), channel_id=1, source_target_pairs={{0,96},{1,25},{2,98},{3,27},{4,100},{5,29},{6,102},{7,31},{8,104},... | collective-permute-start | bytes 2752520 | tf_op jit(solution)/shard_map/ppermute | solution.py:50
  6.8 2.3 %collective-permute-start = (f32[4,2,32,896]{3,2,1,0:T(8,128)S(1)}, f32[4,2,32,896]{3,2,1,0:T(8,128)S(1)}, u32[]{:S(2)}, u32[]{:S(2)}) collective-permute-start(f32[4,2,32,896]{3,2,1,0:T(8,128)S(1)} %pack1.1.refs_1_), channel_id=1, source_target_pairs={{0,64},{1,17},{2,66},{3,19},{4,68},{5,21},{6,70},{7,23},{8,72},{9,... | collective-permute-start | bytes 2752520 | tf_op jit(solution)/shard_map/ppermute | solution.py:50
  9.1 0.8 pack2.3
  9.9 6.4 %collective-permute-start.3 = (f32[32,896]{1,0:T(8,128)S(1)}, f32[32,896]{1,0:T(8,128)S(1)}, u32[]{:S(2)}, u32[]{:S(2)}) collective-permute-start(f32[32,896]{1,0:T(8,128)S(1)} %copy-done.2), channel_id=1, source_target_pairs={{0,128},{1,129},{2,130},{3,131},{4,132},{5,133},{6,134},{7,135},{8... | collective-permute-start | bytes 344072 | tf_op jit(solution)/shard_map/ppermute | solution.py:50
  16.3 5.2 %collective-permute-done.3 = f32[32,896]{1,0:T(8,128)S(1)} collective-permute-done((f32[32,896]{1,0:T(8,128)S(1)}, f32[32,896]{1,0:T(8,128)S(1)}, u32[]{:S(2)}, u32[]{:S(2)}) %collective-permute-start.3) | collective-permute-done | bytes 114720 | tf_op jit(solution)/shard_map/ppermute | solution.py:50
  21.5 6.0 %collective-permute-done.2 = f32[4,2,32,896]{3,2,1,0:T(8,128)S(1)} collective-permute-done((f32[4,2,32,896]{3,2,1,0:T(8,128)S(1)}, f32[4,2,32,896]{3,2,1,0:T(8,128)S(1)}, u32[]{:S(2)}, u32[]{:S(2)}) %collective-permute-start.2) | collective-permute-done | bytes 917536 | tf_op jit(solution)/shard_map/ppermute | solution.py:50
  27.6 3.7 %collective-permute-done.1 = f32[4,2,32,896]{3,2,1,0:T(8,128)S(1)} collective-permute-done((f32[4,2,32,896]{3,2,1,0:T(8,128)S(1)}, f32[4,2,32,896]{3,2,1,0:T(8,128)S(1)}, u32[]{:S(2)}, u32[]{:S(2)}) %collective-permute-start.1) | collective-permute-done | bytes 917536 | tf_op jit(solution)/shard_map/ppermute | solution.py:50
  31.2 0.2 fusion.12
  31.5 3.3 %collective-permute-start.4 = (f32[2,32,896]{2,1,0:T(8,128)S(1)}, f32[2,32,896]{2,1,0:T(8,128)S(1)}, u32[]{:S(2)}, u32[]{:S(2)}) collective-permute-start(f32[2,32,896]{2,1,0:T(8,128)S(1)} %get-tuple-element.18), channel_id=1, source_target_pairs={{0,16},{1,65},{2,18},{3,67},{4,20},{5,69},{6,22},{7,71},{8,24},{9,... | collective-permute-start | bytes 688136 | tf_op jit(solution)/shard_map/ppermute | solution.py:50
  34.7 0.7 collective-permute-start.5
  35.4 2.6 %collective-permute-start.6 = (f32[2,32,896]{2,1,0:T(8,128)S(1)}, f32[2,32,896]{2,1,0:T(8,128)S(1)}, u32[]{:S(2)}, u32[]{:S(2)}) collective-permute-start(f32[2,32,896]{2,1,0:T(8,128)S(1)} %get-tuple-element.19), channel_id=1, source_target_pairs={{0,24},{1,97},{2,26},{3,99},{4,28},{5,101},{6,30},{7,103},{8,0},{9... | collective-permute-start | bytes 688136 | tf_op jit(solution)/shard_map/ppermute | solution.py:50
  38.0 1.1 collective-permute-done.4
  39.1 2.9 %collective-permute-done.5 = f32[2,32,896]{2,1,0:T(8,128)S(1)} collective-permute-done((f32[2,32,896]{2,1,0:T(8,128)S(1)}, f32[2,32,896]{2,1,0:T(8,128)S(1)}, u32[]{:S(2)}, u32[]{:S(2)}) %collective-permute-start.5) | collective-permute-done | bytes 229408 | tf_op jit(solution)/shard_map/ppermute | solution.py:50
  42.1 6.4 %collective-permute-start.7 = (f32[2,32,896]{2,1,0:T(8,128)S(1)}, f32[2,32,896]{2,1,0:T(8,128)S(1)}, u32[]{:S(2)}, u32[]{:S(2)}) collective-permute-start(f32[2,32,896]{2,1,0:T(8,128)S(1)} %fusion.20), channel_id=1, source_target_pairs={{0,128},{1,129},{2,130},{3,131},{4,132},{5,133},{6,134},{7,135},{8... | collective-permute-start | bytes 688136 | tf_op jit(solution)/shard_map/ppermute | solution.py:50
  48.5 1.3 %collective-permute-start.10 = (f32[2,32,896]{2,1,0:T(8,128)S(1)}, f32[2,32,896]{2,1,0:T(8,128)S(1)}, u32[]{:S(2)}, u32[]{:S(2)}) collective-permute-start(f32[2,32,896]{2,1,0:T(8,128)S(1)} %pad_maximum_fusion.2), channel_id=1, source_target_pairs={{0,8},{1,33},{2,10},{3,35},{4,12},{5,37},{6,14},{7,39},{8,16},{9,4... | collective-permute-start | bytes 688136 | tf_op jit(solution)/shard_map/ppermute | solution.py:50
  49.7 1.9 %collective-permute-start.8 = (f32[2,32,896]{2,1,0:T(8,128)S(1)}, f32[2,32,896]{2,1,0:T(8,128)S(1)}, u32[]{:S(2)}, u32[]{:S(2)}) collective-permute-start(f32[2,32,896]{2,1,0:T(8,128)S(1)} %pad_maximum_fusion.2), channel_id=1, source_target_pairs={{0,24},{1,97},{2,26},{3,99},{4,28},{5,101},{6,30},{7,103},{8,0},{9... | collective-permute-start | bytes 688136 | tf_op jit(solution)/shard_map/ppermute | solution.py:50
  51.7 1.5 %collective-permute-start.9 = (f32[2,32,896]{2,1,0:T(8,128)S(1)}, f32[2,32,896]{2,1,0:T(8,128)S(1)}, u32[]{:S(2)}, u32[]{:S(2)}) collective-permute-start(f32[2,32,896]{2,1,0:T(8,128)S(1)} %pad_maximum_fusion.2), channel_id=1, source_target_pairs={{0,16},{1,65},{2,18},{3,67},{4,20},{5,69},{6,22},{7,71},{8,24},{9,... | collective-permute-start | bytes 688136 | tf_op jit(solution)/shard_map/ppermute | solution.py:50
  53.2 3.7 %collective-permute-done.7 = f32[2,32,896]{2,1,0:T(8,128)S(1)} collective-permute-done((f32[2,32,896]{2,1,0:T(8,128)S(1)}, f32[2,32,896]{2,1,0:T(8,128)S(1)}, u32[]{:S(2)}, u32[]{:S(2)}) %collective-permute-start.7) | collective-permute-done | bytes 229408 | tf_op jit(solution)/shard_map/ppermute | solution.py:50
  56.9 2.7 %collective-permute-done.9 = f32[2,32,896]{2,1,0:T(8,128)S(1)} collective-permute-done((f32[2,32,896]{2,1,0:T(8,128)S(1)}, f32[2,32,896]{2,1,0:T(8,128)S(1)}, u32[]{:S(2)}, u32[]{:S(2)}) %collective-permute-start.9) | collective-permute-done | bytes 229408 | tf_op jit(solution)/shard_map/ppermute | solution.py:50
  59.6 0.7 multiply_reduce_fusion
  60.3 0.6 broadcast_in_dim.2
  60.9 0.1 collective-permute-start.11
  61.0 1.2 %collective-permute-done.11 = f32[8,128]{1,0:T(8,128)S(1)} collective-permute-done((f32[8,128]{1,0:T(8,128)S(1)}, f32[8,128]{1,0:T(8,128)S(1)}, u32[]{:S(2)}, u32[]{:S(2)}) %collective-permute-start.11) | collective-permute-done | bytes 4128 | tf_op jit(solution)/shard_map/ppermute | solution.py:50
  62.2 0.6 broadcast_add_fusion
  62.8 1.1 collective-permute-start.12
  63.9 2.4 %collective-permute-start.13 = (f32[8,128]{1,0:T(8,128)S(1)}, f32[8,128]{1,0:T(8,128)S(1)}, u32[]{:S(2)}, u32[]{:S(2)}) collective-permute-start(f32[8,128]{1,0:T(8,128)S(1)} %broadcast_add_fusion), channel_id=1, source_target_pairs={{0,4},{1,5},{2,6},{3,7},{4,0},{5,1},{6,2},{7,3},{8,12},{9,13},{10,... | collective-permute-start | bytes 12296 | tf_op jit(solution)/shard_map/ppermute | solution.py:50
  66.3 0.1 collective-permute-start.14
  66.4 0.1 collective-permute-done.12
  66.5 1.9 %collective-permute-done.13 = f32[8,128]{1,0:T(8,128)S(1)} collective-permute-done((f32[8,128]{1,0:T(8,128)S(1)}, f32[8,128]{1,0:T(8,128)S(1)}, u32[]{:S(2)}, u32[]{:S(2)}) %collective-permute-start.13) | collective-permute-done | bytes 4128 | tf_op jit(solution)/shard_map/ppermute | solution.py:50
  68.4 1.5 %collective-permute-done.14 = f32[8,128]{1,0:T(8,128)S(1)} collective-permute-done((f32[8,128]{1,0:T(8,128)S(1)}, f32[8,128]{1,0:T(8,128)S(1)}, u32[]{:S(2)}, u32[]{:S(2)}) %collective-permute-start.14) | collective-permute-done | bytes 4128 | tf_op jit(solution)/shard_map/ppermute | solution.py:50
  69.9 0.7 add_add_fusion.2
  70.5 1.5 %collective-permute-start.15 = (f32[8,128]{1,0:T(8,128)S(1)}, f32[8,128]{1,0:T(8,128)S(1)}, u32[]{:S(2)}, u32[]{:S(2)}) collective-permute-start(f32[8,128]{1,0:T(8,128)S(1)} %add_add_fusion.2), channel_id=1, source_target_pairs={{0,8},{1,33},{2,10},{3,35},{4,12},{5,37},{6,14},{7,39},{8,16},{9,4... | collective-permute-start | bytes 12296 | tf_op jit(solution)/shard_map/ppermute | solution.py:50
  72.0 1.8 %collective-permute-start.16 = (f32[8,128]{1,0:T(8,128)S(1)}, f32[8,128]{1,0:T(8,128)S(1)}, u32[]{:S(2)}, u32[]{:S(2)}) collective-permute-start(f32[8,128]{1,0:T(8,128)S(1)} %add_add_fusion.2), channel_id=1, source_target_pairs={{0,16},{1,65},{2,18},{3,67},{4,20},{5,69},{6,22},{7,71},{8,24},{9,... | collective-permute-start | bytes 12296 | tf_op jit(solution)/shard_map/ppermute | solution.py:50
  73.9 1.1 collective-permute-start.17
  75.0 0.4 collective-permute-done.15
  75.4 1.7 %collective-permute-done.16 = f32[8,128]{1,0:T(8,128)S(1)} collective-permute-done((f32[8,128]{1,0:T(8,128)S(1)}, f32[8,128]{1,0:T(8,128)S(1)}, u32[]{:S(2)}, u32[]{:S(2)}) %collective-permute-start.16) | collective-permute-done | bytes 4128 | tf_op jit(solution)/shard_map/ppermute | solution.py:50
  77.1 0.3 collective-permute-done.17
  77.5 2.4 %collective-permute-start.21 = (f32[2,32,896]{2,1,0:T(8,128)S(1)}, f32[2,32,896]{2,1,0:T(8,128)S(1)}, u32[]{:S(2)}, u32[]{:S(2)}) collective-permute-start(f32[2,32,896]{2,1,0:T(8,128)S(1)} %get-tuple-element.26), channel_id=1, source_target_pairs={{0,24},{1,97},{2,26},{3,99},{4,28},{5,101},{6,30},{7,103},{8,0},{9... | collective-permute-start | bytes 688136 | tf_op jit(solution)/shard_map/ppermute | solution.py:50
  79.9 0.6 collective-permute-start.24
  80.5 1.4 %collective-permute-start.19 = (f32[8,128]{1,0:T(8,128)S(1)}, f32[8,128]{1,0:T(8,128)S(1)}, u32[]{:S(2)}, u32[]{:S(2)}) collective-permute-start(f32[8,128]{1,0:T(8,128)S(1)} %add_add_fusion.1), channel_id=1, source_target_pairs={{0,64},{1,17},{2,66},{3,19},{4,68},{5,21},{6,70},{7,23},{8,72},{9,... | collective-permute-start | bytes 12296 | tf_op jit(solution)/shard_map/ppermute | solution.py:50
  81.9 1.8 %collective-permute-start.20 = (f32[8,128]{1,0:T(8,128)S(1)}, f32[8,128]{1,0:T(8,128)S(1)}, u32[]{:S(2)}, u32[]{:S(2)}) collective-permute-start(f32[8,128]{1,0:T(8,128)S(1)} %add_add_fusion.1), channel_id=1, source_target_pairs={{0,96},{1,25},{2,98},{3,27},{4,100},{5,29},{6,102},{7,31},{8,104},... | collective-permute-start | bytes 12296 | tf_op jit(solution)/shard_map/ppermute | solution.py:50
  83.6 0.3 collective-permute-start.25
  83.9 1.8 %collective-permute-done.19 = f32[8,128]{1,0:T(8,128)S(1)} collective-permute-done((f32[8,128]{1,0:T(8,128)S(1)}, f32[8,128]{1,0:T(8,128)S(1)}, u32[]{:S(2)}, u32[]{:S(2)}) %collective-permute-start.19) | collective-permute-done | bytes 4128 | tf_op jit(solution)/shard_map/ppermute | solution.py:50
  85.7 0.4 collective-permute-done.20
  86.1 0.5 slice.110
  87.4 3.4 %collective-permute-done.25 = f32[2,32,896]{2,1,0:T(8,128)S(1)} collective-permute-done((f32[2,32,896]{2,1,0:T(8,128)S(1)}, f32[2,32,896]{2,1,0:T(8,128)S(1)}, u32[]{:S(2)}, u32[]{:S(2)}) %collective-permute-start.25) | collective-permute-done | bytes 229408 | tf_op jit(solution)/shard_map/ppermute | solution.py:50
  90.9 0.2 fusion.25
  91.1 2.5 %collective-permute-start.26 = (f32[2,2,32,896]{3,2,1,0:T(8,128)S(1)}, f32[2,2,32,896]{3,2,1,0:T(8,128)S(1)}, u32[]{:S(2)}, u32[]{:S(2)}) collective-permute-start(f32[2,2,32,896]{3,2,1,0:T(8,128)S(1)} %pad_maximum_fusion.1.refs_1_), channel_id=1, source_target_pairs={{0,96},{1,25},{2,98},{3,27},{4,100},{5,29},{6,102},{7,31},{8,104},... | collective-permute-start | bytes 1376264 | tf_op jit(solution)/shard_map/ppermute | solution.py:50
  93.8 0.6 collective-permute-start.28
  94.4 2.7 %collective-permute-start.29 = (f32[2,2,32,896]{3,2,1,0:T(8,128)S(1)}, f32[2,2,32,896]{3,2,1,0:T(8,128)S(1)}, u32[]{:S(2)}, u32[]{:S(2)}) collective-permute-start(f32[2,2,32,896]{3,2,1,0:T(8,128)S(1)} %pad_maximum_fusion.refs_0_), channel_id=1, source_target_pairs={{0,96},{1,25},{2,98},{3,27},{4,100},{5,29},{6,102},{7,31},{8,104},... | collective-permute-start | bytes 1376264 | tf_op jit(solution)/shard_map/ppermute | solution.py:50
  97.1 2.6 %collective-permute-done.26.refs_1_ = f32[2,2,32,896]{3,2,1,0:T(8,128)S(1)} collective-permute-done((f32[2,2,32,896]{3,2,1,0:T(8,128)S(1)}, f32[2,2,32,896]{3,2,1,0:T(8,128)S(1)}, u32[]{:S(2)}, u32[]{:S(2)}) %collective-permute-start.26) | collective-permute-done | bytes 458784 | tf_op jit(solution)/shard_map/ppermute | solution.py:50
  99.7 3.7 %collective-permute-start.27 = (f32[2,2,32,896]{3,2,1,0:T(8,128)S(1)}, f32[2,2,32,896]{3,2,1,0:T(8,128)S(1)}, u32[]{:S(2)}, u32[]{:S(2)}) collective-permute-start(f32[2,2,32,896]{3,2,1,0:T(8,128)S(1)} %collective-permute-done.26.refs_1_), channel_id=1, source_target_pairs={{0,96},{1,25},{2,98},{3,27},{4,100},{5,29},{6,102},{7,31},{8,104},... | collective-permute-start | bytes 1376264 | tf_op jit(solution)/shard_map/ppermute | solution.py:50
  103.4 0.1 collective-permute-done.22.refs_0_
  103.5 0.7 fusion.28
  104.1 1.0 unpack2.4.refs_2_
  105.1 1.0 unpack2.5.refs_2_
  106.1 2.2 %collective-permute-done.28.refs_0_ = f32[2,2,32,896]{3,2,1,0:T(8,128)S(1)} collective-permute-done((f32[2,2,32,896]{3,2,1,0:T(8,128)S(1)}, f32[2,2,32,896]{3,2,1,0:T(8,128)S(1)}, u32[]{:S(2)}, u32[]{:S(2)}) %collective-permute-start.28) | collective-permute-done | bytes 458784 | tf_op jit(solution)/shard_map/ppermute | solution.py:50
  108.4 1.0 unpack2.6.refs_2_
  109.4 0.1 collective-permute-done.27.refs_1_
  109.5 3.8 %collective-permute-done.23.refs_0_ = f32[2,2,32,896]{3,2,1,0:T(8,128)S(1)} collective-permute-done((f32[2,2,32,896]{3,2,1,0:T(8,128)S(1)}, f32[2,2,32,896]{3,2,1,0:T(8,128)S(1)}, u32[]{:S(2)}, u32[]{:S(2)}) %collective-permute-start.23) | collective-permute-done | bytes 458784 | tf_op jit(solution)/shard_map/ppermute | solution.py:50
  113.3 1.0 unpack2.7
  (25 shorter events, 0.4 us)
Async XLA Ops:
  0.6 2.0 %copy-start = (f32[1,32,28672]{2,1,0:T(8,128)S(1)}, f32[1,32,28672]{2,1,0:T(8,128)}, u32[]{:S(2)}) copy-start(f32[1,32,28672]{2,1,0:T(8,128)} %param.4) | copy-start | bytes 11010052
  2.7 6.4 %copy-start.1 = (f32[32,28672]{1,0:T(8,128)S(1)}, f32[32,28672]{1,0:T(8,128)}, u32[]{:S(2)}) copy-start(f32[32,28672]{1,0:T(8,128)} %refs_0_.1) | copy-start | bytes 11010052
  3.9 23.6 %collective-permute-start.2 = (f32[4,2,32,896]{3,2,1,0:T(8,128)S(1)}, f32[4,2,32,896]{3,2,1,0:T(8,128)S(1)}, u32[]{:S(2)}, u32[]{:S(2)}) collective-permute-start(f32[4,2,32,896]{3,2,1,0:T(8,128)S(1)} %get-tuple-element.10.refs_2_), channel_id=1, source_target_pairs={{0,96},{1,25},{2,98},{3,27},{4,100},{5,29},{6,102},{7,31},{8,104},... | collective-permute-start | bytes 2752520 | tf_op jit(solution)/shard_map/ppermute | solution.py:50
  6.8 3.1 %copy-start.2 = (f32[32,896]{1,0:T(8,128)S(1)}, f32[32,896]{1,0:T(8,128)}, u32[]{:S(2)}) copy-start(f32[32,896]{1,0:T(8,128)} %param.5) | copy-start | bytes 344068
  6.8 24.4 %collective-permute-start.1 = (f32[4,2,32,896]{3,2,1,0:T(8,128)S(1)}, f32[4,2,32,896]{3,2,1,0:T(8,128)S(1)}, u32[]{:S(2)}, u32[]{:S(2)}) collective-permute-start(f32[4,2,32,896]{3,2,1,0:T(8,128)S(1)} %get-tuple-element.13), channel_id=1, source_target_pairs={{0,32},{1,9},{2,34},{3,11},{4,36},{5,13},{6,38},{7,15},{8,40},{9,1... | collective-permute-start | bytes 2752520 | tf_op jit(solution)/shard_map/ppermute | solution.py:50
  6.8 24.4 %collective-permute-start = (f32[4,2,32,896]{3,2,1,0:T(8,128)S(1)}, f32[4,2,32,896]{3,2,1,0:T(8,128)S(1)}, u32[]{:S(2)}, u32[]{:S(2)}) collective-permute-start(f32[4,2,32,896]{3,2,1,0:T(8,128)S(1)} %pack1.1.refs_1_), channel_id=1, source_target_pairs={{0,64},{1,17},{2,66},{3,19},{4,68},{5,21},{6,70},{7,23},{8,72},{9,... | collective-permute-start | bytes 2752520 | tf_op jit(solution)/shard_map/ppermute | solution.py:50
  9.9 11.6 %collective-permute-start.3 = (f32[32,896]{1,0:T(8,128)S(1)}, f32[32,896]{1,0:T(8,128)S(1)}, u32[]{:S(2)}, u32[]{:S(2)}) collective-permute-start(f32[32,896]{1,0:T(8,128)S(1)} %copy-done.2), channel_id=1, source_target_pairs={{0,128},{1,129},{2,130},{3,131},{4,132},{5,133},{6,134},{7,135},{8... | collective-permute-start | bytes 344072 | tf_op jit(solution)/shard_map/ppermute | solution.py:50
  31.5 7.6 %collective-permute-start.4 = (f32[2,32,896]{2,1,0:T(8,128)S(1)}, f32[2,32,896]{2,1,0:T(8,128)S(1)}, u32[]{:S(2)}, u32[]{:S(2)}) collective-permute-start(f32[2,32,896]{2,1,0:T(8,128)S(1)} %get-tuple-element.18), channel_id=1, source_target_pairs={{0,16},{1,65},{2,18},{3,67},{4,20},{5,69},{6,22},{7,71},{8,24},{9,... | collective-permute-start | bytes 688136 | tf_op jit(solution)/shard_map/ppermute | solution.py:50
  34.7 7.2 %collective-permute-start.5 = (f32[2,32,896]{2,1,0:T(8,128)S(1)}, f32[2,32,896]{2,1,0:T(8,128)S(1)}, u32[]{:S(2)}, u32[]{:S(2)}) collective-permute-start(f32[2,32,896]{2,1,0:T(8,128)S(1)} %get-tuple-element.20), channel_id=1, source_target_pairs={{0,8},{1,33},{2,10},{3,35},{4,12},{5,37},{6,14},{7,39},{8,16},{9,4... | collective-permute-start | bytes 688136 | tf_op jit(solution)/shard_map/ppermute | solution.py:50
  35.4 6.6 %collective-permute-start.6 = (f32[2,32,896]{2,1,0:T(8,128)S(1)}, f32[2,32,896]{2,1,0:T(8,128)S(1)}, u32[]{:S(2)}, u32[]{:S(2)}) collective-permute-start(f32[2,32,896]{2,1,0:T(8,128)S(1)} %get-tuple-element.19), channel_id=1, source_target_pairs={{0,24},{1,97},{2,26},{3,99},{4,28},{5,101},{6,30},{7,103},{8,0},{9... | collective-permute-start | bytes 688136 | tf_op jit(solution)/shard_map/ppermute | solution.py:50
  42.1 14.8 %collective-permute-start.7 = (f32[2,32,896]{2,1,0:T(8,128)S(1)}, f32[2,32,896]{2,1,0:T(8,128)S(1)}, u32[]{:S(2)}, u32[]{:S(2)}) collective-permute-start(f32[2,32,896]{2,1,0:T(8,128)S(1)} %fusion.20), channel_id=1, source_target_pairs={{0,128},{1,129},{2,130},{3,131},{4,132},{5,133},{6,134},{7,135},{8... | collective-permute-start | bytes 688136 | tf_op jit(solution)/shard_map/ppermute | solution.py:50
  48.5 8.4 %collective-permute-start.10 = (f32[2,32,896]{2,1,0:T(8,128)S(1)}, f32[2,32,896]{2,1,0:T(8,128)S(1)}, u32[]{:S(2)}, u32[]{:S(2)}) collective-permute-start(f32[2,32,896]{2,1,0:T(8,128)S(1)} %pad_maximum_fusion.2), channel_id=1, source_target_pairs={{0,8},{1,33},{2,10},{3,35},{4,12},{5,37},{6,14},{7,39},{8,16},{9,4... | collective-permute-start | bytes 688136 | tf_op jit(solution)/shard_map/ppermute | solution.py:50
  49.7 7.2 %collective-permute-start.8 = (f32[2,32,896]{2,1,0:T(8,128)S(1)}, f32[2,32,896]{2,1,0:T(8,128)S(1)}, u32[]{:S(2)}, u32[]{:S(2)}) collective-permute-start(f32[2,32,896]{2,1,0:T(8,128)S(1)} %pad_maximum_fusion.2), channel_id=1, source_target_pairs={{0,24},{1,97},{2,26},{3,99},{4,28},{5,101},{6,30},{7,103},{8,0},{9... | collective-permute-start | bytes 688136 | tf_op jit(solution)/shard_map/ppermute | solution.py:50
  51.7 7.9 %collective-permute-start.9 = (f32[2,32,896]{2,1,0:T(8,128)S(1)}, f32[2,32,896]{2,1,0:T(8,128)S(1)}, u32[]{:S(2)}, u32[]{:S(2)}) collective-permute-start(f32[2,32,896]{2,1,0:T(8,128)S(1)} %pad_maximum_fusion.2), channel_id=1, source_target_pairs={{0,16},{1,65},{2,18},{3,67},{4,20},{5,69},{6,22},{7,71},{8,24},{9,... | collective-permute-start | bytes 688136 | tf_op jit(solution)/shard_map/ppermute | solution.py:50
  60.9 1.3 %collective-permute-start.11 = (f32[8,128]{1,0:T(8,128)S(1)}, f32[8,128]{1,0:T(8,128)S(1)}, u32[]{:S(2)}, u32[]{:S(2)}) collective-permute-start(f32[8,128]{1,0:T(8,128)S(1)} %broadcast_in_dim.2), channel_id=1, source_target_pairs={{0,1},{1,0},{2,3},{3,2},{4,5},{5,4},{6,7},{7,6},{8,9},{9,8},{10,11... | collective-permute-start | bytes 12296 | tf_op jit(solution)/shard_map/ppermute | solution.py:50
  62.8 3.7 %collective-permute-start.12 = (f32[8,128]{1,0:T(8,128)S(1)}, f32[8,128]{1,0:T(8,128)S(1)}, u32[]{:S(2)}, u32[]{:S(2)}) collective-permute-start(f32[8,128]{1,0:T(8,128)S(1)} %broadcast_add_fusion), channel_id=1, source_target_pairs={{0,2},{1,3},{2,4},{3,5},{4,6},{5,7},{6,0},{7,1},{8,10},{9,11},{10,... | collective-permute-start | bytes 12296 | tf_op jit(solution)/shard_map/ppermute | solution.py:50
  63.9 4.5 %collective-permute-start.13 = (f32[8,128]{1,0:T(8,128)S(1)}, f32[8,128]{1,0:T(8,128)S(1)}, u32[]{:S(2)}, u32[]{:S(2)}) collective-permute-start(f32[8,128]{1,0:T(8,128)S(1)} %broadcast_add_fusion), channel_id=1, source_target_pairs={{0,4},{1,5},{2,6},{3,7},{4,0},{5,1},{6,2},{7,3},{8,12},{9,13},{10,... | collective-permute-start | bytes 12296 | tf_op jit(solution)/shard_map/ppermute | solution.py:50
  66.3 3.6 %collective-permute-start.14 = (f32[8,128]{1,0:T(8,128)S(1)}, f32[8,128]{1,0:T(8,128)S(1)}, u32[]{:S(2)}, u32[]{:S(2)}) collective-permute-start(f32[8,128]{1,0:T(8,128)S(1)} %broadcast_add_fusion), channel_id=1, source_target_pairs={{0,6},{1,7},{2,0},{3,1},{4,2},{5,3},{6,4},{7,5},{8,14},{9,15},{10,... | collective-permute-start | bytes 12296 | tf_op jit(solution)/shard_map/ppermute | solution.py:50
  70.5 4.9 %collective-permute-start.15 = (f32[8,128]{1,0:T(8,128)S(1)}, f32[8,128]{1,0:T(8,128)S(1)}, u32[]{:S(2)}, u32[]{:S(2)}) collective-permute-start(f32[8,128]{1,0:T(8,128)S(1)} %add_add_fusion.2), channel_id=1, source_target_pairs={{0,8},{1,33},{2,10},{3,35},{4,12},{5,37},{6,14},{7,39},{8,16},{9,4... | collective-permute-start | bytes 12296 | tf_op jit(solution)/shard_map/ppermute | solution.py:50
  72.0 5.1 %collective-permute-start.16 = (f32[8,128]{1,0:T(8,128)S(1)}, f32[8,128]{1,0:T(8,128)S(1)}, u32[]{:S(2)}, u32[]{:S(2)}) collective-permute-start(f32[8,128]{1,0:T(8,128)S(1)} %add_add_fusion.2), channel_id=1, source_target_pairs={{0,16},{1,65},{2,18},{3,67},{4,20},{5,69},{6,22},{7,71},{8,24},{9,... | collective-permute-start | bytes 12296 | tf_op jit(solution)/shard_map/ppermute | solution.py:50
  73.9 3.6 %collective-permute-start.17 = (f32[8,128]{1,0:T(8,128)S(1)}, f32[8,128]{1,0:T(8,128)S(1)}, u32[]{:S(2)}, u32[]{:S(2)}) collective-permute-start(f32[8,128]{1,0:T(8,128)S(1)} %add_add_fusion.2), channel_id=1, source_target_pairs={{0,24},{1,97},{2,26},{3,99},{4,28},{5,101},{6,30},{7,103},{8,0},{9... | collective-permute-start | bytes 12296 | tf_op jit(solution)/shard_map/ppermute | solution.py:50
  77.5 6.2 %collective-permute-start.18 = (f32[8,128]{1,0:T(8,128)S(1)}, f32[8,128]{1,0:T(8,128)S(1)}, u32[]{:S(2)}, u32[]{:S(2)}) collective-permute-start(f32[8,128]{1,0:T(8,128)S(1)} %add_add_fusion.1), channel_id=1, source_target_pairs={{0,32},{1,9},{2,34},{3,11},{4,36},{5,13},{6,38},{7,15},{8,40},{9,1... | collective-permute-start | bytes 12296 | tf_op jit(solution)/shard_map/ppermute | solution.py:50
  77.5 9.9 %collective-permute-start.21 = (f32[2,32,896]{2,1,0:T(8,128)S(1)}, f32[2,32,896]{2,1,0:T(8,128)S(1)}, u32[]{:S(2)}, u32[]{:S(2)}) collective-permute-start(f32[2,32,896]{2,1,0:T(8,128)S(1)} %get-tuple-element.26), channel_id=1, source_target_pairs={{0,24},{1,97},{2,26},{3,99},{4,28},{5,101},{6,30},{7,103},{8,0},{9... | collective-permute-start | bytes 688136 | tf_op jit(solution)/shard_map/ppermute | solution.py:50
  79.9 7.5 %collective-permute-start.24 = (f32[2,32,896]{2,1,0:T(8,128)S(1)}, f32[2,32,896]{2,1,0:T(8,128)S(1)}, u32[]{:S(2)}, u32[]{:S(2)}) collective-permute-start(f32[2,32,896]{2,1,0:T(8,128)S(1)} %get-tuple-element.26), channel_id=1, source_target_pairs={{0,16},{1,65},{2,18},{3,67},{4,20},{5,69},{6,22},{7,71},{8,24},{9,... | collective-permute-start | bytes 688136 | tf_op jit(solution)/shard_map/ppermute | solution.py:50
  80.5 5.2 %collective-permute-start.19 = (f32[8,128]{1,0:T(8,128)S(1)}, f32[8,128]{1,0:T(8,128)S(1)}, u32[]{:S(2)}, u32[]{:S(2)}) collective-permute-start(f32[8,128]{1,0:T(8,128)S(1)} %add_add_fusion.1), channel_id=1, source_target_pairs={{0,64},{1,17},{2,66},{3,19},{4,68},{5,21},{6,70},{7,23},{8,72},{9,... | collective-permute-start | bytes 12296 | tf_op jit(solution)/shard_map/ppermute | solution.py:50
  81.9 4.2 %collective-permute-start.20 = (f32[8,128]{1,0:T(8,128)S(1)}, f32[8,128]{1,0:T(8,128)S(1)}, u32[]{:S(2)}, u32[]{:S(2)}) collective-permute-start(f32[8,128]{1,0:T(8,128)S(1)} %add_add_fusion.1), channel_id=1, source_target_pairs={{0,96},{1,25},{2,98},{3,27},{4,100},{5,29},{6,102},{7,31},{8,104},... | collective-permute-start | bytes 12296 | tf_op jit(solution)/shard_map/ppermute | solution.py:50
  83.6 7.2 %collective-permute-start.25 = (f32[2,32,896]{2,1,0:T(8,128)S(1)}, f32[2,32,896]{2,1,0:T(8,128)S(1)}, u32[]{:S(2)}, u32[]{:S(2)}) collective-permute-start(f32[2,32,896]{2,1,0:T(8,128)S(1)} %get-tuple-element.26), channel_id=1, source_target_pairs={{0,8},{1,33},{2,10},{3,35},{4,12},{5,37},{6,14},{7,39},{8,16},{9,4... | collective-permute-start | bytes 688136 | tf_op jit(solution)/shard_map/ppermute | solution.py:50
  91.1 8.6 %collective-permute-start.26 = (f32[2,2,32,896]{3,2,1,0:T(8,128)S(1)}, f32[2,2,32,896]{3,2,1,0:T(8,128)S(1)}, u32[]{:S(2)}, u32[]{:S(2)}) collective-permute-start(f32[2,2,32,896]{3,2,1,0:T(8,128)S(1)} %pad_maximum_fusion.1.refs_1_), channel_id=1, source_target_pairs={{0,96},{1,25},{2,98},{3,27},{4,100},{5,29},{6,102},{7,31},{8,104},... | collective-permute-start | bytes 1376264 | tf_op jit(solution)/shard_map/ppermute | solution.py:50
  93.7 9.8 %collective-permute-start.22 = (f32[2,2,32,896]{3,2,1,0:T(8,128)S(1)}, f32[2,2,32,896]{3,2,1,0:T(8,128)S(1)}, u32[]{:S(2)}, u32[]{:S(2)}) collective-permute-start(f32[2,2,32,896]{3,2,1,0:T(8,128)S(1)} %pad_maximum_fusion.refs_0_), channel_id=1, source_target_pairs={{0,32},{1,9},{2,34},{3,11},{4,36},{5,13},{6,38},{7,15},{8,40},{9,1... | collective-permute-start | bytes 1376264 | tf_op jit(solution)/shard_map/ppermute | solution.py:50
  93.8 14.6 %collective-permute-start.28 = (f32[2,2,32,896]{3,2,1,0:T(8,128)S(1)}, f32[2,2,32,896]{3,2,1,0:T(8,128)S(1)}, u32[]{:S(2)}, u32[]{:S(2)}) collective-permute-start(f32[2,2,32,896]{3,2,1,0:T(8,128)S(1)} %pad_maximum_fusion.1.refs_1_), channel_id=1, source_target_pairs={{0,32},{1,9},{2,34},{3,11},{4,36},{5,13},{6,38},{7,15},{8,40},{9,1... | collective-permute-start | bytes 1376264 | tf_op jit(solution)/shard_map/ppermute | solution.py:50
  94.4 14.0 %collective-permute-start.29 = (f32[2,2,32,896]{3,2,1,0:T(8,128)S(1)}, f32[2,2,32,896]{3,2,1,0:T(8,128)S(1)}, u32[]{:S(2)}, u32[]{:S(2)}) collective-permute-start(f32[2,2,32,896]{3,2,1,0:T(8,128)S(1)} %pad_maximum_fusion.refs_0_), channel_id=1, source_target_pairs={{0,96},{1,25},{2,98},{3,27},{4,100},{5,29},{6,102},{7,31},{8,104},... | collective-permute-start | bytes 1376264 | tf_op jit(solution)/shard_map/ppermute | solution.py:50
  99.7 9.8 %collective-permute-start.27 = (f32[2,2,32,896]{3,2,1,0:T(8,128)S(1)}, f32[2,2,32,896]{3,2,1,0:T(8,128)S(1)}, u32[]{:S(2)}, u32[]{:S(2)}) collective-permute-start(f32[2,2,32,896]{3,2,1,0:T(8,128)S(1)} %collective-permute-done.26.refs_1_), channel_id=1, source_target_pairs={{0,96},{1,25},{2,98},{3,27},{4,100},{5,29},{6,102},{7,31},{8,104},... | collective-permute-start | bytes 1376264 | tf_op jit(solution)/shard_map/ppermute | solution.py:50
  103.5 9.8 %collective-permute-start.23 = (f32[2,2,32,896]{3,2,1,0:T(8,128)S(1)}, f32[2,2,32,896]{3,2,1,0:T(8,128)S(1)}, u32[]{:S(2)}, u32[]{:S(2)}) collective-permute-start(f32[2,2,32,896]{3,2,1,0:T(8,128)S(1)} %collective-permute-done.22.refs_0_), channel_id=1, source_target_pairs={{0,32},{1,9},{2,34},{3,11},{4,36},{5,13},{6,38},{7,15},{8,40},{9,1... | collective-permute-start | bytes 1376264 | tf_op jit(solution)/shard_map/ppermute | solution.py:50

commit v4 on v3

--- a/solution.py
+++ b/solution.py
@@ -135,11 +135,72 @@
     )(*pieces, *given)
 
 
+def squares_kernel(value, total):
+    halves, rows, width = value.shape
+    sums = jnp.zeros((8, 128), jnp.float32)
+    for half in range(halves):
+        for row in range(0, rows, 8):
+            for column in range(0, width, 128):
+                tile = value[half, row : row + 8, column : column + 128]
+                sums = sums + tile * tile
+    total[...] = sums
+
+
+def squares_of(value):
+    return pl.pallas_call(
+        squares_kernel,
+        out_shape=jax.ShapeDtypeStruct((8, 128), value.dtype),
+        in_specs=[pl.BlockSpec(memory_space=pltpu.VMEM)],
+        out_specs=pl.BlockSpec(memory_space=pltpu.VMEM),
+        cost_estimate=pl.CostEstimate(flops=2 * value.size, bytes_accessed=4 * value.size, transcendentals=0),
+        compiler_params=pltpu.CompilerParams(vmem_limit_bytes=ROOM),
+        name="squares",
+    )(value)
+
+
+def update_kernel(count, *refs):
+    squares, base, averages, speeds = refs[:SIDE], refs[SIDE], refs[SIDE + 1 : 2 * SIDE + 1], refs[2 * SIDE + 1 : -3]
+    early, late, kept = refs[-3:]
+    total = squares[0][...]
+    for more in squares[1:]:
+        total = total + more[...]
+    total = jnp.sum(jnp.sum(total, axis=0, keepdims=True), axis=1, keepdims=True)
+    factor = jnp.minimum(1.0, clip_level / jnp.sqrt(total / count + 1e-06))
+    for near in range(SIDE):
+        for half in range(HALVES):
+            clipped = factor * averages[near][half]
+            new_momentum = moment_decay * speeds[near][half] + clipped
+            if near == half == 0:
+                kept[...] = new_momentum
+            (early if near < 2 else late)[near % 2, half] = base[near, half] - outer_rate * (
+                clipped + moment_decay * new_momentum
+            )
+
+
+def update(squares, base, averages, speeds, count):
+    rows, width = base.shape[-2:]
+    part = jax.ShapeDtypeStruct((2, HALVES, rows, width), base.dtype)
+    vmem = pl.BlockSpec(memory_space=pltpu.VMEM)
+    return pl.pallas_call(
+        functools.partial(update_kernel, count),
+        out_shape=[part, part, jax.ShapeDtypeStruct((rows, width), base.dtype)],
+        in_specs=[vmem] * (1 + 3 * SIDE),
+        out_specs=[vmem] * 3,
+        cost_estimate=pl.CostEstimate(flops=8 * base.size, bytes_accessed=16 * base.size, transcendentals=0),
+        compiler_params=pltpu.CompilerParams(vmem_limit_bytes=ROOM),
+        name="update",
+    )(*squares, base, *averages, *speeds)
+
+
 def spread_near(value):
     near = [value] + [None] * (SIDE - 1)
     for step in (2, 1, 3):
         near[SIDE - step] = send(value, SECOND[step])
     return near
+
+
+def exchange(value, route):
+    return value + send(value, route[1]) + send(value, route[2]) + send(value, route[3])
 
 
 def after(value, *others):
@@ -155,18 +216,25 @@
 
     (far,) = pack((local,), ((0, 2),), width)
     right, left = pack((local,), ((0, 1), (0, 3)), width, (far,))
-    far = send(far, FIRST[2])
-    packed = left
-    right, left = send(right, FIRST[1]), send(left, FIRST[3])
-    base, mine = pack((global_weights, local), ((0, 0), (1, 0)), width, (packed,))
+    up, down = send(far[:2], FIRST[1]), send(far[2:], FIRST[3])
+    from_left, from_right = send(right[2:], FIRST[1]), send(left[:2], FIRST[3])
+    base, base_right, base_left, mine = pack(
+        (global_weights, local), ((0, 0), (0, 1), (0, 3), (1, 0)), width, (left,)
+    )
+    up = (base_right[:2] - right[:2]) + (base_right[:2] - up)
+    down = (base_left[2:] - left[2:]) + (base_left[2:] - down)
     speed = after(momentum, base)
     speed = jnp.stack([speed, send(speed, ACROSS)])
-    left = after(left, speed)
+    relay_up, relay_down = send(up, FIRST[1]), send(down, FIRST[3])
+    relay_up = after(relay_up, speed)
     parts = []
     for near in range(SIDE):
+        k = near % 2
         total = base[near] - mine[near]
-        for piece in (far, right, left):
-            total = total + (base[near] - piece[near])
+        if near < 2:
+            total = total + (base[near] - from_right[k]) + relay_up[k]
+        else:
+            total = total + (base[near] - from_left[k]) + relay_down[k]
         parts.append(total)
     got = [send(parts[step], SECOND[step]) for step in (2, 1, 3)]
     pair = parts[0] + got[0] + got[1] + got[2]
@@ -174,25 +242,17 @@
     other = send(pair, ACROSS)
     summed = pair + jnp.stack([other[1], other[0]])
     speeds = spread_near(after(speed, pair))
-    summed = after(summed, *speeds)
     average = summed / islands
     nears = spread_near(average)
 
     count = rows * columns * shards
-    squares = jnp.broadcast_to(jnp.sum(average * average).reshape(1, 1), (8, 128))
+    squares = squares_of(average)
     squares = squares + send(squares, TWIN)
-    for route in (UP, SECOND, FIRST):
-        squares = squares + send(squares, route[1]) + send(squares, route[2]) + send(squares, route[3])
-    spread = jnp.sqrt(squares[0, 0] / count + 1e-06)
-    factor = jnp.minimum(1.0, clip_level / spread)
-
-    def update(base, average, speed):
-        clipped = factor * average
-        return base - outer_rate * (clipped + moment_decay * (moment_decay * speed + clipped))
-
-    new_momentum = moment_decay * momentum + factor * average[0]
-    early = jnp.stack([update(base[k], nears[k], speeds[k]) for k in range(2)])
-    late = jnp.stack([update(base[2 + k], nears[2 + k], speeds[2 + k]) for k in range(2)])
+    squares = after(squares, *speeds)
+    squares = exchange(squares, UP)
+    squares = exchange(squares, SECOND)
+    squares = [squares] + [send(squares, FIRST[step]) for step in (1, 2, 3)]
+    early, late, new_momentum = update(squares, base, nears, speeds, count)
 
     left_early, right_late = send(early, FIRST[1]), send(late, FIRST[3])
     left_late, right_early = send(late, FIRST[1]), send(early, FIRST[3])

time: 115 us -> 104 us (0.904)
  the two profiles are of different devices: /device:TPU:32 before, /device:TPU:2 now
where the time goes in v4:
time: 104 us; the launch traced here: 103 us
  starting transfers between devices  58.6 us (56%)
  waiting for transfers between devices  32.6 us (31%)
  Pallas kernels  7.9 us (8%)
  local copies, waits for them, and re-layouts  2.12 us (2%)
    ppermute x33, starting transfers between devices, send(): return lax.ppermute(value, AXES, route)  58.6 us
    ppermute x33, waiting for transfers between devices, send(): return lax.ppermute(value, AXES, route)  32.6 us
    pallas_call x4, Pallas kernels, unpack(): pl.pallas_call(functools.partial(unpack_kernel, groups, width), out_shape...  3.94 us
    pallas_call x3, Pallas kernels, pack(): pl.pallas_call(functools.partial(pack_kernel, jobs, width), out_shape=[ja...  3 us
  transfers between devices with their start and end apart: 33, of which 18 were waited for; matrix products, arithmetic and copies ran while one was open for 0% of the time, Pallas kernels for 5%

profile of v4, /device:TPU:2, one launch (start us, length us, event | category | flops | bytes accessed | tf_op | source)
XLA Modules:
  0.0 102.7 jit_solution(13898645731119506610)
XLA Ops:
  0.6 2.0 %copy-done = f32[1,32,28672]{2,1,0:T(8,128)S(1)} copy-done((f32[1,32,28672]{2,1,0:T(8,128)S(1)}, f32[1,32,28672]{2,1,0:T(8,128)}, u32[]{:S(2)}) %copy-start) | copy-done | bytes 3670040
  2.7 0.4 pack1.1.refs_1_
  3.1 0.1 fusion.14
  3.2 1.6 %collective-permute-start.1 = (f32[2,2,32,896]{3,2,1,0:T(8,128)S(1)}, f32[2,2,32,896]{3,2,1,0:T(8,128)S(1)}, u32[]{:S(2)}, u32[]{:S(2)}) collective-permute-start(f32[2,2,32,896]{3,2,1,0:T(8,128)S(1)} %get-tuple-element.33), channel_id=1, source_target_pairs={{0,32},{1,9},{2,34},{3,11},{4,36},{5,13},{6,38},{7,15},{8,40},{9,1... | collective-permute-start | bytes 1376264 | tf_op jit(solution)/shard_map/ppermute | solution.py:50
  4.7 0.9 collective-permute-start.5
  5.6 0.8 pack2.1
  6.4 1.8 %pack4.1 = (f32[4,2,32,896]{3,2,1,0:T(8,128)S(1)}, f32[4,2,32,896]{3,2,1,0:T(8,128)S(1)}, f32[4,2,32,896]{3,2,1,0:T(8,128)S(1)}, f32[4,2,32,896]{3,2,1,0:T(8,128)S(1)}) custom-call(f32[32,28672]{1,0:T(8,128)S(1)} %copy-done.1, f32[32,28672]{1,0:T(8,128)S(1)} %bitcast.19, f32[4,2,32,896]{3,2,1,0:T(8,128)S(1)} %get-tuple-element.15.refs_2_), custom_call_target="tpu_custom_call" | custom-call | bytes 7340032 | tf_op jit(solution)/shard_map/pack4/pallas_call | solution.py:93
  8.2 3.7 %collective-permute-done.1 = f32[2,2,32,896]{3,2,1,0:T(8,128)S(1)} collective-permute-done((f32[2,2,32,896]{3,2,1,0:T(8,128)S(1)}, f32[2,2,32,896]{3,2,1,0:T(8,128)S(1)}, u32[]{:S(2)}, u32[]{:S(2)}) %collective-permute-start.1) | collective-permute-done | bytes 458784 | tf_op jit(solution)/shard_map/ppermute | solution.py:50
  12.0 0.1 subtract_add_fusion.1
  12.1 1.3 %collective-permute-start.2 = (f32[2,2,32,896]{3,2,1,0:T(8,128)S(1)}, f32[2,2,32,896]{3,2,1,0:T(8,128)S(1)}, u32[]{:S(2)}, u32[]{:S(2)}) collective-permute-start(f32[2,2,32,896]{3,2,1,0:T(8,128)S(1)} %get-tuple-element.31), channel_id=1, source_target_pairs={{0,32},{1,9},{2,34},{3,11},{4,36},{5,13},{6,38},{7,15},{8,40},{9,1... | collective-permute-start | bytes 1376264 | tf_op jit(solution)/shard_map/ppermute | solution.py:50
  13.4 0.1 fusion.15
  13.5 2.1 %collective-permute-start = (f32[2,2,32,896]{3,2,1,0:T(8,128)S(1)}, f32[2,2,32,896]{3,2,1,0:T(8,128)S(1)}, u32[]{:S(2)}, u32[]{:S(2)}) collective-permute-start(f32[2,2,32,896]{3,2,1,0:T(8,128)S(1)} %get-tuple-element.35), channel_id=1, source_target_pairs={{0,96},{1,25},{2,98},{3,27},{4,100},{5,29},{6,102},{7,31},{8,104},... | collective-permute-start | bytes 1376264 | tf_op jit(solution)/shard_map/ppermute | solution.py:50
  15.6 3.2 %collective-permute-start.6 = (f32[2,2,32,896]{3,2,1,0:T(8,128)S(1)}, f32[2,2,32,896]{3,2,1,0:T(8,128)S(1)}, u32[]{:S(2)}, u32[]{:S(2)}) collective-permute-start(f32[2,2,32,896]{3,2,1,0:T(8,128)S(1)} %get-tuple-element.36), channel_id=1, source_target_pairs={{0,96},{1,25},{2,98},{3,27},{4,100},{5,29},{6,102},{7,31},{8,104},... | collective-permute-start | bytes 1376264 | tf_op jit(solution)/shard_map/ppermute | solution.py:50
  18.8 5.5 %collective-permute-start.3 = (f32[32,896]{1,0:T(8,128)S(1)}, f32[32,896]{1,0:T(8,128)S(1)}, u32[]{:S(2)}, u32[]{:S(2)}) collective-permute-start(f32[32,896]{1,0:T(8,128)S(1)} %copy-done.2), channel_id=1, source_target_pairs={{0,128},{1,129},{2,130},{3,131},{4,132},{5,133},{6,134},{7,135},{8... | collective-permute-start | bytes 344072 | tf_op jit(solution)/shard_map/ppermute | solution.py:50
  24.3 3.3 %collective-permute-done.3 = f32[32,896]{1,0:T(8,128)S(1)} collective-permute-done((f32[32,896]{1,0:T(8,128)S(1)}, f32[32,896]{1,0:T(8,128)S(1)}, u32[]{:S(2)}, u32[]{:S(2)}) %collective-permute-start.3) | collective-permute-done | bytes 114720 | tf_op jit(solution)/shard_map/ppermute | solution.py:50
  27.7 0.2 fusion.5
  27.9 3.7 %collective-permute-start.7 = (f32[2,32,896]{2,1,0:T(8,128)S(1)}, f32[2,32,896]{2,1,0:T(8,128)S(1)}, u32[]{:S(2)}, u32[]{:S(2)}) collective-permute-start(f32[2,32,896]{2,1,0:T(8,128)S(1)} %get-tuple-element.28), channel_id=1, source_target_pairs={{0,16},{1,65},{2,18},{3,67},{4,20},{5,69},{6,22},{7,71},{8,24},{9,... | collective-permute-start | bytes 688136 | tf_op jit(solution)/shard_map/ppermute | solution.py:50
  31.6 0.0 collective-permute-start.8
  31.6 3.2 %collective-permute-start.9 = (f32[2,32,896]{2,1,0:T(8,128)S(1)}, f32[2,32,896]{2,1,0:T(8,128)S(1)}, u32[]{:S(2)}, u32[]{:S(2)}) collective-permute-start(f32[2,32,896]{2,1,0:T(8,128)S(1)} %get-tuple-element.29), channel_id=1, source_target_pairs={{0,24},{1,97},{2,26},{3,99},{4,28},{5,101},{6,30},{7,103},{8,0},{9... | collective-permute-start | bytes 688136 | tf_op jit(solution)/shard_map/ppermute | solution.py:50
  34.8 0.8 collective-permute-done.7
  35.6 3.2 %collective-permute-done.8 = f32[2,32,896]{2,1,0:T(8,128)S(1)} collective-permute-done((f32[2,32,896]{2,1,0:T(8,128)S(1)}, f32[2,32,896]{2,1,0:T(8,128)S(1)}, u32[]{:S(2)}, u32[]{:S(2)}) %collective-permute-start.8) | collective-permute-done | bytes 229408 | tf_op jit(solution)/shard_map/ppermute | solution.py:50
  38.8 0.1 fusion.12
  38.9 6.2 %collective-permute-start.10 = (f32[2,32,896]{2,1,0:T(8,128)S(1)}, f32[2,32,896]{2,1,0:T(8,128)S(1)}, u32[]{:S(2)}, u32[]{:S(2)}) collective-permute-start(f32[2,32,896]{2,1,0:T(8,128)S(1)} %fusion.12), channel_id=1, source_target_pairs={{0,128},{1,129},{2,130},{3,131},{4,132},{5,133},{6,134},{7,135},{8... | collective-permute-start | bytes 688136 | tf_op jit(solution)/shard_map/ppermute | solution.py:50
  45.1 3.2 %collective-permute-start.12 = (f32[2,32,896]{2,1,0:T(8,128)S(1)}, f32[2,32,896]{2,1,0:T(8,128)S(1)}, u32[]{:S(2)}, u32[]{:S(2)}) collective-permute-start(f32[2,32,896]{2,1,0:T(8,128)S(1)} %pad_maximum_fusion.refs_9_), channel_id=1, source_target_pairs={{0,24},{1,97},{2,26},{3,99},{4,28},{5,101},{6,30},{7,103},{8,0},{9... | collective-permute-start | bytes 688136 | tf_op jit(solution)/shard_map/ppermute | solution.py:50
  48.3 0.1 collective-permute-start.13
  48.4 0.7 collective-permute-start.14
  49.1 3.3 %collective-permute-done.10 = f32[2,32,896]{2,1,0:T(8,128)S(1)} collective-permute-done((f32[2,32,896]{2,1,0:T(8,128)S(1)}, f32[2,32,896]{2,1,0:T(8,128)S(1)}, u32[]{:S(2)}, u32[]{:S(2)}) %collective-permute-start.10) | collective-permute-done | bytes 229408 | tf_op jit(solution)/shard_map/ppermute | solution.py:50
  52.5 0.1 squares.1
  52.6 0.1 collective-permute-start.11
  52.7 1.2 %collective-permute-done.11 = f32[8,128]{1,0:T(8,128)S(1)} collective-permute-done((f32[8,128]{1,0:T(8,128)S(1)}, f32[8,128]{1,0:T(8,128)S(1)}, u32[]{:S(2)}, u32[]{:S(2)}) %collective-permute-start.11) | collective-permute-done | bytes 4128 | tf_op jit(solution)/shard_map/ppermute | solution.py:50
  53.8 0.4 collective-permute-done.12.refs_10_
  54.3 1.6 %collective-permute-done.13.refs_11_ = f32[2,32,896]{2,1,0:T(8,128)S(1)} collective-permute-done((f32[2,32,896]{2,1,0:T(8,128)S(1)}, f32[2,32,896]{2,1,0:T(8,128)S(1)}, u32[]{:S(2)}, u32[]{:S(2)}) %collective-permute-start.13) | collective-permute-done | bytes 229408 | tf_op jit(solution)/shard_map/ppermute | solution.py:50
  55.9 2.2 %collective-permute-done.14.refs_12_ = f32[2,32,896]{2,1,0:T(8,128)S(1)} collective-permute-done((f32[2,32,896]{2,1,0:T(8,128)S(1)}, f32[2,32,896]{2,1,0:T(8,128)S(1)}, u32[]{:S(2)}, u32[]{:S(2)}) %collective-permute-start.14) | collective-permute-done | bytes 229408 | tf_op jit(solution)/shard_map/ppermute | solution.py:50
  58.1 1.1 %collective-permute-start.15 = (f32[8,128]{1,0:T(8,128)S(1)}, f32[8,128]{1,0:T(8,128)S(1)}, u32[]{:S(2)}, u32[]{:S(2)}) collective-permute-start(f32[8,128]{1,0:T(8,128)S(1)} %add.97), channel_id=1, source_target_pairs={{0,2},{1,3},{2,4},{3,5},{4,6},{5,7},{6,0},{7,1},{8,10},{9,11},{10,... | collective-permute-start | bytes 12296 | tf_op jit(solution)/shard_map/ppermute | solution.py:50
  59.2 1.4 %collective-permute-start.16 = (f32[8,128]{1,0:T(8,128)S(1)}, f32[8,128]{1,0:T(8,128)S(1)}, u32[]{:S(2)}, u32[]{:S(2)}) collective-permute-start(f32[8,128]{1,0:T(8,128)S(1)} %add.97), channel_id=1, source_target_pairs={{0,4},{1,5},{2,6},{3,7},{4,0},{5,1},{6,2},{7,3},{8,12},{9,13},{10,... | collective-permute-start | bytes 12296 | tf_op jit(solution)/shard_map/ppermute | solution.py:50
  60.6 1.9 %collective-permute-start.17 = (f32[8,128]{1,0:T(8,128)S(1)}, f32[8,128]{1,0:T(8,128)S(1)}, u32[]{:S(2)}, u32[]{:S(2)}) collective-permute-start(f32[8,128]{1,0:T(8,128)S(1)} %add.97), channel_id=1, source_target_pairs={{0,6},{1,7},{2,0},{3,1},{4,2},{5,3},{6,4},{7,5},{8,14},{9,15},{10,... | collective-permute-start | bytes 12296 | tf_op jit(solution)/shard_map/ppermute | solution.py:50
  62.5 1.0 collective-permute-done.15
  63.5 0.2 collective-permute-done.16
  63.7 0.5 collective-permute-done.17
  64.2 2.2 %collective-permute-start.19 = (f32[8,128]{1,0:T(8,128)S(1)}, f32[8,128]{1,0:T(8,128)S(1)}, u32[]{:S(2)}, u32[]{:S(2)}) collective-permute-start(f32[8,128]{1,0:T(8,128)S(1)} %add_add_fusion.1), channel_id=1, source_target_pairs={{0,16},{1,65},{2,18},{3,67},{4,20},{5,69},{6,22},{7,71},{8,24},{9,... | collective-permute-start | bytes 12296 | tf_op jit(solution)/shard_map/ppermute | solution.py:50
  66.4 1.0 collective-permute-start.20
  67.4 0.9 collective-permute-start.24
  68.4 2.1 %collective-permute-start.25 = (f32[2,32,896]{2,1,0:T(8,128)S(1)}, f32[2,32,896]{2,1,0:T(8,128)S(1)}, u32[]{:S(2)}, u32[]{:S(2)}) collective-permute-start(f32[2,32,896]{2,1,0:T(8,128)S(1)} %fusion.13.value.refs_5_), channel_id=1, source_target_pairs={{0,16},{1,65},{2,18},{3,67},{4,20},{5,69},{6,22},{7,71},{8,24},{9,... | collective-permute-start | bytes 688136 | tf_op jit(solution)/shard_map/ppermute | solution.py:50
  70.5 1.2 %collective-permute-start.26 = (f32[2,32,896]{2,1,0:T(8,128)S(1)}, f32[2,32,896]{2,1,0:T(8,128)S(1)}, u32[]{:S(2)}, u32[]{:S(2)}) collective-permute-start(f32[2,32,896]{2,1,0:T(8,128)S(1)} %fusion.13.value.refs_5_), channel_id=1, source_target_pairs={{0,8},{1,33},{2,10},{3,35},{4,12},{5,37},{6,14},{7,39},{8,16},{9,4... | collective-permute-start | bytes 688136 | tf_op jit(solution)/shard_map/ppermute | solution.py:50
  71.8 1.3 %collective-permute-start.21 = (f32[8,128]{1,0:T(8,128)S(1)}, f32[8,128]{1,0:T(8,128)S(1)}, u32[]{:S(2)}, u32[]{:S(2)}) collective-permute-start(f32[8,128]{1,0:T(8,128)S(1)} %add_add_fusion.refs_0_), channel_id=1, source_target_pairs={{0,32},{1,9},{2,34},{3,11},{4,36},{5,13},{6,38},{7,15},{8,40},{9,1... | collective-permute-start | bytes 12296 | tf_op jit(solution)/shard_map/ppermute | solution.py:50
  73.1 2.5 %collective-permute-start.22 = (f32[8,128]{1,0:T(8,128)S(1)}, f32[8,128]{1,0:T(8,128)S(1)}, u32[]{:S(2)}, u32[]{:S(2)}) collective-permute-start(f32[8,128]{1,0:T(8,128)S(1)} %add_add_fusion.refs_0_), channel_id=1, source_target_pairs={{0,64},{1,17},{2,66},{3,19},{4,68},{5,21},{6,70},{7,23},{8,72},{9,... | collective-permute-start | bytes 12296 | tf_op jit(solution)/shard_map/ppermute | solution.py:50
  75.6 2.7 %collective-permute-start.23 = (f32[8,128]{1,0:T(8,128)S(1)}, f32[8,128]{1,0:T(8,128)S(1)}, u32[]{:S(2)}, u32[]{:S(2)}) collective-permute-start(f32[8,128]{1,0:T(8,128)S(1)} %add_add_fusion.refs_0_), channel_id=1, source_target_pairs={{0,96},{1,25},{2,98},{3,27},{4,100},{5,29},{6,102},{7,31},{8,104},... | collective-permute-start | bytes 12296 | tf_op jit(solution)/shard_map/ppermute | solution.py:50
  78.4 1.3 %collective-permute-done.23.refs_3_ = f32[8,128]{1,0:T(8,128)S(1)} collective-permute-done((f32[8,128]{1,0:T(8,128)S(1)}, f32[8,128]{1,0:T(8,128)S(1)}, u32[]{:S(2)}, u32[]{:S(2)}) %collective-permute-start.23) | collective-permute-done | bytes 4128 | tf_op jit(solution)/shard_map/ppermute | solution.py:50
  79.7 0.9 update.1
  80.6 1.5 %collective-permute-start.27 = (f32[2,2,32,896]{3,2,1,0:T(8,128)S(1)}, f32[2,2,32,896]{3,2,1,0:T(8,128)S(1)}, u32[]{:S(2)}, u32[]{:S(2)}) collective-permute-start(f32[2,2,32,896]{3,2,1,0:T(8,128)S(1)} %get-tuple-element.25.refs_0_), channel_id=1, source_target_pairs={{0,32},{1,9},{2,34},{3,11},{4,36},{5,13},{6,38},{7,15},{8,40},{9,1... | collective-permute-start | bytes 1376264 | tf_op jit(solution)/shard_map/ppermute | solution.py:50
  82.1 0.8 collective-permute-start.29
  82.9 2.4 %collective-permute-start.31 = (f32[2,2,32,896]{3,2,1,0:T(8,128)S(1)}, f32[2,2,32,896]{3,2,1,0:T(8,128)S(1)}, u32[]{:S(2)}, u32[]{:S(2)}) collective-permute-start(f32[2,2,32,896]{3,2,1,0:T(8,128)S(1)} %get-tuple-element.26.refs_1_), channel_id=1, source_target_pairs={{0,32},{1,9},{2,34},{3,11},{4,36},{5,13},{6,38},{7,15},{8,40},{9,1... | collective-permute-start | bytes 1376264 | tf_op jit(solution)/shard_map/ppermute | solution.py:50
  85.3 0.8 collective-permute-start.32
  86.1 3.2 %collective-permute-done.27.refs_0_ = f32[2,2,32,896]{3,2,1,0:T(8,128)S(1)} collective-permute-done((f32[2,2,32,896]{3,2,1,0:T(8,128)S(1)}, f32[2,2,32,896]{3,2,1,0:T(8,128)S(1)}, u32[]{:S(2)}, u32[]{:S(2)}) %collective-permute-start.27) | collective-permute-done | bytes 458784 | tf_op jit(solution)/shard_map/ppermute | solution.py:50
  89.3 2.0 %collective-permute-start.28 = (f32[2,2,32,896]{3,2,1,0:T(8,128)S(1)}, f32[2,2,32,896]{3,2,1,0:T(8,128)S(1)}, u32[]{:S(2)}, u32[]{:S(2)}) collective-permute-start(f32[2,2,32,896]{3,2,1,0:T(8,128)S(1)} %collective-permute-done.27.refs_0_), channel_id=1, source_target_pairs={{0,32},{1,9},{2,34},{3,11},{4,36},{5,13},{6,38},{7,15},{8,40},{9,1... | collective-permute-start | bytes 1376264 | tf_op jit(solution)/shard_map/ppermute | solution.py:50
  91.3 0.5 collective-permute-done.29.refs_1_
  91.8 0.8 collective-permute-start.30
  92.6 1.0 unpack2.4.refs_2_
  93.6 1.0 unpack2.5.refs_2_
  94.6 2.1 %collective-permute-done.32.refs_1_ = f32[2,2,32,896]{3,2,1,0:T(8,128)S(1)} collective-permute-done((f32[2,2,32,896]{3,2,1,0:T(8,128)S(1)}, f32[2,2,32,896]{3,2,1,0:T(8,128)S(1)}, u32[]{:S(2)}, u32[]{:S(2)}) %collective-permute-start.32) | collective-permute-done | bytes 458784 | tf_op jit(solution)/shard_map/ppermute | solution.py:50
  96.7 1.0 unpack2.6.refs_2_
  97.7 1.5 %collective-permute-done.28.refs_0_ = f32[2,2,32,896]{3,2,1,0:T(8,128)S(1)} collective-permute-done((f32[2,2,32,896]{3,2,1,0:T(8,128)S(1)}, f32[2,2,32,896]{3,2,1,0:T(8,128)S(1)}, u32[]{:S(2)}, u32[]{:S(2)}) %collective-permute-start.28) | collective-permute-done | bytes 458784 | tf_op jit(solution)/shard_map/ppermute | solution.py:50
  99.2 2.4 %collective-permute-done.30.refs_1_ = f32[2,2,32,896]{3,2,1,0:T(8,128)S(1)} collective-permute-done((f32[2,2,32,896]{3,2,1,0:T(8,128)S(1)}, f32[2,2,32,896]{3,2,1,0:T(8,128)S(1)}, u32[]{:S(2)}, u32[]{:S(2)}) %collective-permute-start.30) | collective-permute-done | bytes 458784 | tf_op jit(solution)/shard_map/ppermute | solution.py:50
  101.6 1.0 unpack2.7
  (28 shorter events, 0.1 us)
Async XLA Ops:
  0.6 2.0 %copy-start = (f32[1,32,28672]{2,1,0:T(8,128)S(1)}, f32[1,32,28672]{2,1,0:T(8,128)}, u32[]{:S(2)}) copy-start(f32[1,32,28672]{2,1,0:T(8,128)} %param.4) | copy-start | bytes 11010052
  3.1 3.3 %copy-start.1 = (f32[32,28672]{1,0:T(8,128)S(1)}, f32[32,28672]{1,0:T(8,128)}, u32[]{:S(2)}) copy-start(f32[32,28672]{1,0:T(8,128)} %refs_0_.1) | copy-start | bytes 11010052
  3.2 8.8 %collective-permute-start.1 = (f32[2,2,32,896]{3,2,1,0:T(8,128)S(1)}, f32[2,2,32,896]{3,2,1,0:T(8,128)S(1)}, u32[]{:S(2)}, u32[]{:S(2)}) collective-permute-start(f32[2,2,32,896]{3,2,1,0:T(8,128)S(1)} %get-tuple-element.33), channel_id=1, source_target_pairs={{0,32},{1,9},{2,34},{3,11},{4,36},{5,13},{6,38},{7,15},{8,40},{9,1... | collective-permute-start | bytes 1376264 | tf_op jit(solution)/shard_map/ppermute | solution.py:50
  4.7 8.7 %collective-permute-start.5 = (f32[2,2,32,896]{3,2,1,0:T(8,128)S(1)}, f32[2,2,32,896]{3,2,1,0:T(8,128)S(1)}, u32[]{:S(2)}, u32[]{:S(2)}) collective-permute-start(f32[2,2,32,896]{3,2,1,0:T(8,128)S(1)} %get-tuple-element.34), channel_id=1, source_target_pairs={{0,96},{1,25},{2,98},{3,27},{4,100},{5,29},{6,102},{7,31},{8,104},... | collective-permute-start | bytes 1376264 | tf_op jit(solution)/shard_map/ppermute | solution.py:50
  8.2 10.6 %copy-start.2 = (f32[32,896]{1,0:T(8,128)S(1)}, f32[32,896]{1,0:T(8,128)}, u32[]{:S(2)}) copy-start(f32[32,896]{1,0:T(8,128)} %param.5) | copy-start | bytes 344068
  12.1 15.6 %collective-permute-start.2 = (f32[2,2,32,896]{3,2,1,0:T(8,128)S(1)}, f32[2,2,32,896]{3,2,1,0:T(8,128)S(1)}, u32[]{:S(2)}, u32[]{:S(2)}) collective-permute-start(f32[2,2,32,896]{3,2,1,0:T(8,128)S(1)} %get-tuple-element.31), channel_id=1, source_target_pairs={{0,32},{1,9},{2,34},{3,11},{4,36},{5,13},{6,38},{7,15},{8,40},{9,1... | collective-permute-start | bytes 1376264 | tf_op jit(solution)/shard_map/ppermute | solution.py:50
  13.5 14.1 %collective-permute-start = (f32[2,2,32,896]{3,2,1,0:T(8,128)S(1)}, f32[2,2,32,896]{3,2,1,0:T(8,128)S(1)}, u32[]{:S(2)}, u32[]{:S(2)}) collective-permute-start(f32[2,2,32,896]{3,2,1,0:T(8,128)S(1)} %get-tuple-element.35), channel_id=1, source_target_pairs={{0,96},{1,25},{2,98},{3,27},{4,100},{5,29},{6,102},{7,31},{8,104},... | collective-permute-start | bytes 1376264 | tf_op jit(solution)/shard_map/ppermute | solution.py:50
  15.6 12.1 %collective-permute-start.6 = (f32[2,2,32,896]{3,2,1,0:T(8,128)S(1)}, f32[2,2,32,896]{3,2,1,0:T(8,128)S(1)}, u32[]{:S(2)}, u32[]{:S(2)}) collective-permute-start(f32[2,2,32,896]{3,2,1,0:T(8,128)S(1)} %get-tuple-element.36), channel_id=1, source_target_pairs={{0,96},{1,25},{2,98},{3,27},{4,100},{5,29},{6,102},{7,31},{8,104},... | collective-permute-start | bytes 1376264 | tf_op jit(solution)/shard_map/ppermute | solution.py:50
  18.8 8.9 %collective-permute-start.4 = (f32[2,2,32,896]{3,2,1,0:T(8,128)S(1)}, f32[2,2,32,896]{3,2,1,0:T(8,128)S(1)}, u32[]{:S(2)}, u32[]{:S(2)}) collective-permute-start(f32[2,2,32,896]{3,2,1,0:T(8,128)S(1)} %get-tuple-element.32), channel_id=1, source_target_pairs={{0,32},{1,9},{2,34},{3,11},{4,36},{5,13},{6,38},{7,15},{8,40},{9,1... | collective-permute-start | bytes 1376264 | tf_op jit(solution)/shard_map/ppermute | solution.py:50
  18.8 8.8 %collective-permute-start.3 = (f32[32,896]{1,0:T(8,128)S(1)}, f32[32,896]{1,0:T(8,128)S(1)}, u32[]{:S(2)}, u32[]{:S(2)}) collective-permute-start(f32[32,896]{1,0:T(8,128)S(1)} %copy-done.2), channel_id=1, source_target_pairs={{0,128},{1,129},{2,130},{3,131},{4,132},{5,133},{6,134},{7,135},{8... | collective-permute-start | bytes 344072 | tf_op jit(solution)/shard_map/ppermute | solution.py:50
  27.9 7.7 %collective-permute-start.7 = (f32[2,32,896]{2,1,0:T(8,128)S(1)}, f32[2,32,896]{2,1,0:T(8,128)S(1)}, u32[]{:S(2)}, u32[]{:S(2)}) collective-permute-start(f32[2,32,896]{2,1,0:T(8,128)S(1)} %get-tuple-element.28), channel_id=1, source_target_pairs={{0,16},{1,65},{2,18},{3,67},{4,20},{5,69},{6,22},{7,71},{8,24},{9,... | collective-permute-start | bytes 688136 | tf_op jit(solution)/shard_map/ppermute | solution.py:50
  31.6 7.2 %collective-permute-start.8 = (f32[2,32,896]{2,1,0:T(8,128)S(1)}, f32[2,32,896]{2,1,0:T(8,128)S(1)}, u32[]{:S(2)}, u32[]{:S(2)}) collective-permute-start(f32[2,32,896]{2,1,0:T(8,128)S(1)} %get-tuple-element.30), channel_id=1, source_target_pairs={{0,8},{1,33},{2,10},{3,35},{4,12},{5,37},{6,14},{7,39},{8,16},{9,4... | collective-permute-start | bytes 688136 | tf_op jit(solution)/shard_map/ppermute | solution.py:50
  31.6 7.2 %collective-permute-start.9 = (f32[2,32,896]{2,1,0:T(8,128)S(1)}, f32[2,32,896]{2,1,0:T(8,128)S(1)}, u32[]{:S(2)}, u32[]{:S(2)}) collective-permute-start(f32[2,32,896]{2,1,0:T(8,128)S(1)} %get-tuple-element.29), channel_id=1, source_target_pairs={{0,24},{1,97},{2,26},{3,99},{4,28},{5,101},{6,30},{7,103},{8,0},{9... | collective-permute-start | bytes 688136 | tf_op jit(solution)/shard_map/ppermute | solution.py:50
  38.9 13.6 %collective-permute-start.10 = (f32[2,32,896]{2,1,0:T(8,128)S(1)}, f32[2,32,896]{2,1,0:T(8,128)S(1)}, u32[]{:S(2)}, u32[]{:S(2)}) collective-permute-start(f32[2,32,896]{2,1,0:T(8,128)S(1)} %fusion.12), channel_id=1, source_target_pairs={{0,128},{1,129},{2,130},{3,131},{4,132},{5,133},{6,134},{7,135},{8... | collective-permute-start | bytes 688136 | tf_op jit(solution)/shard_map/ppermute | solution.py:50
  45.1 9.2 %collective-permute-start.12 = (f32[2,32,896]{2,1,0:T(8,128)S(1)}, f32[2,32,896]{2,1,0:T(8,128)S(1)}, u32[]{:S(2)}, u32[]{:S(2)}) collective-permute-start(f32[2,32,896]{2,1,0:T(8,128)S(1)} %pad_maximum_fusion.refs_9_), channel_id=1, source_target_pairs={{0,24},{1,97},{2,26},{3,99},{4,28},{5,101},{6,30},{7,103},{8,0},{9... | collective-permute-start | bytes 688136 | tf_op jit(solution)/shard_map/ppermute | solution.py:50
  48.3 7.6 %collective-permute-start.13 = (f32[2,32,896]{2,1,0:T(8,128)S(1)}, f32[2,32,896]{2,1,0:T(8,128)S(1)}, u32[]{:S(2)}, u32[]{:S(2)}) collective-permute-start(f32[2,32,896]{2,1,0:T(8,128)S(1)} %pad_maximum_fusion.refs_9_), channel_id=1, source_target_pairs={{0,16},{1,65},{2,18},{3,67},{4,20},{5,69},{6,22},{7,71},{8,24},{9,... | collective-permute-start | bytes 688136 | tf_op jit(solution)/shard_map/ppermute | solution.py:50
  48.4 9.7 %collective-permute-start.14 = (f32[2,32,896]{2,1,0:T(8,128)S(1)}, f32[2,32,896]{2,1,0:T(8,128)S(1)}, u32[]{:S(2)}, u32[]{:S(2)}) collective-permute-start(f32[2,32,896]{2,1,0:T(8,128)S(1)} %pad_maximum_fusion.refs_9_), channel_id=1, source_target_pairs={{0,8},{1,33},{2,10},{3,35},{4,12},{5,37},{6,14},{7,39},{8,16},{9,4... | collective-permute-start | bytes 688136 | tf_op jit(solution)/shard_map/ppermute | solution.py:50
  52.6 1.2 %collective-permute-start.11 = (f32[8,128]{1,0:T(8,128)S(1)}, f32[8,128]{1,0:T(8,128)S(1)}, u32[]{:S(2)}, u32[]{:S(2)}) collective-permute-start(f32[8,128]{1,0:T(8,128)S(1)} %squares.1), channel_id=1, source_target_pairs={{0,1},{1,0},{2,3},{3,2},{4,5},{5,4},{6,7},{7,6},{8,9},{9,8},{10,11... | collective-permute-start | bytes 12296 | tf_op jit(solution)/shard_map/ppermute | solution.py:50
  58.1 5.4 %collective-permute-start.15 = (f32[8,128]{1,0:T(8,128)S(1)}, f32[8,128]{1,0:T(8,128)S(1)}, u32[]{:S(2)}, u32[]{:S(2)}) collective-permute-start(f32[8,128]{1,0:T(8,128)S(1)} %add.97), channel_id=1, source_target_pairs={{0,2},{1,3},{2,4},{3,5},{4,6},{5,7},{6,0},{7,1},{8,10},{9,11},{10,... | collective-permute-start | bytes 12296 | tf_op jit(solution)/shard_map/ppermute | solution.py:50
  59.2 4.5 %collective-permute-start.16 = (f32[8,128]{1,0:T(8,128)S(1)}, f32[8,128]{1,0:T(8,128)S(1)}, u32[]{:S(2)}, u32[]{:S(2)}) collective-permute-start(f32[8,128]{1,0:T(8,128)S(1)} %add.97), channel_id=1, source_target_pairs={{0,4},{1,5},{2,6},{3,7},{4,0},{5,1},{6,2},{7,3},{8,12},{9,13},{10,... | collective-permute-start | bytes 12296 | tf_op jit(solution)/shard_map/ppermute | solution.py:50
  60.6 3.6 %collective-permute-start.17 = (f32[8,128]{1,0:T(8,128)S(1)}, f32[8,128]{1,0:T(8,128)S(1)}, u32[]{:S(2)}, u32[]{:S(2)}) collective-permute-start(f32[8,128]{1,0:T(8,128)S(1)} %add.97), channel_id=1, source_target_pairs={{0,6},{1,7},{2,0},{3,1},{4,2},{5,3},{6,4},{7,5},{8,14},{9,15},{10,... | collective-permute-start | bytes 12296 | tf_op jit(solution)/shard_map/ppermute | solution.py:50
  64.2 6.3 %collective-permute-start.18 = (f32[8,128]{1,0:T(8,128)S(1)}, f32[8,128]{1,0:T(8,128)S(1)}, u32[]{:S(2)}, u32[]{:S(2)}) collective-permute-start(f32[8,128]{1,0:T(8,128)S(1)} %add_add_fusion.1), channel_id=1, source_target_pairs={{0,8},{1,33},{2,10},{3,35},{4,12},{5,37},{6,14},{7,39},{8,16},{9,4... | collective-permute-start | bytes 12296 | tf_op jit(solution)/shard_map/ppermute | solution.py:50
  64.2 7.6 %collective-permute-start.19 = (f32[8,128]{1,0:T(8,128)S(1)}, f32[8,128]{1,0:T(8,128)S(1)}, u32[]{:S(2)}, u32[]{:S(2)}) collective-permute-start(f32[8,128]{1,0:T(8,128)S(1)} %add_add_fusion.1), channel_id=1, source_target_pairs={{0,16},{1,65},{2,18},{3,67},{4,20},{5,69},{6,22},{7,71},{8,24},{9,... | collective-permute-start | bytes 12296 | tf_op jit(solution)/shard_map/ppermute | solution.py:50
  66.4 5.4 %collective-permute-start.20 = (f32[8,128]{1,0:T(8,128)S(1)}, f32[8,128]{1,0:T(8,128)S(1)}, u32[]{:S(2)}, u32[]{:S(2)}) collective-permute-start(f32[8,128]{1,0:T(8,128)S(1)} %add_add_fusion.1), channel_id=1, source_target_pairs={{0,24},{1,97},{2,26},{3,99},{4,28},{5,101},{6,30},{7,103},{8,0},{9... | collective-permute-start | bytes 12296 | tf_op jit(solution)/shard_map/ppermute | solution.py:50
  67.4 12.3 %collective-permute-start.24 = (f32[2,32,896]{2,1,0:T(8,128)S(1)}, f32[2,32,896]{2,1,0:T(8,128)S(1)}, u32[]{:S(2)}, u32[]{:S(2)}) collective-permute-start(f32[2,32,896]{2,1,0:T(8,128)S(1)} %fusion.13.value.refs_5_), channel_id=1, source_target_pairs={{0,24},{1,97},{2,26},{3,99},{4,28},{5,101},{6,30},{7,103},{8,0},{9... | collective-permute-start | bytes 688136 | tf_op jit(solution)/shard_map/ppermute | solution.py:50
  68.4 11.3 %collective-permute-start.25 = (f32[2,32,896]{2,1,0:T(8,128)S(1)}, f32[2,32,896]{2,1,0:T(8,128)S(1)}, u32[]{:S(2)}, u32[]{:S(2)}) collective-permute-start(f32[2,32,896]{2,1,0:T(8,128)S(1)} %fusion.13.value.refs_5_), channel_id=1, source_target_pairs={{0,16},{1,65},{2,18},{3,67},{4,20},{5,69},{6,22},{7,71},{8,24},{9,... | collective-permute-start | bytes 688136 | tf_op jit(solution)/shard_map/ppermute | solution.py:50
  70.5 9.2 %collective-permute-start.26 = (f32[2,32,896]{2,1,0:T(8,128)S(1)}, f32[2,32,896]{2,1,0:T(8,128)S(1)}, u32[]{:S(2)}, u32[]{:S(2)}) collective-permute-start(f32[2,32,896]{2,1,0:T(8,128)S(1)} %fusion.13.value.refs_5_), channel_id=1, source_target_pairs={{0,8},{1,33},{2,10},{3,35},{4,12},{5,37},{6,14},{7,39},{8,16},{9,4... | collective-permute-start | bytes 688136 | tf_op jit(solution)/shard_map/ppermute | solution.py:50
  71.8 3.8 %collective-permute-start.21 = (f32[8,128]{1,0:T(8,128)S(1)}, f32[8,128]{1,0:T(8,128)S(1)}, u32[]{:S(2)}, u32[]{:S(2)}) collective-permute-start(f32[8,128]{1,0:T(8,128)S(1)} %add_add_fusion.refs_0_), channel_id=1, source_target_pairs={{0,32},{1,9},{2,34},{3,11},{4,36},{5,13},{6,38},{7,15},{8,40},{9,1... | collective-permute-start | bytes 12296 | tf_op jit(solution)/shard_map/ppermute | solution.py:50
  73.1 5.3 %collective-permute-start.22 = (f32[8,128]{1,0:T(8,128)S(1)}, f32[8,128]{1,0:T(8,128)S(1)}, u32[]{:S(2)}, u32[]{:S(2)}) collective-permute-start(f32[8,128]{1,0:T(8,128)S(1)} %add_add_fusion.refs_0_), channel_id=1, source_target_pairs={{0,64},{1,17},{2,66},{3,19},{4,68},{5,21},{6,70},{7,23},{8,72},{9,... | collective-permute-start | bytes 12296 | tf_op jit(solution)/shard_map/ppermute | solution.py:50
  75.6 4.1 %collective-permute-start.23 = (f32[8,128]{1,0:T(8,128)S(1)}, f32[8,128]{1,0:T(8,128)S(1)}, u32[]{:S(2)}, u32[]{:S(2)}) collective-permute-start(f32[8,128]{1,0:T(8,128)S(1)} %add_add_fusion.refs_0_), channel_id=1, source_target_pairs={{0,96},{1,25},{2,98},{3,27},{4,100},{5,29},{6,102},{7,31},{8,104},... | collective-permute-start | bytes 12296 | tf_op jit(solution)/shard_map/ppermute | solution.py:50
  80.6 8.7 %collective-permute-start.27 = (f32[2,2,32,896]{3,2,1,0:T(8,128)S(1)}, f32[2,2,32,896]{3,2,1,0:T(8,128)S(1)}, u32[]{:S(2)}, u32[]{:S(2)}) collective-permute-start(f32[2,2,32,896]{3,2,1,0:T(8,128)S(1)} %get-tuple-element.25.refs_0_), channel_id=1, source_target_pairs={{0,32},{1,9},{2,34},{3,11},{4,36},{5,13},{6,38},{7,15},{8,40},{9,1... | collective-permute-start | bytes 1376264 | tf_op jit(solution)/shard_map/ppermute | solution.py:50
  82.1 9.7 %collective-permute-start.29 = (f32[2,2,32,896]{3,2,1,0:T(8,128)S(1)}, f32[2,2,32,896]{3,2,1,0:T(8,128)S(1)}, u32[]{:S(2)}, u32[]{:S(2)}) collective-permute-start(f32[2,2,32,896]{3,2,1,0:T(8,128)S(1)} %get-tuple-element.26.refs_1_), channel_id=1, source_target_pairs={{0,96},{1,25},{2,98},{3,27},{4,100},{5,29},{6,102},{7,31},{8,104},... | collective-permute-start | bytes 1376264 | tf_op jit(solution)/shard_map/ppermute | solution.py:50
  82.9 11.7 %collective-permute-start.31 = (f32[2,2,32,896]{3,2,1,0:T(8,128)S(1)}, f32[2,2,32,896]{3,2,1,0:T(8,128)S(1)}, u32[]{:S(2)}, u32[]{:S(2)}) collective-permute-start(f32[2,2,32,896]{3,2,1,0:T(8,128)S(1)} %get-tuple-element.26.refs_1_), channel_id=1, source_target_pairs={{0,32},{1,9},{2,34},{3,11},{4,36},{5,13},{6,38},{7,15},{8,40},{9,1... | collective-permute-start | bytes 1376264 | tf_op jit(solution)/shard_map/ppermute | solution.py:50
  85.3 11.4 %collective-permute-start.32 = (f32[2,2,32,896]{3,2,1,0:T(8,128)S(1)}, f32[2,2,32,896]{3,2,1,0:T(8,128)S(1)}, u32[]{:S(2)}, u32[]{:S(2)}) collective-permute-start(f32[2,2,32,896]{3,2,1,0:T(8,128)S(1)} %get-tuple-element.25.refs_0_), channel_id=1, source_target_pairs={{0,96},{1,25},{2,98},{3,27},{4,100},{5,29},{6,102},{7,31},{8,104},... | collective-permute-start | bytes 1376264 | tf_op jit(solution)/shard_map/ppermute | solution.py:50
  89.3 9.8 %collective-permute-start.28 = (f32[2,2,32,896]{3,2,1,0:T(8,128)S(1)}, f32[2,2,32,896]{3,2,1,0:T(8,128)S(1)}, u32[]{:S(2)}, u32[]{:S(2)}) collective-permute-start(f32[2,2,32,896]{3,2,1,0:T(8,128)S(1)} %collective-permute-done.27.refs_0_), channel_id=1, source_target_pairs={{0,32},{1,9},{2,34},{3,11},{4,36},{5,13},{6,38},{7,15},{8,40},{9,1... | collective-permute-start | bytes 1376264 | tf_op jit(solution)/shard_map/ppermute | solution.py:50
  91.8 9.8 %collective-permute-start.30 = (f32[2,2,32,896]{3,2,1,0:T(8,128)S(1)}, f32[2,2,32,896]{3,2,1,0:T(8,128)S(1)}, u32[]{:S(2)}, u32[]{:S(2)}) collective-permute-start(f32[2,2,32,896]{3,2,1,0:T(8,128)S(1)} %collective-permute-done.29.refs_1_), channel_id=1, source_target_pairs={{0,96},{1,25},{2,98},{3,27},{4,100},{5,29},{6,102},{7,31},{8,104},... | collective-permute-start | bytes 1376264 | tf_op jit(solution)/shard_map/ppermute | solution.py:50

commit v5 on v4

--- a/solution.py
+++ b/solution.py
@@ -212,7 +212,7 @@
     shards = lax.axis_size("fsdp")
     rows, columns = global_weights.shape
     width = columns // islands
-    local = local_weights[0]
+    local = pltpu.with_memory_space_constraint(local_weights[0], pltpu.HBM)
 
     (far,) = pack((local,), ((0, 2),), width)
     right, left = pack((local,), ((0, 1), (0, 3)), width, (far,))

time: 104 us -> 103 us (level)
  Pallas kernels: 7.9 us -> 10.5 us
  local copies, waits for them, and re-layouts: 2.12 us -> 0.09 us
  waiting for transfers between devices: 32.6 us -> 30.9 us
    pallas_call x3, Pallas kernels: 3 us -> 5.64 us  [pack(): pl.pallas_call(functools.partial(pack_kernel, jobs, width), out_shape=[ja...]
    unnamed x6 -> x4, local copies, waits for them, and re-layouts: 2.04 us -> 0.01 us
    ppermute x33, waiting for transfers between devices: 32.6 us -> 30.9 us  [send(): return lax.ppermute(value, AXES, route)]
  transfers between devices with their start and end apart: 33 -> 33, of which waited for: 18 -> 18; matrix products, arithmetic and copies ran while one was open for 0% -> 0% of each run, Pallas kernels for 5% -> 7%
where the time goes in v5:
time: 103 us; the launch traced here: 102 us
  starting transfers between devices  58.6 us (57%)
  waiting for transfers between devices  30.9 us (30%)
  Pallas kernels  10.5 us (10%)
    ppermute x33, starting transfers between devices, send(): return lax.ppermute(value, AXES, route)  58.6 us
    ppermute x33, waiting for transfers between devices, send(): return lax.ppermute(value, AXES, route)  30.9 us
    pallas_call x3, Pallas kernels, pack(): pl.pallas_call(functools.partial(pack_kernel, jobs, width), out_shape=[ja...  5.64 us
    pallas_call x4, Pallas kernels, unpack(): pl.pallas_call(functools.partial(unpack_kernel, groups, width), out_shape...  3.94 us
  transfers between devices with their start and end apart: 33, of which 18 were waited for; matrix products, arithmetic and copies ran while one was open for 0% of the time, Pallas kernels for 7%

profile of v5, /device:TPU:2, one launch (start us, length us, event | category | flops | bytes accessed | tf_op | source)
XLA Modules:
  0.0 101.6 jit_solution(4397293000572632926)
XLA Ops:
  0.6 1.4 %pack1.1.refs_1_ = f32[4,2,32,896]{3,2,1,0:T(8,128)S(1)} custom-call(f32[32,28672]{1,0:T(8,128)} %bitcast.17), custom_call_target="tpu_custom_call" | custom-call | bytes 1835008 | tf_op jit(solution)/shard_map/pack1/pallas_call | solution.py:93
  2.0 0.0 copy-start
  2.0 0.1 fusion.14
  2.1 1.6 %collective-permute-start.1 = (f32[2,2,32,896]{3,2,1,0:T(8,128)S(1)}, f32[2,2,32,896]{3,2,1,0:T(8,128)S(1)}, u32[]{:S(2)}, u32[]{:S(2)}) collective-permute-start(f32[2,2,32,896]{3,2,1,0:T(8,128)S(1)} %get-tuple-element.33), channel_id=1, source_target_pairs={{0,32},{1,9},{2,34},{3,11},{4,36},{5,13},{6,38},{7,15},{8,40},{9,1... | collective-permute-start | bytes 1376264 | tf_op jit(solution)/shard_map/ppermute | solution.py:50
  3.6 0.9 collective-permute-start.5
  4.5 1.7 %pack2.1 = (f32[4,2,32,896]{3,2,1,0:T(8,128)S(1)}, f32[4,2,32,896]{3,2,1,0:T(8,128)S(1)}) custom-call(f32[32,28672]{1,0:T(8,128)} %bitcast.18, f32[4,2,32,896]{3,2,1,0:T(8,128)S(1)} %pack1.1.refs_1_), custom_call_target="tpu_custom_call" | custom-call | bytes 3670016 | tf_op jit(solution)/shard_map/pack2/pallas_call | solution.py:93
  6.2 2.6 %pack4.1 = (f32[4,2,32,896]{3,2,1,0:T(8,128)S(1)}, f32[4,2,32,896]{3,2,1,0:T(8,128)S(1)}, f32[4,2,32,896]{3,2,1,0:T(8,128)S(1)}, f32[4,2,32,896]{3,2,1,0:T(8,128)S(1)}) custom-call(f32[32,28672]{1,0:T(8,128)S(1)} %copy-done, f32[32,28672]{1,0:T(8,128)} %bitcast.19, f32[4,2,32,896]{3,2,1,0:T(8,128)S(1)} %get-tuple-element.15.refs_2_), custom_call_target="tpu_custom_call" | custom-call | bytes 7340032 | tf_op jit(solution)/shard_map/pack4/pallas_call | solution.py:93
  8.8 2.0 %collective-permute-done.1 = f32[2,2,32,896]{3,2,1,0:T(8,128)S(1)} collective-permute-done((f32[2,2,32,896]{3,2,1,0:T(8,128)S(1)}, f32[2,2,32,896]{3,2,1,0:T(8,128)S(1)}, u32[]{:S(2)}, u32[]{:S(2)}) %collective-permute-start.1) | collective-permute-done | bytes 458784 | tf_op jit(solution)/shard_map/ppermute | solution.py:50
  10.9 0.1 subtract_add_fusion.1
  11.0 1.3 %collective-permute-start.2 = (f32[2,2,32,896]{3,2,1,0:T(8,128)S(1)}, f32[2,2,32,896]{3,2,1,0:T(8,128)S(1)}, u32[]{:S(2)}, u32[]{:S(2)}) collective-permute-start(f32[2,2,32,896]{3,2,1,0:T(8,128)S(1)} %get-tuple-element.31), channel_id=1, source_target_pairs={{0,32},{1,9},{2,34},{3,11},{4,36},{5,13},{6,38},{7,15},{8,40},{9,1... | collective-permute-start | bytes 1376264 | tf_op jit(solution)/shard_map/ppermute | solution.py:50
  12.3 0.1 fusion.15
  12.4 2.1 %collective-permute-start = (f32[2,2,32,896]{3,2,1,0:T(8,128)S(1)}, f32[2,2,32,896]{3,2,1,0:T(8,128)S(1)}, u32[]{:S(2)}, u32[]{:S(2)}) collective-permute-start(f32[2,2,32,896]{3,2,1,0:T(8,128)S(1)} %get-tuple-element.35), channel_id=1, source_target_pairs={{0,96},{1,25},{2,98},{3,27},{4,100},{5,29},{6,102},{7,31},{8,104},... | collective-permute-start | bytes 1376264 | tf_op jit(solution)/shard_map/ppermute | solution.py:50
  14.5 3.2 %collective-permute-start.6 = (f32[2,2,32,896]{3,2,1,0:T(8,128)S(1)}, f32[2,2,32,896]{3,2,1,0:T(8,128)S(1)}, u32[]{:S(2)}, u32[]{:S(2)}) collective-permute-start(f32[2,2,32,896]{3,2,1,0:T(8,128)S(1)} %get-tuple-element.36), channel_id=1, source_target_pairs={{0,96},{1,25},{2,98},{3,27},{4,100},{5,29},{6,102},{7,31},{8,104},... | collective-permute-start | bytes 1376264 | tf_op jit(solution)/shard_map/ppermute | solution.py:50
  17.7 5.5 %collective-permute-start.3 = (f32[32,896]{1,0:T(8,128)S(1)}, f32[32,896]{1,0:T(8,128)S(1)}, u32[]{:S(2)}, u32[]{:S(2)}) collective-permute-start(f32[32,896]{1,0:T(8,128)S(1)} %copy-done.1), channel_id=1, source_target_pairs={{0,128},{1,129},{2,130},{3,131},{4,132},{5,133},{6,134},{7,135},{8... | collective-permute-start | bytes 344072 | tf_op jit(solution)/shard_map/ppermute | solution.py:50
  23.2 3.3 %collective-permute-done.3 = f32[32,896]{1,0:T(8,128)S(1)} collective-permute-done((f32[32,896]{1,0:T(8,128)S(1)}, f32[32,896]{1,0:T(8,128)S(1)}, u32[]{:S(2)}, u32[]{:S(2)}) %collective-permute-start.3) | collective-permute-done | bytes 114720 | tf_op jit(solution)/shard_map/ppermute | solution.py:50
  26.6 0.2 fusion.5
  26.8 3.7 %collective-permute-start.7 = (f32[2,32,896]{2,1,0:T(8,128)S(1)}, f32[2,32,896]{2,1,0:T(8,128)S(1)}, u32[]{:S(2)}, u32[]{:S(2)}) collective-permute-start(f32[2,32,896]{2,1,0:T(8,128)S(1)} %get-tuple-element.28), channel_id=1, source_target_pairs={{0,16},{1,65},{2,18},{3,67},{4,20},{5,69},{6,22},{7,71},{8,24},{9,... | collective-permute-start | bytes 688136 | tf_op jit(solution)/shard_map/ppermute | solution.py:50
  30.5 0.0 collective-permute-start.8
  30.5 3.2 %collective-permute-start.9 = (f32[2,32,896]{2,1,0:T(8,128)S(1)}, f32[2,32,896]{2,1,0:T(8,128)S(1)}, u32[]{:S(2)}, u32[]{:S(2)}) collective-permute-start(f32[2,32,896]{2,1,0:T(8,128)S(1)} %get-tuple-element.29), channel_id=1, source_target_pairs={{0,24},{1,97},{2,26},{3,99},{4,28},{5,101},{6,30},{7,103},{8,0},{9... | collective-permute-start | bytes 688136 | tf_op jit(solution)/shard_map/ppermute | solution.py:50
  33.7 0.8 collective-permute-done.7
  34.5 3.2 %collective-permute-done.8 = f32[2,32,896]{2,1,0:T(8,128)S(1)} collective-permute-done((f32[2,32,896]{2,1,0:T(8,128)S(1)}, f32[2,32,896]{2,1,0:T(8,128)S(1)}, u32[]{:S(2)}, u32[]{:S(2)}) %collective-permute-start.8) | collective-permute-done | bytes 229408 | tf_op jit(solution)/shard_map/ppermute | solution.py:50
  37.7 0.1 fusion.12
  37.8 6.2 %collective-permute-start.10 = (f32[2,32,896]{2,1,0:T(8,128)S(1)}, f32[2,32,896]{2,1,0:T(8,128)S(1)}, u32[]{:S(2)}, u32[]{:S(2)}) collective-permute-start(f32[2,32,896]{2,1,0:T(8,128)S(1)} %fusion.12), channel_id=1, source_target_pairs={{0,128},{1,129},{2,130},{3,131},{4,132},{5,133},{6,134},{7,135},{8... | collective-permute-start | bytes 688136 | tf_op jit(solution)/shard_map/ppermute | solution.py:50
  43.9 3.2 %collective-permute-start.12 = (f32[2,32,896]{2,1,0:T(8,128)S(1)}, f32[2,32,896]{2,1,0:T(8,128)S(1)}, u32[]{:S(2)}, u32[]{:S(2)}) collective-permute-start(f32[2,32,896]{2,1,0:T(8,128)S(1)} %pad_maximum_fusion.refs_9_), channel_id=1, source_target_pairs={{0,24},{1,97},{2,26},{3,99},{4,28},{5,101},{6,30},{7,103},{8,0},{9... | collective-permute-start | bytes 688136 | tf_op jit(solution)/shard_map/ppermute | solution.py:50
  47.2 0.1 collective-permute-start.13
  47.3 0.7 collective-permute-start.14
  48.0 3.3 %collective-permute-done.10 = f32[2,32,896]{2,1,0:T(8,128)S(1)} collective-permute-done((f32[2,32,896]{2,1,0:T(8,128)S(1)}, f32[2,32,896]{2,1,0:T(8,128)S(1)}, u32[]{:S(2)}, u32[]{:S(2)}) %collective-permute-start.10) | collective-permute-done | bytes 229408 | tf_op jit(solution)/shard_map/ppermute | solution.py:50
  51.4 0.1 squares.1
  51.5 0.1 collective-permute-start.11
  51.6 1.2 %collective-permute-done.11 = f32[8,128]{1,0:T(8,128)S(1)} collective-permute-done((f32[8,128]{1,0:T(8,128)S(1)}, f32[8,128]{1,0:T(8,128)S(1)}, u32[]{:S(2)}, u32[]{:S(2)}) %collective-permute-start.11) | collective-permute-done | bytes 4128 | tf_op jit(solution)/shard_map/ppermute | solution.py:50
  52.7 0.4 collective-permute-done.12.refs_10_
  53.2 1.6 %collective-permute-done.13.refs_11_ = f32[2,32,896]{2,1,0:T(8,128)S(1)} collective-permute-done((f32[2,32,896]{2,1,0:T(8,128)S(1)}, f32[2,32,896]{2,1,0:T(8,128)S(1)}, u32[]{:S(2)}, u32[]{:S(2)}) %collective-permute-start.13) | collective-permute-done | bytes 229408 | tf_op jit(solution)/shard_map/ppermute | solution.py:50
  54.8 2.2 %collective-permute-done.14.refs_12_ = f32[2,32,896]{2,1,0:T(8,128)S(1)} collective-permute-done((f32[2,32,896]{2,1,0:T(8,128)S(1)}, f32[2,32,896]{2,1,0:T(8,128)S(1)}, u32[]{:S(2)}, u32[]{:S(2)}) %collective-permute-start.14) | collective-permute-done | bytes 229408 | tf_op jit(solution)/shard_map/ppermute | solution.py:50
  57.0 1.1 %collective-permute-start.15 = (f32[8,128]{1,0:T(8,128)S(1)}, f32[8,128]{1,0:T(8,128)S(1)}, u32[]{:S(2)}, u32[]{:S(2)}) collective-permute-start(f32[8,128]{1,0:T(8,128)S(1)} %add.97), channel_id=1, source_target_pairs={{0,2},{1,3},{2,4},{3,5},{4,6},{5,7},{6,0},{7,1},{8,10},{9,11},{10,... | collective-permute-start | bytes 12296 | tf_op jit(solution)/shard_map/ppermute | solution.py:50
  58.1 1.4 %collective-permute-start.16 = (f32[8,128]{1,0:T(8,128)S(1)}, f32[8,128]{1,0:T(8,128)S(1)}, u32[]{:S(2)}, u32[]{:S(2)}) collective-permute-start(f32[8,128]{1,0:T(8,128)S(1)} %add.97), channel_id=1, source_target_pairs={{0,4},{1,5},{2,6},{3,7},{4,0},{5,1},{6,2},{7,3},{8,12},{9,13},{10,... | collective-permute-start | bytes 12296 | tf_op jit(solution)/shard_map/ppermute | solution.py:50
  59.5 1.9 %collective-permute-start.17 = (f32[8,128]{1,0:T(8,128)S(1)}, f32[8,128]{1,0:T(8,128)S(1)}, u32[]{:S(2)}, u32[]{:S(2)}) collective-permute-start(f32[8,128]{1,0:T(8,128)S(1)} %add.97), channel_id=1, source_target_pairs={{0,6},{1,7},{2,0},{3,1},{4,2},{5,3},{6,4},{7,5},{8,14},{9,15},{10,... | collective-permute-start | bytes 12296 | tf_op jit(solution)/shard_map/ppermute | solution.py:50
  61.4 1.0 collective-permute-done.15
  62.4 0.2 collective-permute-done.16
  62.6 0.5 collective-permute-done.17
  63.1 2.2 %collective-permute-start.19 = (f32[8,128]{1,0:T(8,128)S(1)}, f32[8,128]{1,0:T(8,128)S(1)}, u32[]{:S(2)}, u32[]{:S(2)}) collective-permute-start(f32[8,128]{1,0:T(8,128)S(1)} %add_add_fusion.1), channel_id=1, source_target_pairs={{0,16},{1,65},{2,18},{3,67},{4,20},{5,69},{6,22},{7,71},{8,24},{9,... | collective-permute-start | bytes 12296 | tf_op jit(solution)/shard_map/ppermute | solution.py:50
  65.3 1.0 collective-permute-start.20
  66.3 0.9 collective-permute-start.24
  67.3 2.1 %collective-permute-start.25 = (f32[2,32,896]{2,1,0:T(8,128)S(1)}, f32[2,32,896]{2,1,0:T(8,128)S(1)}, u32[]{:S(2)}, u32[]{:S(2)}) collective-permute-start(f32[2,32,896]{2,1,0:T(8,128)S(1)} %fusion.13.value.refs_5_), channel_id=1, source_target_pairs={{0,16},{1,65},{2,18},{3,67},{4,20},{5,69},{6,22},{7,71},{8,24},{9,... | collective-permute-start | bytes 688136 | tf_op jit(solution)/shard_map/ppermute | solution.py:50
  69.4 1.2 %collective-permute-start.26 = (f32[2,32,896]{2,1,0:T(8,128)S(1)}, f32[2,32,896]{2,1,0:T(8,128)S(1)}, u32[]{:S(2)}, u32[]{:S(2)}) collective-permute-start(f32[2,32,896]{2,1,0:T(8,128)S(1)} %fusion.13.value.refs_5_), channel_id=1, source_target_pairs={{0,8},{1,33},{2,10},{3,35},{4,12},{5,37},{6,14},{7,39},{8,16},{9,4... | collective-permute-start | bytes 688136 | tf_op jit(solution)/shard_map/ppermute | solution.py:50
  70.7 1.3 %collective-permute-start.21 = (f32[8,128]{1,0:T(8,128)S(1)}, f32[8,128]{1,0:T(8,128)S(1)}, u32[]{:S(2)}, u32[]{:S(2)}) collective-permute-start(f32[8,128]{1,0:T(8,128)S(1)} %add_add_fusion.refs_0_), channel_id=1, source_target_pairs={{0,32},{1,9},{2,34},{3,11},{4,36},{5,13},{6,38},{7,15},{8,40},{9,1... | collective-permute-start | bytes 12296 | tf_op jit(solution)/shard_map/ppermute | solution.py:50
  72.0 2.5 %collective-permute-start.22 = (f32[8,128]{1,0:T(8,128)S(1)}, f32[8,128]{1,0:T(8,128)S(1)}, u32[]{:S(2)}, u32[]{:S(2)}) collective-permute-start(f32[8,128]{1,0:T(8,128)S(1)} %add_add_fusion.refs_0_), channel_id=1, source_target_pairs={{0,64},{1,17},{2,66},{3,19},{4,68},{5,21},{6,70},{7,23},{8,72},{9,... | collective-permute-start | bytes 12296 | tf_op jit(solution)/shard_map/ppermute | solution.py:50
  74.5 2.7 %collective-permute-start.23 = (f32[8,128]{1,0:T(8,128)S(1)}, f32[8,128]{1,0:T(8,128)S(1)}, u32[]{:S(2)}, u32[]{:S(2)}) collective-permute-start(f32[8,128]{1,0:T(8,128)S(1)} %add_add_fusion.refs_0_), channel_id=1, source_target_pairs={{0,96},{1,25},{2,98},{3,27},{4,100},{5,29},{6,102},{7,31},{8,104},... | collective-permute-start | bytes 12296 | tf_op jit(solution)/shard_map/ppermute | solution.py:50
  77.3 1.3 %collective-permute-done.23.refs_3_ = f32[8,128]{1,0:T(8,128)S(1)} collective-permute-done((f32[8,128]{1,0:T(8,128)S(1)}, f32[8,128]{1,0:T(8,128)S(1)}, u32[]{:S(2)}, u32[]{:S(2)}) %collective-permute-start.23) | collective-permute-done | bytes 4128 | tf_op jit(solution)/shard_map/ppermute | solution.py:50
  78.6 0.9 update.1
  79.5 1.5 %collective-permute-start.27 = (f32[2,2,32,896]{3,2,1,0:T(8,128)S(1)}, f32[2,2,32,896]{3,2,1,0:T(8,128)S(1)}, u32[]{:S(2)}, u32[]{:S(2)}) collective-permute-start(f32[2,2,32,896]{3,2,1,0:T(8,128)S(1)} %get-tuple-element.25.refs_0_), channel_id=1, source_target_pairs={{0,32},{1,9},{2,34},{3,11},{4,36},{5,13},{6,38},{7,15},{8,40},{9,1... | collective-permute-start | bytes 1376264 | tf_op jit(solution)/shard_map/ppermute | solution.py:50
  81.0 0.8 collective-permute-start.29
  81.8 2.4 %collective-permute-start.31 = (f32[2,2,32,896]{3,2,1,0:T(8,128)S(1)}, f32[2,2,32,896]{3,2,1,0:T(8,128)S(1)}, u32[]{:S(2)}, u32[]{:S(2)}) collective-permute-start(f32[2,2,32,896]{3,2,1,0:T(8,128)S(1)} %get-tuple-element.26.refs_1_), channel_id=1, source_target_pairs={{0,32},{1,9},{2,34},{3,11},{4,36},{5,13},{6,38},{7,15},{8,40},{9,1... | collective-permute-start | bytes 1376264 | tf_op jit(solution)/shard_map/ppermute | solution.py:50
  84.2 0.8 collective-permute-start.32
  85.0 3.2 %collective-permute-done.27.refs_0_ = f32[2,2,32,896]{3,2,1,0:T(8,128)S(1)} collective-permute-done((f32[2,2,32,896]{3,2,1,0:T(8,128)S(1)}, f32[2,2,32,896]{3,2,1,0:T(8,128)S(1)}, u32[]{:S(2)}, u32[]{:S(2)}) %collective-permute-start.27) | collective-permute-done | bytes 458784 | tf_op jit(solution)/shard_map/ppermute | solution.py:50
  88.2 2.0 %collective-permute-start.28 = (f32[2,2,32,896]{3,2,1,0:T(8,128)S(1)}, f32[2,2,32,896]{3,2,1,0:T(8,128)S(1)}, u32[]{:S(2)}, u32[]{:S(2)}) collective-permute-start(f32[2,2,32,896]{3,2,1,0:T(8,128)S(1)} %collective-permute-done.27.refs_0_), channel_id=1, source_target_pairs={{0,32},{1,9},{2,34},{3,11},{4,36},{5,13},{6,38},{7,15},{8,40},{9,1... | collective-permute-start | bytes 1376264 | tf_op jit(solution)/shard_map/ppermute | solution.py:50
  90.2 0.5 collective-permute-done.29.refs_1_
  90.7 0.8 collective-permute-start.30
  91.5 1.0 unpack2.4.refs_2_
  92.5 1.0 unpack2.5.refs_2_
  93.5 2.1 %collective-permute-done.32.refs_1_ = f32[2,2,32,896]{3,2,1,0:T(8,128)S(1)} collective-permute-done((f32[2,2,32,896]{3,2,1,0:T(8,128)S(1)}, f32[2,2,32,896]{3,2,1,0:T(8,128)S(1)}, u32[]{:S(2)}, u32[]{:S(2)}) %collective-permute-start.32) | collective-permute-done | bytes 458784 | tf_op jit(solution)/shard_map/ppermute | solution.py:50
  95.6 1.0 unpack2.6.refs_2_
  96.6 1.5 %collective-permute-done.28.refs_0_ = f32[2,2,32,896]{3,2,1,0:T(8,128)S(1)} collective-permute-done((f32[2,2,32,896]{3,2,1,0:T(8,128)S(1)}, f32[2,2,32,896]{3,2,1,0:T(8,128)S(1)}, u32[]{:S(2)}, u32[]{:S(2)}) %collective-permute-start.28) | collective-permute-done | bytes 458784 | tf_op jit(solution)/shard_map/ppermute | solution.py:50
  98.1 2.4 %collective-permute-done.30.refs_1_ = f32[2,2,32,896]{3,2,1,0:T(8,128)S(1)} collective-permute-done((f32[2,2,32,896]{3,2,1,0:T(8,128)S(1)}, f32[2,2,32,896]{3,2,1,0:T(8,128)S(1)}, u32[]{:S(2)}, u32[]{:S(2)}) %collective-permute-start.30) | collective-permute-done | bytes 458784 | tf_op jit(solution)/shard_map/ppermute | solution.py:50
  100.5 1.0 unpack2.7
  (26 shorter events, 0.1 us)
Async XLA Ops:
  2.0 4.2 %copy-start = (f32[32,28672]{1,0:T(8,128)S(1)}, f32[32,28672]{1,0:T(8,128)}, u32[]{:S(2)}) copy-start(f32[32,28672]{1,0:T(8,128)} %refs_0_.1) | copy-start | bytes 11010052
  2.1 8.8 %collective-permute-start.1 = (f32[2,2,32,896]{3,2,1,0:T(8,128)S(1)}, f32[2,2,32,896]{3,2,1,0:T(8,128)S(1)}, u32[]{:S(2)}, u32[]{:S(2)}) collective-permute-start(f32[2,2,32,896]{3,2,1,0:T(8,128)S(1)} %get-tuple-element.33), channel_id=1, source_target_pairs={{0,32},{1,9},{2,34},{3,11},{4,36},{5,13},{6,38},{7,15},{8,40},{9,1... | collective-permute-start | bytes 1376264 | tf_op jit(solution)/shard_map/ppermute | solution.py:50
  3.6 8.7 %collective-permute-start.5 = (f32[2,2,32,896]{3,2,1,0:T(8,128)S(1)}, f32[2,2,32,896]{3,2,1,0:T(8,128)S(1)}, u32[]{:S(2)}, u32[]{:S(2)}) collective-permute-start(f32[2,2,32,896]{3,2,1,0:T(8,128)S(1)} %get-tuple-element.34), channel_id=1, source_target_pairs={{0,96},{1,25},{2,98},{3,27},{4,100},{5,29},{6,102},{7,31},{8,104},... | collective-permute-start | bytes 1376264 | tf_op jit(solution)/shard_map/ppermute | solution.py:50
  8.8 8.9 %copy-start.1 = (f32[32,896]{1,0:T(8,128)S(1)}, f32[32,896]{1,0:T(8,128)}, u32[]{:S(2)}) copy-start(f32[32,896]{1,0:T(8,128)} %param.5) | copy-start | bytes 344068
  11.0 15.6 %collective-permute-start.2 = (f32[2,2,32,896]{3,2,1,0:T(8,128)S(1)}, f32[2,2,32,896]{3,2,1,0:T(8,128)S(1)}, u32[]{:S(2)}, u32[]{:S(2)}) collective-permute-start(f32[2,2,32,896]{3,2,1,0:T(8,128)S(1)} %get-tuple-element.31), channel_id=1, source_target_pairs={{0,32},{1,9},{2,34},{3,11},{4,36},{5,13},{6,38},{7,15},{8,40},{9,1... | collective-permute-start | bytes 1376264 | tf_op jit(solution)/shard_map/ppermute | solution.py:50
  12.4 14.1 %collective-permute-start = (f32[2,2,32,896]{3,2,1,0:T(8,128)S(1)}, f32[2,2,32,896]{3,2,1,0:T(8,128)S(1)}, u32[]{:S(2)}, u32[]{:S(2)}) collective-permute-start(f32[2,2,32,896]{3,2,1,0:T(8,128)S(1)} %get-tuple-element.35), channel_id=1, source_target_pairs={{0,96},{1,25},{2,98},{3,27},{4,100},{5,29},{6,102},{7,31},{8,104},... | collective-permute-start | bytes 1376264 | tf_op jit(solution)/shard_map/ppermute | solution.py:50
  14.5 12.1 %collective-permute-start.6 = (f32[2,2,32,896]{3,2,1,0:T(8,128)S(1)}, f32[2,2,32,896]{3,2,1,0:T(8,128)S(1)}, u32[]{:S(2)}, u32[]{:S(2)}) collective-permute-start(f32[2,2,32,896]{3,2,1,0:T(8,128)S(1)} %get-tuple-element.36), channel_id=1, source_target_pairs={{0,96},{1,25},{2,98},{3,27},{4,100},{5,29},{6,102},{7,31},{8,104},... | collective-permute-start | bytes 1376264 | tf_op jit(solution)/shard_map/ppermute | solution.py:50
  17.7 8.9 %collective-permute-start.4 = (f32[2,2,32,896]{3,2,1,0:T(8,128)S(1)}, f32[2,2,32,896]{3,2,1,0:T(8,128)S(1)}, u32[]{:S(2)}, u32[]{:S(2)}) collective-permute-start(f32[2,2,32,896]{3,2,1,0:T(8,128)S(1)} %get-tuple-element.32), channel_id=1, source_target_pairs={{0,32},{1,9},{2,34},{3,11},{4,36},{5,13},{6,38},{7,15},{8,40},{9,1... | collective-permute-start | bytes 1376264 | tf_op jit(solution)/shard_map/ppermute | solution.py:50
  17.7 8.8 %collective-permute-start.3 = (f32[32,896]{1,0:T(8,128)S(1)}, f32[32,896]{1,0:T(8,128)S(1)}, u32[]{:S(2)}, u32[]{:S(2)}) collective-permute-start(f32[32,896]{1,0:T(8,128)S(1)} %copy-done.1), channel_id=1, source_target_pairs={{0,128},{1,129},{2,130},{3,131},{4,132},{5,133},{6,134},{7,135},{8... | collective-permute-start | bytes 344072 | tf_op jit(solution)/shard_map/ppermute | solution.py:50
  26.8 7.7 %collective-permute-start.7 = (f32[2,32,896]{2,1,0:T(8,128)S(1)}, f32[2,32,896]{2,1,0:T(8,128)S(1)}, u32[]{:S(2)}, u32[]{:S(2)}) collective-permute-start(f32[2,32,896]{2,1,0:T(8,128)S(1)} %get-tuple-element.28), channel_id=1, source_target_pairs={{0,16},{1,65},{2,18},{3,67},{4,20},{5,69},{6,22},{7,71},{8,24},{9,... | collective-permute-start | bytes 688136 | tf_op jit(solution)/shard_map/ppermute | solution.py:50
  30.5 7.2 %collective-permute-start.8 = (f32[2,32,896]{2,1,0:T(8,128)S(1)}, f32[2,32,896]{2,1,0:T(8,128)S(1)}, u32[]{:S(2)}, u32[]{:S(2)}) collective-permute-start(f32[2,32,896]{2,1,0:T(8,128)S(1)} %get-tuple-element.30), channel_id=1, source_target_pairs={{0,8},{1,33},{2,10},{3,35},{4,12},{5,37},{6,14},{7,39},{8,16},{9,4... | collective-permute-start | bytes 688136 | tf_op jit(solution)/shard_map/ppermute | solution.py:50
  30.5 7.2 %collective-permute-start.9 = (f32[2,32,896]{2,1,0:T(8,128)S(1)}, f32[2,32,896]{2,1,0:T(8,128)S(1)}, u32[]{:S(2)}, u32[]{:S(2)}) collective-permute-start(f32[2,32,896]{2,1,0:T(8,128)S(1)} %get-tuple-element.29), channel_id=1, source_target_pairs={{0,24},{1,97},{2,26},{3,99},{4,28},{5,101},{6,30},{7,103},{8,0},{9... | collective-permute-start | bytes 688136 | tf_op jit(solution)/shard_map/ppermute | solution.py:50
  37.8 13.6 %collective-permute-start.10 = (f32[2,32,896]{2,1,0:T(8,128)S(1)}, f32[2,32,896]{2,1,0:T(8,128)S(1)}, u32[]{:S(2)}, u32[]{:S(2)}) collective-permute-start(f32[2,32,896]{2,1,0:T(8,128)S(1)} %fusion.12), channel_id=1, source_target_pairs={{0,128},{1,129},{2,130},{3,131},{4,132},{5,133},{6,134},{7,135},{8... | collective-permute-start | bytes 688136 | tf_op jit(solution)/shard_map/ppermute | solution.py:50
  43.9 9.2 %collective-permute-start.12 = (f32[2,32,896]{2,1,0:T(8,128)S(1)}, f32[2,32,896]{2,1,0:T(8,128)S(1)}, u32[]{:S(2)}, u32[]{:S(2)}) collective-permute-start(f32[2,32,896]{2,1,0:T(8,128)S(1)} %pad_maximum_fusion.refs_9_), channel_id=1, source_target_pairs={{0,24},{1,97},{2,26},{3,99},{4,28},{5,101},{6,30},{7,103},{8,0},{9... | collective-permute-start | bytes 688136 | tf_op jit(solution)/shard_map/ppermute | solution.py:50
  47.2 7.6 %collective-permute-start.13 = (f32[2,32,896]{2,1,0:T(8,128)S(1)}, f32[2,32,896]{2,1,0:T(8,128)S(1)}, u32[]{:S(2)}, u32[]{:S(2)}) collective-permute-start(f32[2,32,896]{2,1,0:T(8,128)S(1)} %pad_maximum_fusion.refs_9_), channel_id=1, source_target_pairs={{0,16},{1,65},{2,18},{3,67},{4,20},{5,69},{6,22},{7,71},{8,24},{9,... | collective-permute-start | bytes 688136 | tf_op jit(solution)/shard_map/ppermute | solution.py:50
  47.3 9.7 %collective-permute-start.14 = (f32[2,32,896]{2,1,0:T(8,128)S(1)}, f32[2,32,896]{2,1,0:T(8,128)S(1)}, u32[]{:S(2)}, u32[]{:S(2)}) collective-permute-start(f32[2,32,896]{2,1,0:T(8,128)S(1)} %pad_maximum_fusion.refs_9_), channel_id=1, source_target_pairs={{0,8},{1,33},{2,10},{3,35},{4,12},{5,37},{6,14},{7,39},{8,16},{9,4... | collective-permute-start | bytes 688136 | tf_op jit(solution)/shard_map/ppermute | solution.py:50
  51.5 1.2 %collective-permute-start.11 = (f32[8,128]{1,0:T(8,128)S(1)}, f32[8,128]{1,0:T(8,128)S(1)}, u32[]{:S(2)}, u32[]{:S(2)}) collective-permute-start(f32[8,128]{1,0:T(8,128)S(1)} %squares.1), channel_id=1, source_target_pairs={{0,1},{1,0},{2,3},{3,2},{4,5},{5,4},{6,7},{7,6},{8,9},{9,8},{10,11... | collective-permute-start | bytes 12296 | tf_op jit(solution)/shard_map/ppermute | solution.py:50
  57.0 5.4 %collective-permute-start.15 = (f32[8,128]{1,0:T(8,128)S(1)}, f32[8,128]{1,0:T(8,128)S(1)}, u32[]{:S(2)}, u32[]{:S(2)}) collective-permute-start(f32[8,128]{1,0:T(8,128)S(1)} %add.97), channel_id=1, source_target_pairs={{0,2},{1,3},{2,4},{3,5},{4,6},{5,7},{6,0},{7,1},{8,10},{9,11},{10,... | collective-permute-start | bytes 12296 | tf_op jit(solution)/shard_map/ppermute | solution.py:50
  58.1 4.5 %collective-permute-start.16 = (f32[8,128]{1,0:T(8,128)S(1)}, f32[8,128]{1,0:T(8,128)S(1)}, u32[]{:S(2)}, u32[]{:S(2)}) collective-permute-start(f32[8,128]{1,0:T(8,128)S(1)} %add.97), channel_id=1, source_target_pairs={{0,4},{1,5},{2,6},{3,7},{4,0},{5,1},{6,2},{7,3},{8,12},{9,13},{10,... | collective-permute-start | bytes 12296 | tf_op jit(solution)/shard_map/ppermute | solution.py:50
  59.5 3.6 %collective-permute-start.17 = (f32[8,128]{1,0:T(8,128)S(1)}, f32[8,128]{1,0:T(8,128)S(1)}, u32[]{:S(2)}, u32[]{:S(2)}) collective-permute-start(f32[8,128]{1,0:T(8,128)S(1)} %add.97), channel_id=1, source_target_pairs={{0,6},{1,7},{2,0},{3,1},{4,2},{5,3},{6,4},{7,5},{8,14},{9,15},{10,... | collective-permute-start | bytes 12296 | tf_op jit(solution)/shard_map/ppermute | solution.py:50
  63.1 6.3 %collective-permute-start.18 = (f32[8,128]{1,0:T(8,128)S(1)}, f32[8,128]{1,0:T(8,128)S(1)}, u32[]{:S(2)}, u32[]{:S(2)}) collective-permute-start(f32[8,128]{1,0:T(8,128)S(1)} %add_add_fusion.1), channel_id=1, source_target_pairs={{0,8},{1,33},{2,10},{3,35},{4,12},{5,37},{6,14},{7,39},{8,16},{9,4... | collective-permute-start | bytes 12296 | tf_op jit(solution)/shard_map/ppermute | solution.py:50
  63.1 7.6 %collective-permute-start.19 = (f32[8,128]{1,0:T(8,128)S(1)}, f32[8,128]{1,0:T(8,128)S(1)}, u32[]{:S(2)}, u32[]{:S(2)}) collective-permute-start(f32[8,128]{1,0:T(8,128)S(1)} %add_add_fusion.1), channel_id=1, source_target_pairs={{0,16},{1,65},{2,18},{3,67},{4,20},{5,69},{6,22},{7,71},{8,24},{9,... | collective-permute-start | bytes 12296 | tf_op jit(solution)/shard_map/ppermute | solution.py:50
  65.3 5.4 %collective-permute-start.20 = (f32[8,128]{1,0:T(8,128)S(1)}, f32[8,128]{1,0:T(8,128)S(1)}, u32[]{:S(2)}, u32[]{:S(2)}) collective-permute-start(f32[8,128]{1,0:T(8,128)S(1)} %add_add_fusion.1), channel_id=1, source_target_pairs={{0,24},{1,97},{2,26},{3,99},{4,28},{5,101},{6,30},{7,103},{8,0},{9... | collective-permute-start | bytes 12296 | tf_op jit(solution)/shard_map/ppermute | solution.py:50
  66.3 12.3 %collective-permute-start.24 = (f32[2,32,896]{2,1,0:T(8,128)S(1)}, f32[2,32,896]{2,1,0:T(8,128)S(1)}, u32[]{:S(2)}, u32[]{:S(2)}) collective-permute-start(f32[2,32,896]{2,1,0:T(8,128)S(1)} %fusion.13.value.refs_5_), channel_id=1, source_target_pairs={{0,24},{1,97},{2,26},{3,99},{4,28},{5,101},{6,30},{7,103},{8,0},{9... | collective-permute-start | bytes 688136 | tf_op jit(solution)/shard_map/ppermute | solution.py:50
  67.3 11.3 %collective-permute-start.25 = (f32[2,32,896]{2,1,0:T(8,128)S(1)}, f32[2,32,896]{2,1,0:T(8,128)S(1)}, u32[]{:S(2)}, u32[]{:S(2)}) collective-permute-start(f32[2,32,896]{2,1,0:T(8,128)S(1)} %fusion.13.value.refs_5_), channel_id=1, source_target_pairs={{0,16},{1,65},{2,18},{3,67},{4,20},{5,69},{6,22},{7,71},{8,24},{9,... | collective-permute-start | bytes 688136 | tf_op jit(solution)/shard_map/ppermute | solution.py:50
  69.4 9.2 %collective-permute-start.26 = (f32[2,32,896]{2,1,0:T(8,128)S(1)}, f32[2,32,896]{2,1,0:T(8,128)S(1)}, u32[]{:S(2)}, u32[]{:S(2)}) collective-permute-start(f32[2,32,896]{2,1,0:T(8,128)S(1)} %fusion.13.value.refs_5_), channel_id=1, source_target_pairs={{0,8},{1,33},{2,10},{3,35},{4,12},{5,37},{6,14},{7,39},{8,16},{9,4... | collective-permute-start | bytes 688136 | tf_op jit(solution)/shard_map/ppermute | solution.py:50
  70.7 3.8 %collective-permute-start.21 = (f32[8,128]{1,0:T(8,128)S(1)}, f32[8,128]{1,0:T(8,128)S(1)}, u32[]{:S(2)}, u32[]{:S(2)}) collective-permute-start(f32[8,128]{1,0:T(8,128)S(1)} %add_add_fusion.refs_0_), channel_id=1, source_target_pairs={{0,32},{1,9},{2,34},{3,11},{4,36},{5,13},{6,38},{7,15},{8,40},{9,1... | collective-permute-start | bytes 12296 | tf_op jit(solution)/shard_map/ppermute | solution.py:50
  72.0 5.3 %collective-permute-start.22 = (f32[8,128]{1,0:T(8,128)S(1)}, f32[8,128]{1,0:T(8,128)S(1)}, u32[]{:S(2)}, u32[]{:S(2)}) collective-permute-start(f32[8,128]{1,0:T(8,128)S(1)} %add_add_fusion.refs_0_), channel_id=1, source_target_pairs={{0,64},{1,17},{2,66},{3,19},{4,68},{5,21},{6,70},{7,23},{8,72},{9,... | collective-permute-start | bytes 12296 | tf_op jit(solution)/shard_map/ppermute | solution.py:50
  74.5 4.1 %collective-permute-start.23 = (f32[8,128]{1,0:T(8,128)S(1)}, f32[8,128]{1,0:T(8,128)S(1)}, u32[]{:S(2)}, u32[]{:S(2)}) collective-permute-start(f32[8,128]{1,0:T(8,128)S(1)} %add_add_fusion.refs_0_), channel_id=1, source_target_pairs={{0,96},{1,25},{2,98},{3,27},{4,100},{5,29},{6,102},{7,31},{8,104},... | collective-permute-start | bytes 12296 | tf_op jit(solution)/shard_map/ppermute | solution.py:50
  79.5 8.7 %collective-permute-start.27 = (f32[2,2,32,896]{3,2,1,0:T(8,128)S(1)}, f32[2,2,32,896]{3,2,1,0:T(8,128)S(1)}, u32[]{:S(2)}, u32[]{:S(2)}) collective-permute-start(f32[2,2,32,896]{3,2,1,0:T(8,128)S(1)} %get-tuple-element.25.refs_0_), channel_id=1, source_target_pairs={{0,32},{1,9},{2,34},{3,11},{4,36},{5,13},{6,38},{7,15},{8,40},{9,1... | collective-permute-start | bytes 1376264 | tf_op jit(solution)/shard_map/ppermute | solution.py:50
  81.0 9.7 %collective-permute-start.29 = (f32[2,2,32,896]{3,2,1,0:T(8,128)S(1)}, f32[2,2,32,896]{3,2,1,0:T(8,128)S(1)}, u32[]{:S(2)}, u32[]{:S(2)}) collective-permute-start(f32[2,2,32,896]{3,2,1,0:T(8,128)S(1)} %get-tuple-element.26.refs_1_), channel_id=1, source_target_pairs={{0,96},{1,25},{2,98},{3,27},{4,100},{5,29},{6,102},{7,31},{8,104},... | collective-permute-start | bytes 1376264 | tf_op jit(solution)/shard_map/ppermute | solution.py:50
  81.8 11.7 %collective-permute-start.31 = (f32[2,2,32,896]{3,2,1,0:T(8,128)S(1)}, f32[2,2,32,896]{3,2,1,0:T(8,128)S(1)}, u32[]{:S(2)}, u32[]{:S(2)}) collective-permute-start(f32[2,2,32,896]{3,2,1,0:T(8,128)S(1)} %get-tuple-element.26.refs_1_), channel_id=1, source_target_pairs={{0,32},{1,9},{2,34},{3,11},{4,36},{5,13},{6,38},{7,15},{8,40},{9,1... | collective-permute-start | bytes 1376264 | tf_op jit(solution)/shard_map/ppermute | solution.py:50
  84.2 11.4 %collective-permute-start.32 = (f32[2,2,32,896]{3,2,1,0:T(8,128)S(1)}, f32[2,2,32,896]{3,2,1,0:T(8,128)S(1)}, u32[]{:S(2)}, u32[]{:S(2)}) collective-permute-start(f32[2,2,32,896]{3,2,1,0:T(8,128)S(1)} %get-tuple-element.25.refs_0_), channel_id=1, source_target_pairs={{0,96},{1,25},{2,98},{3,27},{4,100},{5,29},{6,102},{7,31},{8,104},... | collective-permute-start | bytes 1376264 | tf_op jit(solution)/shard_map/ppermute | solution.py:50
  88.2 9.8 %collective-permute-start.28 = (f32[2,2,32,896]{3,2,1,0:T(8,128)S(1)}, f32[2,2,32,896]{3,2,1,0:T(8,128)S(1)}, u32[]{:S(2)}, u32[]{:S(2)}) collective-permute-start(f32[2,2,32,896]{3,2,1,0:T(8,128)S(1)} %collective-permute-done.27.refs_0_), channel_id=1, source_target_pairs={{0,32},{1,9},{2,34},{3,11},{4,36},{5,13},{6,38},{7,15},{8,40},{9,1... | collective-permute-start | bytes 1376264 | tf_op jit(solution)/shard_map/ppermute | solution.py:50
  90.7 9.8 %collective-permute-start.30 = (f32[2,2,32,896]{3,2,1,0:T(8,128)S(1)}, f32[2,2,32,896]{3,2,1,0:T(8,128)S(1)}, u32[]{:S(2)}, u32[]{:S(2)}) collective-permute-start(f32[2,2,32,896]{3,2,1,0:T(8,128)S(1)} %collective-permute-done.29.refs_1_), channel_id=1, source_target_pairs={{0,96},{1,25},{2,98},{3,27},{4,100},{5,29},{6,102},{7,31},{8,104},... | collective-permute-start | bytes 1376264 | tf_op jit(solution)/shard_map/ppermute | solution.py:50

commit v6 on v5

--- a/solution.py
+++ b/solution.py
@@ -259,8 +259,8 @@
     far_early, far_late = send(left_early, FIRST[1]), send(right_late, FIRST[3])
     groups = ((0, 0), (0, 1), (3, 0), (1, 1), (3, 1), (1, 0), (2, 0), (2, 1))
     pieces = (early, late, left_early, right_late, left_late, right_early, far_early, far_late)
-    new_global = None
-    for n in range(0, len(groups), 2):
+    new_global = unpack(groups[:4], pieces[:4], None, (rows, columns))
+    for n in (4, 6):
         new_global = unpack(groups[n : n + 2], pieces[n : n + 2], new_global, (rows, columns))
     return (new_global, new_momentum)
 

time: 103 us -> 105 us (1.019)
  waiting for transfers between devices: 30.9 us -> 32.2 us
    ppermute x33, waiting for transfers between devices: 30.9 us -> 32.2 us  [send(): return lax.ppermute(value, AXES, route)]
    pallas_call x4 -> x3, Pallas kernels: 3.94 us -> 3.3 us  [unpack(): pl.pallas_call(functools.partial(unpack_kernel, groups, width), out_shape...]
  transfers between devices with their start and end apart: 33 -> 33, of which waited for: 18 -> 20; matrix products, arithmetic and copies ran while one was open for 0% -> 0% of each run, Pallas kernels for 7% -> 6%
where the time goes in v6:
time: 105 us; the launch traced here: 103 us
  starting transfers between devices  59.6 us (57%)
  waiting for transfers between devices  32.2 us (31%)
  Pallas kernels  9.9 us (9%)
    ppermute x33, starting transfers between devices, send(): return lax.ppermute(value, AXES, route)  59.6 us
    ppermute x33, waiting for transfers between devices, send(): return lax.ppermute(value, AXES, route)  32.2 us
    pallas_call x3, Pallas kernels, pack(): pl.pallas_call(functools.partial(pack_kernel, jobs, width), out_shape=[ja...  5.64 us
    pallas_call x3, Pallas kernels, unpack(): pl.pallas_call(functools.partial(unpack_kernel, groups, width), out_shape...  3.3 us
  transfers between devices with their start and end apart: 33, of which 20 were waited for; matrix products, arithmetic and copies ran while one was open for 0% of the time, Pallas kernels for 6%

profile of v6, /device:TPU:2, one launch (start us, length us, event | category | flops | bytes accessed | tf_op | source)
XLA Modules:
  0.0 103.3 jit_solution(3703764825798178356)
XLA Ops:
  0.6 1.4 %pack1.1.refs_1_ = f32[4,2,32,896]{3,2,1,0:T(8,128)S(1)} custom-call(f32[32,28672]{1,0:T(8,128)} %bitcast.17), custom_call_target="tpu_custom_call" | custom-call | bytes 1835008 | tf_op jit(solution)/shard_map/pack1/pallas_call | solution.py:93
  2.0 0.1 fusion.14
  2.1 1.6 %collective-permute-start.1 = (f32[2,2,32,896]{3,2,1,0:T(8,128)S(1)}, f32[2,2,32,896]{3,2,1,0:T(8,128)S(1)}, u32[]{:S(2)}, u32[]{:S(2)}) collective-permute-start(f32[2,2,32,896]{3,2,1,0:T(8,128)S(1)} %get-tuple-element.33), channel_id=1, source_target_pairs={{0,32},{1,9},{2,34},{3,11},{4,36},{5,13},{6,38},{7,15},{8,40},{9,1... | collective-permute-start | bytes 1376264 | tf_op jit(solution)/shard_map/ppermute | solution.py:50
  3.6 0.9 collective-permute-start.5
  4.5 1.7 %pack2.1 = (f32[4,2,32,896]{3,2,1,0:T(8,128)S(1)}, f32[4,2,32,896]{3,2,1,0:T(8,128)S(1)}) custom-call(f32[32,28672]{1,0:T(8,128)} %bitcast.18, f32[4,2,32,896]{3,2,1,0:T(8,128)S(1)} %pack1.1.refs_1_), custom_call_target="tpu_custom_call" | custom-call | bytes 3670016 | tf_op jit(solution)/shard_map/pack2/pallas_call | solution.py:93
  6.2 2.6 %pack4.1 = (f32[4,2,32,896]{3,2,1,0:T(8,128)S(1)}, f32[4,2,32,896]{3,2,1,0:T(8,128)S(1)}, f32[4,2,32,896]{3,2,1,0:T(8,128)S(1)}, f32[4,2,32,896]{3,2,1,0:T(8,128)S(1)}) custom-call(f32[32,28672]{1,0:T(8,128)S(1)} %copy-done, f32[32,28672]{1,0:T(8,128)} %bitcast.19, f32[4,2,32,896]{3,2,1,0:T(8,128)S(1)} %get-tuple-element.15.refs_2_), custom_call_target="tpu_custom_call" | custom-call | bytes 7340032 | tf_op jit(solution)/shard_map/pack4/pallas_call | solution.py:93
  8.8 2.0 %collective-permute-done.1 = f32[2,2,32,896]{3,2,1,0:T(8,128)S(1)} collective-permute-done((f32[2,2,32,896]{3,2,1,0:T(8,128)S(1)}, f32[2,2,32,896]{3,2,1,0:T(8,128)S(1)}, u32[]{:S(2)}, u32[]{:S(2)}) %collective-permute-start.1) | collective-permute-done | bytes 458784 | tf_op jit(solution)/shard_map/ppermute | solution.py:50
  10.9 0.1 subtract_add_fusion.1
  11.0 1.3 %collective-permute-start.2 = (f32[2,2,32,896]{3,2,1,0:T(8,128)S(1)}, f32[2,2,32,896]{3,2,1,0:T(8,128)S(1)}, u32[]{:S(2)}, u32[]{:S(2)}) collective-permute-start(f32[2,2,32,896]{3,2,1,0:T(8,128)S(1)} %get-tuple-element.31), channel_id=1, source_target_pairs={{0,32},{1,9},{2,34},{3,11},{4,36},{5,13},{6,38},{7,15},{8,40},{9,1... | collective-permute-start | bytes 1376264 | tf_op jit(solution)/shard_map/ppermute | solution.py:50
  12.3 0.1 fusion.15
  12.4 2.1 %collective-permute-start = (f32[2,2,32,896]{3,2,1,0:T(8,128)S(1)}, f32[2,2,32,896]{3,2,1,0:T(8,128)S(1)}, u32[]{:S(2)}, u32[]{:S(2)}) collective-permute-start(f32[2,2,32,896]{3,2,1,0:T(8,128)S(1)} %get-tuple-element.35), channel_id=1, source_target_pairs={{0,96},{1,25},{2,98},{3,27},{4,100},{5,29},{6,102},{7,31},{8,104},... | collective-permute-start | bytes 1376264 | tf_op jit(solution)/shard_map/ppermute | solution.py:50
  14.5 3.2 %collective-permute-start.6 = (f32[2,2,32,896]{3,2,1,0:T(8,128)S(1)}, f32[2,2,32,896]{3,2,1,0:T(8,128)S(1)}, u32[]{:S(2)}, u32[]{:S(2)}) collective-permute-start(f32[2,2,32,896]{3,2,1,0:T(8,128)S(1)} %get-tuple-element.36), channel_id=1, source_target_pairs={{0,96},{1,25},{2,98},{3,27},{4,100},{5,29},{6,102},{7,31},{8,104},... | collective-permute-start | bytes 1376264 | tf_op jit(solution)/shard_map/ppermute | solution.py:50
  17.7 5.5 %collective-permute-start.3 = (f32[32,896]{1,0:T(8,128)S(1)}, f32[32,896]{1,0:T(8,128)S(1)}, u32[]{:S(2)}, u32[]{:S(2)}) collective-permute-start(f32[32,896]{1,0:T(8,128)S(1)} %copy-done.1), channel_id=1, source_target_pairs={{0,128},{1,129},{2,130},{3,131},{4,132},{5,133},{6,134},{7,135},{8... | collective-permute-start | bytes 344072 | tf_op jit(solution)/shard_map/ppermute | solution.py:50
  23.2 3.3 %collective-permute-done.3 = f32[32,896]{1,0:T(8,128)S(1)} collective-permute-done((f32[32,896]{1,0:T(8,128)S(1)}, f32[32,896]{1,0:T(8,128)S(1)}, u32[]{:S(2)}, u32[]{:S(2)}) %collective-permute-start.3) | collective-permute-done | bytes 114720 | tf_op jit(solution)/shard_map/ppermute | solution.py:50
  26.6 0.2 fusion.5
  26.8 3.7 %collective-permute-start.7 = (f32[2,32,896]{2,1,0:T(8,128)S(1)}, f32[2,32,896]{2,1,0:T(8,128)S(1)}, u32[]{:S(2)}, u32[]{:S(2)}) collective-permute-start(f32[2,32,896]{2,1,0:T(8,128)S(1)} %get-tuple-element.28), channel_id=1, source_target_pairs={{0,16},{1,65},{2,18},{3,67},{4,20},{5,69},{6,22},{7,71},{8,24},{9,... | collective-permute-start | bytes 688136 | tf_op jit(solution)/shard_map/ppermute | solution.py:50
  30.5 0.4 collective-permute-start.9
  30.9 1.6 %collective-permute-start.8 = (f32[2,32,896]{2,1,0:T(8,128)S(1)}, f32[2,32,896]{2,1,0:T(8,128)S(1)}, u32[]{:S(2)}, u32[]{:S(2)}) collective-permute-start(f32[2,32,896]{2,1,0:T(8,128)S(1)} %get-tuple-element.30), channel_id=1, source_target_pairs={{0,8},{1,33},{2,10},{3,35},{4,12},{5,37},{6,14},{7,39},{8,16},{9,4... | collective-permute-start | bytes 688136 | tf_op jit(solution)/shard_map/ppermute | solution.py:50
  32.5 2.0 %collective-permute-done.7 = f32[2,32,896]{2,1,0:T(8,128)S(1)} collective-permute-done((f32[2,32,896]{2,1,0:T(8,128)S(1)}, f32[2,32,896]{2,1,0:T(8,128)S(1)}, u32[]{:S(2)}, u32[]{:S(2)}) %collective-permute-start.7) | collective-permute-done | bytes 229408 | tf_op jit(solution)/shard_map/ppermute | solution.py:50
  34.5 2.5 %collective-permute-done.9 = f32[2,32,896]{2,1,0:T(8,128)S(1)} collective-permute-done((f32[2,32,896]{2,1,0:T(8,128)S(1)}, f32[2,32,896]{2,1,0:T(8,128)S(1)}, u32[]{:S(2)}, u32[]{:S(2)}) %collective-permute-start.9) | collective-permute-done | bytes 229408 | tf_op jit(solution)/shard_map/ppermute | solution.py:50
  37.0 1.2 %collective-permute-done.8 = f32[2,32,896]{2,1,0:T(8,128)S(1)} collective-permute-done((f32[2,32,896]{2,1,0:T(8,128)S(1)}, f32[2,32,896]{2,1,0:T(8,128)S(1)}, u32[]{:S(2)}, u32[]{:S(2)}) %collective-permute-start.8) | collective-permute-done | bytes 229408 | tf_op jit(solution)/shard_map/ppermute | solution.py:50
  38.1 0.1 fusion.12
  38.2 6.8 %collective-permute-start.10 = (f32[2,32,896]{2,1,0:T(8,128)S(1)}, f32[2,32,896]{2,1,0:T(8,128)S(1)}, u32[]{:S(2)}, u32[]{:S(2)}) collective-permute-start(f32[2,32,896]{2,1,0:T(8,128)S(1)} %fusion.12), channel_id=1, source_target_pairs={{0,128},{1,129},{2,130},{3,131},{4,132},{5,133},{6,134},{7,135},{8... | collective-permute-start | bytes 688136 | tf_op jit(solution)/shard_map/ppermute | solution.py:50
  45.0 0.2 collective-permute-start.14
  45.2 2.8 %collective-permute-start.13 = (f32[2,32,896]{2,1,0:T(8,128)S(1)}, f32[2,32,896]{2,1,0:T(8,128)S(1)}, u32[]{:S(2)}, u32[]{:S(2)}) collective-permute-start(f32[2,32,896]{2,1,0:T(8,128)S(1)} %pad_maximum_fusion.refs_9_), channel_id=1, source_target_pairs={{0,16},{1,65},{2,18},{3,67},{4,20},{5,69},{6,22},{7,71},{8,24},{9,... | collective-permute-start | bytes 688136 | tf_op jit(solution)/shard_map/ppermute | solution.py:50
  48.0 1.3 %collective-permute-start.12 = (f32[2,32,896]{2,1,0:T(8,128)S(1)}, f32[2,32,896]{2,1,0:T(8,128)S(1)}, u32[]{:S(2)}, u32[]{:S(2)}) collective-permute-start(f32[2,32,896]{2,1,0:T(8,128)S(1)} %pad_maximum_fusion.refs_9_), channel_id=1, source_target_pairs={{0,24},{1,97},{2,26},{3,99},{4,28},{5,101},{6,30},{7,103},{8,0},{9... | collective-permute-start | bytes 688136 | tf_op jit(solution)/shard_map/ppermute | solution.py:50
  49.4 2.0 %collective-permute-done.10 = f32[2,32,896]{2,1,0:T(8,128)S(1)} collective-permute-done((f32[2,32,896]{2,1,0:T(8,128)S(1)}, f32[2,32,896]{2,1,0:T(8,128)S(1)}, u32[]{:S(2)}, u32[]{:S(2)}) %collective-permute-start.10) | collective-permute-done | bytes 229408 | tf_op jit(solution)/shard_map/ppermute | solution.py:50
  51.5 0.1 squares.1
  51.5 0.1 collective-permute-start.11
  51.6 1.2 %collective-permute-done.11 = f32[8,128]{1,0:T(8,128)S(1)} collective-permute-done((f32[8,128]{1,0:T(8,128)S(1)}, f32[8,128]{1,0:T(8,128)S(1)}, u32[]{:S(2)}, u32[]{:S(2)}) %collective-permute-start.11) | collective-permute-done | bytes 4128 | tf_op jit(solution)/shard_map/ppermute | solution.py:50
  52.8 2.0 %collective-permute-done.14.refs_12_ = f32[2,32,896]{2,1,0:T(8,128)S(1)} collective-permute-done((f32[2,32,896]{2,1,0:T(8,128)S(1)}, f32[2,32,896]{2,1,0:T(8,128)S(1)}, u32[]{:S(2)}, u32[]{:S(2)}) %collective-permute-start.14) | collective-permute-done | bytes 229408 | tf_op jit(solution)/shard_map/ppermute | solution.py:50
  54.7 0.9 collective-permute-done.12.refs_10_
  55.6 1.9 %collective-permute-start.17 = (f32[8,128]{1,0:T(8,128)S(1)}, f32[8,128]{1,0:T(8,128)S(1)}, u32[]{:S(2)}, u32[]{:S(2)}) collective-permute-start(f32[8,128]{1,0:T(8,128)S(1)} %add.97), channel_id=1, source_target_pairs={{0,6},{1,7},{2,0},{3,1},{4,2},{5,3},{6,4},{7,5},{8,14},{9,15},{10,... | collective-permute-start | bytes 12296 | tf_op jit(solution)/shard_map/ppermute | solution.py:50
  57.5 0.6 collective-permute-start.16
  58.2 0.9 collective-permute-start.15
  59.1 0.1 collective-permute-done.17
  59.2 2.8 %collective-permute-done.16 = f32[8,128]{1,0:T(8,128)S(1)} collective-permute-done((f32[8,128]{1,0:T(8,128)S(1)}, f32[8,128]{1,0:T(8,128)S(1)}, u32[]{:S(2)}, u32[]{:S(2)}) %collective-permute-start.16) | collective-permute-done | bytes 4128 | tf_op jit(solution)/shard_map/ppermute | solution.py:50
  62.0 1.5 %collective-permute-done.15 = f32[8,128]{1,0:T(8,128)S(1)} collective-permute-done((f32[8,128]{1,0:T(8,128)S(1)}, f32[8,128]{1,0:T(8,128)S(1)}, u32[]{:S(2)}, u32[]{:S(2)}) %collective-permute-start.15) | collective-permute-done | bytes 4128 | tf_op jit(solution)/shard_map/ppermute | solution.py:50
  63.6 2.7 %collective-permute-start.20 = (f32[8,128]{1,0:T(8,128)S(1)}, f32[8,128]{1,0:T(8,128)S(1)}, u32[]{:S(2)}, u32[]{:S(2)}) collective-permute-start(f32[8,128]{1,0:T(8,128)S(1)} %add_add_fusion.1), channel_id=1, source_target_pairs={{0,24},{1,97},{2,26},{3,99},{4,28},{5,101},{6,30},{7,103},{8,0},{9... | collective-permute-start | bytes 12296 | tf_op jit(solution)/shard_map/ppermute | solution.py:50
  66.2 0.5 collective-permute-start.19
  66.7 0.5 collective-permute-start.18
  67.2 2.5 %collective-permute-start.26 = (f32[2,32,896]{2,1,0:T(8,128)S(1)}, f32[2,32,896]{2,1,0:T(8,128)S(1)}, u32[]{:S(2)}, u32[]{:S(2)}) collective-permute-start(f32[2,32,896]{2,1,0:T(8,128)S(1)} %fusion.13.value.refs_5_), channel_id=1, source_target_pairs={{0,8},{1,33},{2,10},{3,35},{4,12},{5,37},{6,14},{7,39},{8,16},{9,4... | collective-permute-start | bytes 688136 | tf_op jit(solution)/shard_map/ppermute | solution.py:50
  69.7 1.7 %collective-permute-start.25 = (f32[2,32,896]{2,1,0:T(8,128)S(1)}, f32[2,32,896]{2,1,0:T(8,128)S(1)}, u32[]{:S(2)}, u32[]{:S(2)}) collective-permute-start(f32[2,32,896]{2,1,0:T(8,128)S(1)} %fusion.13.value.refs_5_), channel_id=1, source_target_pairs={{0,16},{1,65},{2,18},{3,67},{4,20},{5,69},{6,22},{7,71},{8,24},{9,... | collective-permute-start | bytes 688136 | tf_op jit(solution)/shard_map/ppermute | solution.py:50
  71.4 1.0 collective-permute-start.24
  72.4 2.1 %collective-permute-start.23 = (f32[8,128]{1,0:T(8,128)S(1)}, f32[8,128]{1,0:T(8,128)S(1)}, u32[]{:S(2)}, u32[]{:S(2)}) collective-permute-start(f32[8,128]{1,0:T(8,128)S(1)} %add_add_fusion.refs_0_), channel_id=1, source_target_pairs={{0,96},{1,25},{2,98},{3,27},{4,100},{5,29},{6,102},{7,31},{8,104},... | collective-permute-start | bytes 12296 | tf_op jit(solution)/shard_map/ppermute | solution.py:50
  74.5 1.5 %collective-permute-start.22 = (f32[8,128]{1,0:T(8,128)S(1)}, f32[8,128]{1,0:T(8,128)S(1)}, u32[]{:S(2)}, u32[]{:S(2)}) collective-permute-start(f32[8,128]{1,0:T(8,128)S(1)} %add_add_fusion.refs_0_), channel_id=1, source_target_pairs={{0,64},{1,17},{2,66},{3,19},{4,68},{5,21},{6,70},{7,23},{8,72},{9,... | collective-permute-start | bytes 12296 | tf_op jit(solution)/shard_map/ppermute | solution.py:50
  76.1 0.1 collective-permute-done.23.refs_3_
  76.1 2.5 %collective-permute-start.21 = (f32[8,128]{1,0:T(8,128)S(1)}, f32[8,128]{1,0:T(8,128)S(1)}, u32[]{:S(2)}, u32[]{:S(2)}) collective-permute-start(f32[8,128]{1,0:T(8,128)S(1)} %add_add_fusion.refs_0_), channel_id=1, source_target_pairs={{0,32},{1,9},{2,34},{3,11},{4,36},{5,13},{6,38},{7,15},{8,40},{9,1... | collective-permute-start | bytes 12296 | tf_op jit(solution)/shard_map/ppermute | solution.py:50
  78.6 1.1 %collective-permute-done.22.refs_2_ = f32[8,128]{1,0:T(8,128)S(1)} collective-permute-done((f32[8,128]{1,0:T(8,128)S(1)}, f32[8,128]{1,0:T(8,128)S(1)}, u32[]{:S(2)}, u32[]{:S(2)}) %collective-permute-start.22) | collective-permute-done | bytes 4128 | tf_op jit(solution)/shard_map/ppermute | solution.py:50
  79.7 0.4 collective-permute-done.21.refs_1_
  80.1 0.9 update.1
  81.0 2.6 %collective-permute-start.27 = (f32[2,2,32,896]{3,2,1,0:T(8,128)S(1)}, f32[2,2,32,896]{3,2,1,0:T(8,128)S(1)}, u32[]{:S(2)}, u32[]{:S(2)}) collective-permute-start(f32[2,2,32,896]{3,2,1,0:T(8,128)S(1)} %get-tuple-element.25.refs_0_), channel_id=1, source_target_pairs={{0,32},{1,9},{2,34},{3,11},{4,36},{5,13},{6,38},{7,15},{8,40},{9,1... | collective-permute-start | bytes 1376264 | tf_op jit(solution)/shard_map/ppermute | solution.py:50
  83.6 0.9 collective-permute-start.29
  84.4 3.2 %collective-permute-start.32 = (f32[2,2,32,896]{3,2,1,0:T(8,128)S(1)}, f32[2,2,32,896]{3,2,1,0:T(8,128)S(1)}, u32[]{:S(2)}, u32[]{:S(2)}) collective-permute-start(f32[2,2,32,896]{3,2,1,0:T(8,128)S(1)} %get-tuple-element.25.refs_0_), channel_id=1, source_target_pairs={{0,96},{1,25},{2,98},{3,27},{4,100},{5,29},{6,102},{7,31},{8,104},... | collective-permute-start | bytes 1376264 | tf_op jit(solution)/shard_map/ppermute | solution.py:50
  87.7 3.2 %collective-permute-done.27.refs_2_ = f32[2,2,32,896]{3,2,1,0:T(8,128)S(1)} collective-permute-done((f32[2,2,32,896]{3,2,1,0:T(8,128)S(1)}, f32[2,2,32,896]{3,2,1,0:T(8,128)S(1)}, u32[]{:S(2)}, u32[]{:S(2)}) %collective-permute-start.27) | collective-permute-done | bytes 458784 | tf_op jit(solution)/shard_map/ppermute | solution.py:50
  90.9 1.2 %collective-permute-start.28 = (f32[2,2,32,896]{3,2,1,0:T(8,128)S(1)}, f32[2,2,32,896]{3,2,1,0:T(8,128)S(1)}, u32[]{:S(2)}, u32[]{:S(2)}) collective-permute-start(f32[2,2,32,896]{3,2,1,0:T(8,128)S(1)} %collective-permute-done.27.refs_2_), channel_id=1, source_target_pairs={{0,32},{1,9},{2,34},{3,11},{4,36},{5,13},{6,38},{7,15},{8,40},{9,1... | collective-permute-start | bytes 1376264 | tf_op jit(solution)/shard_map/ppermute | solution.py:50
  92.1 0.3 collective-permute-done.29.refs_3_
  92.3 1.8 %collective-permute-start.30 = (f32[2,2,32,896]{3,2,1,0:T(8,128)S(1)}, f32[2,2,32,896]{3,2,1,0:T(8,128)S(1)}, u32[]{:S(2)}, u32[]{:S(2)}) collective-permute-start(f32[2,2,32,896]{3,2,1,0:T(8,128)S(1)} %collective-permute-done.29.refs_3_), channel_id=1, source_target_pairs={{0,96},{1,25},{2,98},{3,27},{4,100},{5,29},{6,102},{7,31},{8,104},... | collective-permute-start | bytes 1376264 | tf_op jit(solution)/shard_map/ppermute | solution.py:50
  94.1 1.3 %unpack4.1.refs_2_ = f32[32,28672]{1,0:T(8,128)} custom-call(f32[2,2,32,896]{3,2,1,0:T(8,128)S(1)} %get-tuple-element.25.refs_0_, f32[2,2,32,896]{3,2,1,0:T(8,128)S(1)} %get-tuple-element.26.refs_1_, f32[2,2,32,896]{3,2,1,0:T(8,128)S(1)} %collective-permute-done.27.refs_2_, f32[2,2,32,896]{3,2,1,0:T(8,128)S(1)} %collective-permute-done.29.refs_3_), custom_call_target="tpu_custom_call" | custom-call | bytes 3670016 | tf_op jit(solution)/shard_map/unpack4/pallas_call | solution.py:125
  95.5 1.7 %collective-permute-done.32.refs_1_ = f32[2,2,32,896]{3,2,1,0:T(8,128)S(1)} collective-permute-done((f32[2,2,32,896]{3,2,1,0:T(8,128)S(1)}, f32[2,2,32,896]{3,2,1,0:T(8,128)S(1)}, u32[]{:S(2)}, u32[]{:S(2)}) %collective-permute-start.32) | collective-permute-done | bytes 458784 | tf_op jit(solution)/shard_map/ppermute | solution.py:50
  97.2 1.0 unpack2.2.refs_2_
  98.2 2.9 %collective-permute-done.28.refs_0_ = f32[2,2,32,896]{3,2,1,0:T(8,128)S(1)} collective-permute-done((f32[2,2,32,896]{3,2,1,0:T(8,128)S(1)}, f32[2,2,32,896]{3,2,1,0:T(8,128)S(1)}, u32[]{:S(2)}, u32[]{:S(2)}) %collective-permute-start.28) | collective-permute-done | bytes 458784 | tf_op jit(solution)/shard_map/ppermute | solution.py:50
  101.1 1.1 %collective-permute-done.30.refs_1_ = f32[2,2,32,896]{3,2,1,0:T(8,128)S(1)} collective-permute-done((f32[2,2,32,896]{3,2,1,0:T(8,128)S(1)}, f32[2,2,32,896]{3,2,1,0:T(8,128)S(1)}, u32[]{:S(2)}, u32[]{:S(2)}) %collective-permute-start.30) | collective-permute-done | bytes 458784 | tf_op jit(solution)/shard_map/ppermute | solution.py:50
  102.1 1.0 unpack2.3
  (25 shorter events, 0.1 us)
Async XLA Ops:
  2.0 4.2 %copy-start = (f32[32,28672]{1,0:T(8,128)S(1)}, f32[32,28672]{1,0:T(8,128)}, u32[]{:S(2)}) copy-start(f32[32,28672]{1,0:T(8,128)} %refs_0_.1) | copy-start | bytes 11010052
  2.1 8.8 %collective-permute-start.1 = (f32[2,2,32,896]{3,2,1,0:T(8,128)S(1)}, f32[2,2,32,896]{3,2,1,0:T(8,128)S(1)}, u32[]{:S(2)}, u32[]{:S(2)}) collective-permute-start(f32[2,2,32,896]{3,2,1,0:T(8,128)S(1)} %get-tuple-element.33), channel_id=1, source_target_pairs={{0,32},{1,9},{2,34},{3,11},{4,36},{5,13},{6,38},{7,15},{8,40},{9,1... | collective-permute-start | bytes 1376264 | tf_op jit(solution)/shard_map/ppermute | solution.py:50
  3.6 8.7 %collective-permute-start.5 = (f32[2,2,32,896]{3,2,1,0:T(8,128)S(1)}, f32[2,2,32,896]{3,2,1,0:T(8,128)S(1)}, u32[]{:S(2)}, u32[]{:S(2)}) collective-permute-start(f32[2,2,32,896]{3,2,1,0:T(8,128)S(1)} %get-tuple-element.34), channel_id=1, source_target_pairs={{0,96},{1,25},{2,98},{3,27},{4,100},{5,29},{6,102},{7,31},{8,104},... | collective-permute-start | bytes 1376264 | tf_op jit(solution)/shard_map/ppermute | solution.py:50
  8.8 8.9 %copy-start.1 = (f32[32,896]{1,0:T(8,128)S(1)}, f32[32,896]{1,0:T(8,128)}, u32[]{:S(2)}) copy-start(f32[32,896]{1,0:T(8,128)} %param.5) | copy-start | bytes 344068
  11.0 15.6 %collective-permute-start.2 = (f32[2,2,32,896]{3,2,1,0:T(8,128)S(1)}, f32[2,2,32,896]{3,2,1,0:T(8,128)S(1)}, u32[]{:S(2)}, u32[]{:S(2)}) collective-permute-start(f32[2,2,32,896]{3,2,1,0:T(8,128)S(1)} %get-tuple-element.31), channel_id=1, source_target_pairs={{0,32},{1,9},{2,34},{3,11},{4,36},{5,13},{6,38},{7,15},{8,40},{9,1... | collective-permute-start | bytes 1376264 | tf_op jit(solution)/shard_map/ppermute | solution.py:50
  12.4 14.1 %collective-permute-start = (f32[2,2,32,896]{3,2,1,0:T(8,128)S(1)}, f32[2,2,32,896]{3,2,1,0:T(8,128)S(1)}, u32[]{:S(2)}, u32[]{:S(2)}) collective-permute-start(f32[2,2,32,896]{3,2,1,0:T(8,128)S(1)} %get-tuple-element.35), channel_id=1, source_target_pairs={{0,96},{1,25},{2,98},{3,27},{4,100},{5,29},{6,102},{7,31},{8,104},... | collective-permute-start | bytes 1376264 | tf_op jit(solution)/shard_map/ppermute | solution.py:50
  14.5 12.1 %collective-permute-start.6 = (f32[2,2,32,896]{3,2,1,0:T(8,128)S(1)}, f32[2,2,32,896]{3,2,1,0:T(8,128)S(1)}, u32[]{:S(2)}, u32[]{:S(2)}) collective-permute-start(f32[2,2,32,896]{3,2,1,0:T(8,128)S(1)} %get-tuple-element.36), channel_id=1, source_target_pairs={{0,96},{1,25},{2,98},{3,27},{4,100},{5,29},{6,102},{7,31},{8,104},... | collective-permute-start | bytes 1376264 | tf_op jit(solution)/shard_map/ppermute | solution.py:50
  17.7 8.9 %collective-permute-start.4 = (f32[2,2,32,896]{3,2,1,0:T(8,128)S(1)}, f32[2,2,32,896]{3,2,1,0:T(8,128)S(1)}, u32[]{:S(2)}, u32[]{:S(2)}) collective-permute-start(f32[2,2,32,896]{3,2,1,0:T(8,128)S(1)} %get-tuple-element.32), channel_id=1, source_target_pairs={{0,32},{1,9},{2,34},{3,11},{4,36},{5,13},{6,38},{7,15},{8,40},{9,1... | collective-permute-start | bytes 1376264 | tf_op jit(solution)/shard_map/ppermute | solution.py:50
  17.7 8.8 %collective-permute-start.3 = (f32[32,896]{1,0:T(8,128)S(1)}, f32[32,896]{1,0:T(8,128)S(1)}, u32[]{:S(2)}, u32[]{:S(2)}) collective-permute-start(f32[32,896]{1,0:T(8,128)S(1)} %copy-done.1), channel_id=1, source_target_pairs={{0,128},{1,129},{2,130},{3,131},{4,132},{5,133},{6,134},{7,135},{8... | collective-permute-start | bytes 344072 | tf_op jit(solution)/shard_map/ppermute | solution.py:50
  26.8 7.7 %collective-permute-start.7 = (f32[2,32,896]{2,1,0:T(8,128)S(1)}, f32[2,32,896]{2,1,0:T(8,128)S(1)}, u32[]{:S(2)}, u32[]{:S(2)}) collective-permute-start(f32[2,32,896]{2,1,0:T(8,128)S(1)} %get-tuple-element.28), channel_id=1, source_target_pairs={{0,16},{1,65},{2,18},{3,67},{4,20},{5,69},{6,22},{7,71},{8,24},{9,... | collective-permute-start | bytes 688136 | tf_op jit(solution)/shard_map/ppermute | solution.py:50
  30.5 6.5 %collective-permute-start.9 = (f32[2,32,896]{2,1,0:T(8,128)S(1)}, f32[2,32,896]{2,1,0:T(8,128)S(1)}, u32[]{:S(2)}, u32[]{:S(2)}) collective-permute-start(f32[2,32,896]{2,1,0:T(8,128)S(1)} %get-tuple-element.29), channel_id=1, source_target_pairs={{0,24},{1,97},{2,26},{3,99},{4,28},{5,101},{6,30},{7,103},{8,0},{9... | collective-permute-start | bytes 688136 | tf_op jit(solution)/shard_map/ppermute | solution.py:50
  30.9 7.2 %collective-permute-start.8 = (f32[2,32,896]{2,1,0:T(8,128)S(1)}, f32[2,32,896]{2,1,0:T(8,128)S(1)}, u32[]{:S(2)}, u32[]{:S(2)}) collective-permute-start(f32[2,32,896]{2,1,0:T(8,128)S(1)} %get-tuple-element.30), channel_id=1, source_target_pairs={{0,8},{1,33},{2,10},{3,35},{4,12},{5,37},{6,14},{7,39},{8,16},{9,4... | collective-permute-start | bytes 688136 | tf_op jit(solution)/shard_map/ppermute | solution.py:50
  38.2 13.2 %collective-permute-start.10 = (f32[2,32,896]{2,1,0:T(8,128)S(1)}, f32[2,32,896]{2,1,0:T(8,128)S(1)}, u32[]{:S(2)}, u32[]{:S(2)}) collective-permute-start(f32[2,32,896]{2,1,0:T(8,128)S(1)} %fusion.12), channel_id=1, source_target_pairs={{0,128},{1,129},{2,130},{3,131},{4,132},{5,133},{6,134},{7,135},{8... | collective-permute-start | bytes 688136 | tf_op jit(solution)/shard_map/ppermute | solution.py:50
  45.0 9.7 %collective-permute-start.14 = (f32[2,32,896]{2,1,0:T(8,128)S(1)}, f32[2,32,896]{2,1,0:T(8,128)S(1)}, u32[]{:S(2)}, u32[]{:S(2)}) collective-permute-start(f32[2,32,896]{2,1,0:T(8,128)S(1)} %pad_maximum_fusion.refs_9_), channel_id=1, source_target_pairs={{0,8},{1,33},{2,10},{3,35},{4,12},{5,37},{6,14},{7,39},{8,16},{9,4... | collective-permute-start | bytes 688136 | tf_op jit(solution)/shard_map/ppermute | solution.py:50
  45.2 9.5 %collective-permute-start.13 = (f32[2,32,896]{2,1,0:T(8,128)S(1)}, f32[2,32,896]{2,1,0:T(8,128)S(1)}, u32[]{:S(2)}, u32[]{:S(2)}) collective-permute-start(f32[2,32,896]{2,1,0:T(8,128)S(1)} %pad_maximum_fusion.refs_9_), channel_id=1, source_target_pairs={{0,16},{1,65},{2,18},{3,67},{4,20},{5,69},{6,22},{7,71},{8,24},{9,... | collective-permute-start | bytes 688136 | tf_op jit(solution)/shard_map/ppermute | solution.py:50
  48.0 7.6 %collective-permute-start.12 = (f32[2,32,896]{2,1,0:T(8,128)S(1)}, f32[2,32,896]{2,1,0:T(8,128)S(1)}, u32[]{:S(2)}, u32[]{:S(2)}) collective-permute-start(f32[2,32,896]{2,1,0:T(8,128)S(1)} %pad_maximum_fusion.refs_9_), channel_id=1, source_target_pairs={{0,24},{1,97},{2,26},{3,99},{4,28},{5,101},{6,30},{7,103},{8,0},{9... | collective-permute-start | bytes 688136 | tf_op jit(solution)/shard_map/ppermute | solution.py:50
  51.5 1.2 %collective-permute-start.11 = (f32[8,128]{1,0:T(8,128)S(1)}, f32[8,128]{1,0:T(8,128)S(1)}, u32[]{:S(2)}, u32[]{:S(2)}) collective-permute-start(f32[8,128]{1,0:T(8,128)S(1)} %squares.1), channel_id=1, source_target_pairs={{0,1},{1,0},{2,3},{3,2},{4,5},{5,4},{6,7},{7,6},{8,9},{9,8},{10,11... | collective-permute-start | bytes 12296 | tf_op jit(solution)/shard_map/ppermute | solution.py:50
  55.6 3.6 %collective-permute-start.17 = (f32[8,128]{1,0:T(8,128)S(1)}, f32[8,128]{1,0:T(8,128)S(1)}, u32[]{:S(2)}, u32[]{:S(2)}) collective-permute-start(f32[8,128]{1,0:T(8,128)S(1)} %add.97), channel_id=1, source_target_pairs={{0,6},{1,7},{2,0},{3,1},{4,2},{5,3},{6,4},{7,5},{8,14},{9,15},{10,... | collective-permute-start | bytes 12296 | tf_op jit(solution)/shard_map/ppermute | solution.py:50
  57.5 4.5 %collective-permute-start.16 = (f32[8,128]{1,0:T(8,128)S(1)}, f32[8,128]{1,0:T(8,128)S(1)}, u32[]{:S(2)}, u32[]{:S(2)}) collective-permute-start(f32[8,128]{1,0:T(8,128)S(1)} %add.97), channel_id=1, source_target_pairs={{0,4},{1,5},{2,6},{3,7},{4,0},{5,1},{6,2},{7,3},{8,12},{9,13},{10,... | collective-permute-start | bytes 12296 | tf_op jit(solution)/shard_map/ppermute | solution.py:50
  58.2 5.4 %collective-permute-start.15 = (f32[8,128]{1,0:T(8,128)S(1)}, f32[8,128]{1,0:T(8,128)S(1)}, u32[]{:S(2)}, u32[]{:S(2)}) collective-permute-start(f32[8,128]{1,0:T(8,128)S(1)} %add.97), channel_id=1, source_target_pairs={{0,2},{1,3},{2,4},{3,5},{4,6},{5,7},{6,0},{7,1},{8,10},{9,11},{10,... | collective-permute-start | bytes 12296 | tf_op jit(solution)/shard_map/ppermute | solution.py:50
  63.6 7.8 %collective-permute-start.20 = (f32[8,128]{1,0:T(8,128)S(1)}, f32[8,128]{1,0:T(8,128)S(1)}, u32[]{:S(2)}, u32[]{:S(2)}) collective-permute-start(f32[8,128]{1,0:T(8,128)S(1)} %add_add_fusion.1), channel_id=1, source_target_pairs={{0,24},{1,97},{2,26},{3,99},{4,28},{5,101},{6,30},{7,103},{8,0},{9... | collective-permute-start | bytes 12296 | tf_op jit(solution)/shard_map/ppermute | solution.py:50
  66.2 6.2 %collective-permute-start.19 = (f32[8,128]{1,0:T(8,128)S(1)}, f32[8,128]{1,0:T(8,128)S(1)}, u32[]{:S(2)}, u32[]{:S(2)}) collective-permute-start(f32[8,128]{1,0:T(8,128)S(1)} %add_add_fusion.1), channel_id=1, source_target_pairs={{0,16},{1,65},{2,18},{3,67},{4,20},{5,69},{6,22},{7,71},{8,24},{9,... | collective-permute-start | bytes 12296 | tf_op jit(solution)/shard_map/ppermute | solution.py:50
  66.7 5.7 %collective-permute-start.18 = (f32[8,128]{1,0:T(8,128)S(1)}, f32[8,128]{1,0:T(8,128)S(1)}, u32[]{:S(2)}, u32[]{:S(2)}) collective-permute-start(f32[8,128]{1,0:T(8,128)S(1)} %add_add_fusion.1), channel_id=1, source_target_pairs={{0,8},{1,33},{2,10},{3,35},{4,12},{5,37},{6,14},{7,39},{8,16},{9,4... | collective-permute-start | bytes 12296 | tf_op jit(solution)/shard_map/ppermute | solution.py:50
  67.2 12.9 %collective-permute-start.26 = (f32[2,32,896]{2,1,0:T(8,128)S(1)}, f32[2,32,896]{2,1,0:T(8,128)S(1)}, u32[]{:S(2)}, u32[]{:S(2)}) collective-permute-start(f32[2,32,896]{2,1,0:T(8,128)S(1)} %fusion.13.value.refs_5_), channel_id=1, source_target_pairs={{0,8},{1,33},{2,10},{3,35},{4,12},{5,37},{6,14},{7,39},{8,16},{9,4... | collective-permute-start | bytes 688136 | tf_op jit(solution)/shard_map/ppermute | solution.py:50
  69.7 10.3 %collective-permute-start.25 = (f32[2,32,896]{2,1,0:T(8,128)S(1)}, f32[2,32,896]{2,1,0:T(8,128)S(1)}, u32[]{:S(2)}, u32[]{:S(2)}) collective-permute-start(f32[2,32,896]{2,1,0:T(8,128)S(1)} %fusion.13.value.refs_5_), channel_id=1, source_target_pairs={{0,16},{1,65},{2,18},{3,67},{4,20},{5,69},{6,22},{7,71},{8,24},{9,... | collective-permute-start | bytes 688136 | tf_op jit(solution)/shard_map/ppermute | solution.py:50
  71.4 8.6 %collective-permute-start.24 = (f32[2,32,896]{2,1,0:T(8,128)S(1)}, f32[2,32,896]{2,1,0:T(8,128)S(1)}, u32[]{:S(2)}, u32[]{:S(2)}) collective-permute-start(f32[2,32,896]{2,1,0:T(8,128)S(1)} %fusion.13.value.refs_5_), channel_id=1, source_target_pairs={{0,24},{1,97},{2,26},{3,99},{4,28},{5,101},{6,30},{7,103},{8,0},{9... | collective-permute-start | bytes 688136 | tf_op jit(solution)/shard_map/ppermute | solution.py:50
  72.4 3.7 %collective-permute-start.23 = (f32[8,128]{1,0:T(8,128)S(1)}, f32[8,128]{1,0:T(8,128)S(1)}, u32[]{:S(2)}, u32[]{:S(2)}) collective-permute-start(f32[8,128]{1,0:T(8,128)S(1)} %add_add_fusion.refs_0_), channel_id=1, source_target_pairs={{0,96},{1,25},{2,98},{3,27},{4,100},{5,29},{6,102},{7,31},{8,104},... | collective-permute-start | bytes 12296 | tf_op jit(solution)/shard_map/ppermute | solution.py:50
  74.5 5.1 %collective-permute-start.22 = (f32[8,128]{1,0:T(8,128)S(1)}, f32[8,128]{1,0:T(8,128)S(1)}, u32[]{:S(2)}, u32[]{:S(2)}) collective-permute-start(f32[8,128]{1,0:T(8,128)S(1)} %add_add_fusion.refs_0_), channel_id=1, source_target_pairs={{0,64},{1,17},{2,66},{3,19},{4,68},{5,21},{6,70},{7,23},{8,72},{9,... | collective-permute-start | bytes 12296 | tf_op jit(solution)/shard_map/ppermute | solution.py:50
  76.1 3.9 %collective-permute-start.21 = (f32[8,128]{1,0:T(8,128)S(1)}, f32[8,128]{1,0:T(8,128)S(1)}, u32[]{:S(2)}, u32[]{:S(2)}) collective-permute-start(f32[8,128]{1,0:T(8,128)S(1)} %add_add_fusion.refs_0_), channel_id=1, source_target_pairs={{0,32},{1,9},{2,34},{3,11},{4,36},{5,13},{6,38},{7,15},{8,40},{9,1... | collective-permute-start | bytes 12296 | tf_op jit(solution)/shard_map/ppermute | solution.py:50
  81.0 9.9 %collective-permute-start.27 = (f32[2,2,32,896]{3,2,1,0:T(8,128)S(1)}, f32[2,2,32,896]{3,2,1,0:T(8,128)S(1)}, u32[]{:S(2)}, u32[]{:S(2)}) collective-permute-start(f32[2,2,32,896]{3,2,1,0:T(8,128)S(1)} %get-tuple-element.25.refs_0_), channel_id=1, source_target_pairs={{0,32},{1,9},{2,34},{3,11},{4,36},{5,13},{6,38},{7,15},{8,40},{9,1... | collective-permute-start | bytes 1376264 | tf_op jit(solution)/shard_map/ppermute | solution.py:50
  83.6 8.7 %collective-permute-start.29 = (f32[2,2,32,896]{3,2,1,0:T(8,128)S(1)}, f32[2,2,32,896]{3,2,1,0:T(8,128)S(1)}, u32[]{:S(2)}, u32[]{:S(2)}) collective-permute-start(f32[2,2,32,896]{3,2,1,0:T(8,128)S(1)} %get-tuple-element.26.refs_1_), channel_id=1, source_target_pairs={{0,96},{1,25},{2,98},{3,27},{4,100},{5,29},{6,102},{7,31},{8,104},... | collective-permute-start | bytes 1376264 | tf_op jit(solution)/shard_map/ppermute | solution.py:50
  84.4 12.8 %collective-permute-start.32 = (f32[2,2,32,896]{3,2,1,0:T(8,128)S(1)}, f32[2,2,32,896]{3,2,1,0:T(8,128)S(1)}, u32[]{:S(2)}, u32[]{:S(2)}) collective-permute-start(f32[2,2,32,896]{3,2,1,0:T(8,128)S(1)} %get-tuple-element.25.refs_0_), channel_id=1, source_target_pairs={{0,96},{1,25},{2,98},{3,27},{4,100},{5,29},{6,102},{7,31},{8,104},... | collective-permute-start | bytes 1376264 | tf_op jit(solution)/shard_map/ppermute | solution.py:50
  87.7 9.6 %collective-permute-start.31 = (f32[2,2,32,896]{3,2,1,0:T(8,128)S(1)}, f32[2,2,32,896]{3,2,1,0:T(8,128)S(1)}, u32[]{:S(2)}, u32[]{:S(2)}) collective-permute-start(f32[2,2,32,896]{3,2,1,0:T(8,128)S(1)} %get-tuple-element.26.refs_1_), channel_id=1, source_target_pairs={{0,32},{1,9},{2,34},{3,11},{4,36},{5,13},{6,38},{7,15},{8,40},{9,1... | collective-permute-start | bytes 1376264 | tf_op jit(solution)/shard_map/ppermute | solution.py:50
  90.9 10.2 %collective-permute-start.28 = (f32[2,2,32,896]{3,2,1,0:T(8,128)S(1)}, f32[2,2,32,896]{3,2,1,0:T(8,128)S(1)}, u32[]{:S(2)}, u32[]{:S(2)}) collective-permute-start(f32[2,2,32,896]{3,2,1,0:T(8,128)S(1)} %collective-permute-done.27.refs_2_), channel_id=1, source_target_pairs={{0,32},{1,9},{2,34},{3,11},{4,36},{5,13},{6,38},{7,15},{8,40},{9,1... | collective-permute-start | bytes 1376264 | tf_op jit(solution)/shard_map/ppermute | solution.py:50
  92.3 9.8 %collective-permute-start.30 = (f32[2,2,32,896]{3,2,1,0:T(8,128)S(1)}, f32[2,2,32,896]{3,2,1,0:T(8,128)S(1)}, u32[]{:S(2)}, u32[]{:S(2)}) collective-permute-start(f32[2,2,32,896]{3,2,1,0:T(8,128)S(1)} %collective-permute-done.29.refs_3_), channel_id=1, source_target_pairs={{0,96},{1,25},{2,98},{3,27},{4,100},{5,29},{6,102},{7,31},{8,104},... | collective-permute-start | bytes 1376264 | tf_op jit(solution)/shard_map/ppermute | solution.py:50
